TPU v7x, 32 devices: a whole 2x2x4 slice. The times are simulated.
32 devices in a mesh: seq: 16 (over z, y, x), blk: 2 (over core).
Axes of the slice: x: 2, y: 2, z: 4, core: 2. Of those that a mesh axis runs over, the one named last changes fastest.
Arguments:
- inputs: bfloat16 [24576, 768], P(('seq', 'blk')), may hold values from -6 to 6
- segment_ids: int32 [24576], P(('seq', 'blk')), may hold values from 0 to 1027, as said below
- qkv_weight: bfloat16 [3, 4, 192, 192], replicated, may hold values from -0.4375 to 0.4375
- out_weight: bfloat16 [768, 768], replicated, may hold values from -1.75 to 1.75
- ffn_in_weight: bfloat16 [4, 192, 768], replicated, may hold values from -0.4375 to 0.4375
- ffn_out_weight: bfloat16 [4, 768, 192], replicated, may hold values from -0.21875 to 0.21875
- attn_gain: float32 [768], replicated, may hold values from 0.25 to 1.75
- attn_shift: float32 [768], replicated, may hold values from -3 to 3
- ffn_gain: float32 [768], replicated, may hold values from 0.25 to 1.75
- ffn_shift: float32 [768], replicated, may hold values from -3 to 3
- out_cotangent: bfloat16 [24576, 768], P(('seq', 'blk')), may hold values from -6 to 6
Outputs:
- output: bfloat16 [24576, 768], P(('seq', 'blk'))
- grad_input: bfloat16 [24576, 768], P(('seq', 'blk'))
- grad_qkv_weight: float32 [3, 4, 192, 192], replicated
- grad_out_weight: float32 [768, 768], replicated
- grad_ffn_in_weight: float32 [4, 192, 768], replicated
- grad_ffn_out_weight: float32 [4, 768, 192], replicated
- grad_attn_gain: float32 [768], replicated
- grad_attn_shift: float32 [768], replicated
- grad_ffn_gain: float32 [768], replicated
- grad_ffn_shift: float32 [768], replicated
Inputs may be any that keep to these rules, and one draw needn't show every extreme that they name: `segment_ids`: on the two devices of one seq index, the first k * 256 rows of both devices hold k sequences of 512 tokens, k from 1 to 2 and varying between seq indices: rows j * 256 to (j + 1) * 256 - 1 of both devices carry id j. Each device's other rows hold runs of equal ids of 1 to 128 tokens, ids over 2 that appear in no other run of the pair; every device has a run of exactly 128 tokens, and the last run of the second device of every pair carries the largest id. Ids are compared only within one seq index.
All inputs are finite; a program needn't handle non-finite values.
Results may differ from a plain program's by a relative error of at most 0.014.
Values may be sent and summed in bfloat16 or wider, within the bound.
No kernel may reach another device: no remote copies, remote signals or barrier semaphores. Data moves between devices by JAX's collectives and lax.ppermute only.
A program may use at most 192 MiB of HBM per device.

v0:
```python
from functools import partial

import jax
import jax.numpy as jnp
from jax import lax
from jax.sharding import PartitionSpec as P

HEADS = 12
HEAD_DIM = 64


EPSILON = 1e-05
heads_per_block = 4


def swapped(x, axis, distance):
    return lax.ppermute(x, axis, [(i, i ^ 1 << distance) for i in range(lax.axis_size(axis))])


def grouped(values, weight):
    row_count = values.shape[0]
    split_rows = values.reshape(row_count, weight.shape[0], weight.shape[1])
    return jnp.einsum(
        "ngi,gio->ngo", split_rows, weight, preferred_element_type=jnp.float32
    ).reshape(row_count, -1)


def grouped_back(grad_rows, weight):
    row_count = grad_rows.shape[0]
    split_rows = grad_rows.reshape(row_count, weight.shape[0], weight.shape[2])
    return jnp.einsum(
        "ngo,gio->ngi", split_rows, weight, preferred_element_type=jnp.float32
    ).reshape(row_count, -1)


def grouped_weight(values, grad_rows, groups):
    row_count = values.shape[0]
    return jnp.einsum(
        "ngi,ngo->gio",
        values.reshape(row_count, groups, -1),
        grad_rows.reshape(row_count, groups, -1),
        preferred_element_type=jnp.float32,
    )


def norm_forward(residual, norm_gain, norm_shift):
    centre = residual - jnp.mean(residual, -1, keepdims=True)
    inverse = lax.rsqrt(jnp.mean(centre * centre, -1, keepdims=True) + EPSILON)
    normed = centre * inverse
    return (normed * norm_gain + norm_shift, normed, inverse)


def norm_backward(grad_out, normed, inverse, norm_gain):
    scaled = grad_out * norm_gain
    grad_res = inverse * (
        scaled
        - jnp.mean(scaled, -1, keepdims=True)
        - normed * jnp.mean(scaled * normed, -1, keepdims=True)
    )
    return (grad_res, jnp.sum(grad_out * normed, 0), jnp.sum(grad_out, 0))


def head_slice(source, block_index):
    block_width = heads_per_block * HEAD_DIM
    block_piece = lax.dynamic_slice_in_dim(source, block_index * block_width, block_width, 1)
    return block_piece.reshape(source.shape[0], heads_per_block, HEAD_DIM)


def join_heads(stacked):
    return jnp.moveaxis(stacked, 0, 1).reshape(stacked.shape[1], -1)


def masked_scores(query_h, key_h, allowed):
    scores = jnp.einsum(
        "qhe,khe->hqk", query_h, key_h, preferred_element_type=jnp.float32
    ) * HEAD_DIM ** (-0.5)
    return jnp.where(allowed[None], scores, -1e30)


def attend(queries, key_set, value_set, allowed):

    def one_block(block_index):
        query_h = head_slice(queries, block_index)
        scores = masked_scores(query_h, head_slice(key_set, block_index), allowed)
        row_top = jnp.max(scores, -1, keepdims=True)
        log_total = row_top + jnp.log(jnp.sum(jnp.exp(scores - row_top), -1, keepdims=True))
        softmax = jnp.exp(scores - log_total).astype(jnp.bfloat16)
        context = jnp.einsum(
            "hqk,khe->qhe",
            softmax,
            head_slice(value_set, block_index),
            preferred_element_type=jnp.float32,
        )
        return (context, log_total[..., 0])

    context, log_total = lax.map(one_block, jnp.arange(HEADS // heads_per_block))
    return (join_heads(context), log_total.reshape(HEADS, queries.shape[0]))


def attend_back(queries, grad_ctx, key_set, value_set, allowed, log_total):

    def one_block(block_index):
        query_h = head_slice(queries, block_index)
        grad_h = head_slice(grad_ctx, block_index)
        key_h = head_slice(key_set, block_index)
        value_h = head_slice(value_set, block_index)
        total_h = lax.dynamic_slice_in_dim(
            log_total, block_index * heads_per_block, heads_per_block, 0
        )
        softmax = jnp.exp(masked_scores(query_h, key_h, allowed) - total_h[..., None])
        grad_probs = jnp.einsum("qhe,khe->hqk", grad_h, value_h, preferred_element_type=jnp.float32)
        row_dots = jnp.sum(softmax * grad_probs, -1)
        grad_scores = (softmax * (grad_probs - row_dots[..., None])).astype(jnp.bfloat16)
        kept_probs = softmax.astype(jnp.bfloat16)
        grad_keys = jnp.einsum(
            "hqk,qhe->khe", grad_scores, query_h, preferred_element_type=jnp.float32
        ) * HEAD_DIM ** (-0.5)
        grad_values = jnp.einsum(
            "hqk,qhe->khe", kept_probs, grad_h, preferred_element_type=jnp.float32
        )
        result = (grad_keys, grad_values, row_dots)
        grad_queries = jnp.einsum(
            "hqk,khe->qhe", grad_scores, key_h, preferred_element_type=jnp.float32
        ) * HEAD_DIM ** (-0.5)
        result = result + (grad_queries,)
        return result

    outputs = lax.map(one_block, jnp.arange(HEADS // heads_per_block))
    grad_queries = join_heads(outputs[3])
    return (
        join_heads(outputs[0]),
        join_heads(outputs[1]),
        outputs[2].reshape(HEADS, queries.shape[0]),
        grad_queries,
    )


def per_device(
    inputs,
    segment_ids,
    qkv_weight,
    out_weight,
    ffn_in_weight,
    ffn_out_weight,
    attn_gain,
    attn_shift,
    ffn_gain,
    ffn_shift,
    out_cotangent,
):
    row_count = inputs.shape[0]
    groups = qkv_weight.shape[1]
    partner_ids = swapped(segment_ids, "blk", 0)
    split_inputs = inputs.reshape(row_count, groups, -1)
    projected = jnp.einsum(
        "ngi,tgio->tngo", split_inputs, qkv_weight, preferred_element_type=jnp.float32
    )
    projected = projected.reshape(3, row_count, -1).astype(jnp.bfloat16)
    queries, keys_own, values_own = (projected[0], projected[1], projected[2])
    partner_kv = swapped(jnp.stack((keys_own, values_own)), "blk", 0)
    key_set = jnp.concatenate((keys_own, partner_kv[0]), 0)
    value_set = jnp.concatenate((values_own, partner_kv[1]), 0)
    allowed = segment_ids[:, None] == jnp.concatenate((segment_ids, partner_ids))[None, :]
    context, log_total = attend(queries, key_set, value_set, allowed)
    context_low = context.astype(jnp.bfloat16)
    attended = jnp.dot(context_low, out_weight, preferred_element_type=jnp.float32)
    hidden, normed_one, inverse_one = norm_forward(
        inputs.astype(jnp.float32) + attended, attn_gain, attn_shift
    )
    hidden_low = hidden.astype(jnp.bfloat16)
    upward = grouped(hidden_low, ffn_in_weight)
    activated, gelu_pull = jax.vjp(partial(jax.nn.gelu, approximate=False), upward)
    activated_low = activated.astype(jnp.bfloat16)
    feed_out = grouped(activated_low, ffn_out_weight)
    result, normed_two, inverse_two = norm_forward(hidden + feed_out, ffn_gain, ffn_shift)
    output = result.astype(jnp.bfloat16)
    grad_second, grad_ffn_gain, grad_ffn_shift = norm_backward(
        out_cotangent.astype(jnp.float32), normed_two, inverse_two, ffn_gain
    )
    grad_feed = grad_second.astype(jnp.bfloat16)
    grad_ffn_out = grouped_weight(activated_low, grad_feed, groups)
    grad_upward = gelu_pull(grouped_back(grad_feed, ffn_out_weight))[0].astype(jnp.bfloat16)
    grad_ffn_in = grouped_weight(hidden_low, grad_upward, groups)
    grad_hidden = grad_second + grouped_back(grad_upward, ffn_in_weight)
    grad_first, grad_attn_gain, grad_attn_shift = norm_backward(
        grad_hidden, normed_one, inverse_one, attn_gain
    )
    grad_attended = grad_first.astype(jnp.bfloat16)
    grad_out = jnp.einsum(
        "nd,ne->de", context_low, grad_attended, preferred_element_type=jnp.float32
    )
    grad_context = jnp.einsum(
        "ne,de->nd", grad_attended, out_weight, preferred_element_type=jnp.float32
    ).astype(jnp.bfloat16)
    keys_grad_all, values_grad_all, row_dots, grad_queries = attend_back(
        queries, grad_context, key_set, value_set, allowed, log_total
    )
    returned = swapped(
        jnp.stack((keys_grad_all[row_count:], values_grad_all[row_count:])).astype(jnp.bfloat16),
        "blk",
        0,
    ).astype(jnp.float32)
    grad_keys = keys_grad_all[:row_count] + returned[0]
    grad_values = values_grad_all[:row_count] + returned[1]
    grads_low = (
        jnp.stack((grad_queries, grad_keys, grad_values))
        .astype(jnp.bfloat16)
        .reshape(3, row_count, groups, -1)
    )
    grad_qkv = jnp.einsum(
        "ngi,tngo->tgio", split_inputs, grads_low, preferred_element_type=jnp.float32
    )
    through_qkv = jnp.einsum(
        "tngo,tgio->ngi", grads_low, qkv_weight, preferred_element_type=jnp.float32
    ).reshape(row_count, -1)
    grad_input = (grad_first + through_qkv).astype(jnp.bfloat16)
    totals = lax.psum(
        (
            grad_qkv,
            grad_out,
            grad_ffn_in,
            grad_ffn_out,
            grad_attn_gain,
            grad_attn_shift,
            grad_ffn_gain,
            grad_ffn_shift,
        ),
        ("seq", "blk"),
    )
    return (output, grad_input) + tuple(totals)


def solution(mesh):
    in_specs = (
        P(("seq", "blk"), None),
        P(("seq", "blk")),
        P(),
        P(),
        P(),
        P(),
        P(),
        P(),
        P(),
        P(),
        P(("seq", "blk"), None),
    )
    out_specs = (
        P(("seq", "blk"), None),
        P(("seq", "blk"), None),
        P(),
        P(),
        P(),
        P(),
        P(),
        P(),
        P(),
        P(),
    )
    return jax.shard_map(
        per_device, mesh=mesh, in_specs=in_specs, out_specs=out_specs, check_vma=False
    )
```

profile of v0, /device:TPU:1, one launch (start us, length us, event | category | flops | bytes accessed | tf_op | source)
XLA Modules:
  0.0 557.5 jit_solution(13414753893887148470)
XLA Ops:
  25.1 65.9 %while.28 = (s32[]{:T(128)}, bf16[3,768,4,64]{1,3,2,0:T(8,128)(2,1)}, f32[3,4,768]{2,1,0:T(4,128)}, s32[3]{0:T(128)S(1)}, bf16[1536,768]{0,1:T(8,128)(2,1)}, /*i...) while((s32[]{:T(128)}, ...), condition=%wide.region_3.4_spmd.clone, body=%wide.region_0.3_spmd.clone.sunk | while | flops 1261040640 | bytes 72852720 | solution.py:96
  33.9 5.9 %exponential_reduce_fusion.2 = f32[4,768]{1,0:T(4,128)S(1)} fusion(f32[4,768,1536]{2,1,0:T(8,128)S(1)} %get-tuple-element.425, f32[4,768]{1,0:T(4,128)S(1)} %get-tuple-element.426, pred[768,1536]{1,0:T(8,128)(4,1)S(1)} %broadcast_compare_fusion.4), kind=kLoop, calls=%fused_computation.3.clone.1 | loop fusion | flops 18871296 | bytes 20078592 | tf_op jit(solution)/shard_map/while/body/eval_jaxpr/reduce_sum | solution.py:86
  40.4 6.6 %fusion.131 = bf16[3,768,4,64]{1,3,2,0:T(8,128)(2,1)} fusion(bf16[3,768,4,64]{1,3,2,0:T(8,128)(2,1)} %get-tuple-element.459, s32[]{:T(128)S(6)} %copy.62, bf16[1536,4,64]{0,2,1:T(8,128)(2,1)S(1)} %bitcast.261, f32[4,768,1536]{2,1,0:T(8,128)S(1)} %get-tuple-element.425, f32[4,768]{1,0:T(4,128)S(1)} %get-tuple-element.427, pred[768,1536]{1,0:T(8,128)(4,1)} %copy-done.3), kind=kOutput, calls=%fused_computation.10.clone.1 | convolution fusion | flops 622854144 | bytes 21639172 | tf_op jit(solution)/shard_map/while/body/eval_jaxpr/hqk,khe->qhe/dot_general | solution.py:88
  55.7 5.9 %exponential_reduce_fusion.2 = f32[4,768]{1,0:T(4,128)S(1)} fusion(f32[4,768,1536]{2,1,0:T(8,128)S(1)} %get-tuple-element.425, f32[4,768]{1,0:T(4,128)S(1)} %get-tuple-element.426, pred[768,1536]{1,0:T(8,128)(4,1)S(1)} %broadcast_compare_fusion.4), kind=kLoop, calls=%fused_computation.3.clone.1 | loop fusion | flops 18871296 | bytes 20078592 | tf_op jit(solution)/shard_map/while/body/eval_jaxpr/reduce_sum | solution.py:86
  62.2 6.6 %fusion.131 = bf16[3,768,4,64]{1,3,2,0:T(8,128)(2,1)} fusion(bf16[3,768,4,64]{1,3,2,0:T(8,128)(2,1)} %get-tuple-element.459, s32[]{:T(128)S(6)} %copy.62, bf16[1536,4,64]{0,2,1:T(8,128)(2,1)S(1)} %bitcast.261, f32[4,768,1536]{2,1,0:T(8,128)S(1)} %get-tuple-element.425, f32[4,768]{1,0:T(4,128)S(1)} %get-tuple-element.427, pred[768,1536]{1,0:T(8,128)(4,1)} %copy-done.3), kind=kOutput, calls=%fused_computation.10.clone.1 | convolution fusion | flops 622854144 | bytes 21639172 | tf_op jit(solution)/shard_map/while/body/eval_jaxpr/hqk,khe->qhe/dot_general | solution.py:88
  77.6 5.9 %exponential_reduce_fusion.2 = f32[4,768]{1,0:T(4,128)S(1)} fusion(f32[4,768,1536]{2,1,0:T(8,128)S(1)} %get-tuple-element.425, f32[4,768]{1,0:T(4,128)S(1)} %get-tuple-element.426, pred[768,1536]{1,0:T(8,128)(4,1)S(1)} %broadcast_compare_fusion.4), kind=kLoop, calls=%fused_computation.3.clone.1 | loop fusion | flops 18871296 | bytes 20078592 | tf_op jit(solution)/shard_map/while/body/eval_jaxpr/reduce_sum | solution.py:86
  84.1 6.6 %fusion.131 = bf16[3,768,4,64]{1,3,2,0:T(8,128)(2,1)} fusion(bf16[3,768,4,64]{1,3,2,0:T(8,128)(2,1)} %get-tuple-element.459, s32[]{:T(128)S(6)} %copy.62, bf16[1536,4,64]{0,2,1:T(8,128)(2,1)S(1)} %bitcast.261, f32[4,768,1536]{2,1,0:T(8,128)S(1)} %get-tuple-element.425, f32[4,768]{1,0:T(4,128)S(1)} %get-tuple-element.427, pred[768,1536]{1,0:T(8,128)(4,1)} %copy-done.3), kind=kOutput, calls=%fused_computation.10.clone.1 | convolution fusion | flops 622854144 | bytes 21639172 | tf_op jit(solution)/shard_map/while/body/eval_jaxpr/hqk,khe->qhe/dot_general | solution.py:88
  96.1 23.6 %fusion.36 = (bf16[768,4,768]{2,0,1:T(8,128)(2,1)S(1)}, f32[768,4,768]{2,0,1:T(8,128)}, f32[4,768,768]{2,1,0:T(8,128)}) fusion(bf16[768,4,192]{0,2,1:T(8,128)(2,1)S(1)} %bitcast.272, bf16[4,192,768]{2,1,0:T(8,128)(2,1)S(1)} %copy-done), kind=kOutput, calls=%fused_computation.57 | convolution fusion | flops 1059323904 | bytes 25952256 | tf_op jit(solution)/shard_map/ngi,gio->ngo/dot_general | solution.py:23
  126.0 9.0 %fusion.33 = bf16[768,4,768]{2,0,1:T(8,128)(2,1)S(1)} fusion(f32[768,4,768]{2,0,1:T(8,128)} %get-tuple-element.275, f32[4,768,768]{2,1,0:T(8,128)} %get-tuple-element.294, bf16[768,4,192]{0,2,1:T(8,128)(2,1)S(1)} %bitcast.278, bf16[4,768,192]{1,2,0:T(8,128)(2,1)S(1)} %copy-done.28), kind=kOutput, calls=%fused_computation.49 | convolution fusion | flops 938999808 | bytes 25952256 | tf_op jit(solution)/shard_map/ngo,gio->ngi/dot_general | solution.py:31
  144.9 180.7 %while.29 = (s32[]{:T(128)}, f32[3,1536,4,64]{1,3,2,0:T(8,128)}, f32[3,1536,4,64]{1,3,2,0:T(8,128)}, bf16[3,768,4,64]{1,3,2,0:T(8,128)(2,1)}, s32[3]{0:T(128)S(1...) while((s32[]{:T(128)}, f32[3,1536,4,64]{1,3,2,0:T(8,128)}, ...), condition=%wide.region_14.15_spmd.clone, body=%wide.region_12.14_spmd.clone.sunk | while | flops 3092444160 | bytes 244675968 | solution.py:128
  162.5 6.4 %copy-done.2 = f32[4,768,1536]{2,1,0:T(8,128)} copy-done((f32[4,768,1536]{2,1,0:T(8,128)}, f32[4,768,1536]{2,1,0:T(8,128)S(1)}, u32[]{:S(2)}) %copy-start.2) | copy-done | bytes 18874392 | tf_op jit(solution)/shard_map/while
  169.0 6.1 %fusion.144 = f32[3,1536,4,64]{1,3,2,0:T(8,128)} fusion(f32[3,1536,4,64]{1,3,2,0:T(8,128)} %get-tuple-element.504, s32[]{:T(128)S(6)} %copy.72, bf16[768,4,64]{0,2,1:T(8,128)(2,1)S(1)} %bitcast.259, f32[4,768,1536]{2,1,0:T(8,128)S(1)} %fusion.142, f32[4,768]{1,0:T(4,128)S(1)} %constant_dynamic-slice_fusion.18, ...), kind=kOutput, calls=%fused_computation.28.clone.1 | convolution fusion | flops 622854144 | bytes 22032388 | tf_op jit(solution)/shard_map/while/body/eval_jaxpr/hqk,qhe->khe/dot_general | solution.py:118
  175.0 17.0 %multiply_reduce_fusion.7 = (f32[4,768]{1,0:T(4,128)S(1)}, f32[4,768,1536]{2,1,0:T(8,128)}) fusion(f32[4,768,1536]{2,1,0:T(8,128)} %copy-done.2, f32[4,768]{1,0:T(4,128)S(1)} %constant_dynamic-slice_fusion.18, pred[768,1536]{1,0:T(8,128)(4,1)S(1)} %broadcast_compare_fusion.5, bf16[768,4,64]{0,2,1:T(8,128)(2,1)S(1)} %bitcast.260, ...), kind=kOutput, calls=%fused_computation.19.clone.1 | convolution fusion | flops 627569664 | bytes 40132608 | tf_op jit(solution)/shard_map/while/body/eval_jaxpr/qhe,khe->hqk/dot_general | solution.py:111
  192.1 13.4 %multiply_convert_fusion.2 = bf16[4,768,1536]{2,1,0:T(8,128)(2,1)S(1)} fusion(f32[4,768,1536]{2,1,0:T(8,128)} %get-tuple-element.443, f32[4,768,1536]{2,1,0:T(8,128)} %copy-done.2, f32[4,768]{1,0:T(4,128)S(1)} %get-tuple-element.444, f32[4,768]{1,0:T(4,128)S(1)} %constant_dynamic-slice_fusion.18, pred[768,1536]{1,0:T(8,128)(4,1)S(1)} %broadcast_compare_fusion.5), kind=kLoop, calls=%fused_computation.18.clone.1 | loop fusion | flops 28311552 | bytes 48390144 | tf_op jit(solution)/shard_map/while/body/eval_jaxpr/convert_element_type | solution.py:113
  219.5 6.4 %copy-done.2 = f32[4,768,1536]{2,1,0:T(8,128)} copy-done((f32[4,768,1536]{2,1,0:T(8,128)}, f32[4,768,1536]{2,1,0:T(8,128)S(1)}, u32[]{:S(2)}) %copy-start.2) | copy-done | bytes 18874392 | tf_op jit(solution)/shard_map/while
  226.0 6.1 %fusion.144 = f32[3,1536,4,64]{1,3,2,0:T(8,128)} fusion(f32[3,1536,4,64]{1,3,2,0:T(8,128)} %get-tuple-element.504, s32[]{:T(128)S(6)} %copy.72, bf16[768,4,64]{0,2,1:T(8,128)(2,1)S(1)} %bitcast.259, f32[4,768,1536]{2,1,0:T(8,128)S(1)} %fusion.142, f32[4,768]{1,0:T(4,128)S(1)} %constant_dynamic-slice_fusion.18, ...), kind=kOutput, calls=%fused_computation.28.clone.1 | convolution fusion | flops 622854144 | bytes 22032388 | tf_op jit(solution)/shard_map/while/body/eval_jaxpr/hqk,qhe->khe/dot_general | solution.py:118
  232.1 17.0 %multiply_reduce_fusion.7 = (f32[4,768]{1,0:T(4,128)S(1)}, f32[4,768,1536]{2,1,0:T(8,128)}) fusion(f32[4,768,1536]{2,1,0:T(8,128)} %copy-done.2, f32[4,768]{1,0:T(4,128)S(1)} %constant_dynamic-slice_fusion.18, pred[768,1536]{1,0:T(8,128)(4,1)S(1)} %broadcast_compare_fusion.5, bf16[768,4,64]{0,2,1:T(8,128)(2,1)S(1)} %bitcast.260, ...), kind=kOutput, calls=%fused_computation.19.clone.1 | convolution fusion | flops 627569664 | bytes 40132608 | tf_op jit(solution)/shard_map/while/body/eval_jaxpr/qhe,khe->hqk/dot_general | solution.py:111
  249.1 13.4 %multiply_convert_fusion.2 = bf16[4,768,1536]{2,1,0:T(8,128)(2,1)S(1)} fusion(f32[4,768,1536]{2,1,0:T(8,128)} %get-tuple-element.443, f32[4,768,1536]{2,1,0:T(8,128)} %copy-done.2, f32[4,768]{1,0:T(4,128)S(1)} %get-tuple-element.444, f32[4,768]{1,0:T(4,128)S(1)} %constant_dynamic-slice_fusion.18, pred[768,1536]{1,0:T(8,128)(4,1)S(1)} %broadcast_compare_fusion.5), kind=kLoop, calls=%fused_computation.18.clone.1 | loop fusion | flops 28311552 | bytes 48390144 | tf_op jit(solution)/shard_map/while/body/eval_jaxpr/convert_element_type | solution.py:113
  276.6 6.4 %copy-done.2 = f32[4,768,1536]{2,1,0:T(8,128)} copy-done((f32[4,768,1536]{2,1,0:T(8,128)}, f32[4,768,1536]{2,1,0:T(8,128)S(1)}, u32[]{:S(2)}) %copy-start.2) | copy-done | bytes 18874392 | tf_op jit(solution)/shard_map/while
  283.1 6.0 %fusion.144 = f32[3,1536,4,64]{1,3,2,0:T(8,128)} fusion(f32[3,1536,4,64]{1,3,2,0:T(8,128)} %get-tuple-element.504, s32[]{:T(128)S(6)} %copy.72, bf16[768,4,64]{0,2,1:T(8,128)(2,1)S(1)} %bitcast.259, f32[4,768,1536]{2,1,0:T(8,128)S(1)} %fusion.142, f32[4,768]{1,0:T(4,128)S(1)} %constant_dynamic-slice_fusion.18, ...), kind=kOutput, calls=%fused_computation.28.clone.1 | convolution fusion | flops 622854144 | bytes 22032388 | tf_op jit(solution)/shard_map/while/body/eval_jaxpr/hqk,qhe->khe/dot_general | solution.py:118
  289.1 17.0 %multiply_reduce_fusion.7 = (f32[4,768]{1,0:T(4,128)S(1)}, f32[4,768,1536]{2,1,0:T(8,128)}) fusion(f32[4,768,1536]{2,1,0:T(8,128)} %copy-done.2, f32[4,768]{1,0:T(4,128)S(1)} %constant_dynamic-slice_fusion.18, pred[768,1536]{1,0:T(8,128)(4,1)S(1)} %broadcast_compare_fusion.5, bf16[768,4,64]{0,2,1:T(8,128)(2,1)S(1)} %bitcast.260, ...), kind=kOutput, calls=%fused_computation.19.clone.1 | convolution fusion | flops 627569664 | bytes 40132608 | tf_op jit(solution)/shard_map/while/body/eval_jaxpr/qhe,khe->hqk/dot_general | solution.py:111
  306.1 13.4 %multiply_convert_fusion.2 = bf16[4,768,1536]{2,1,0:T(8,128)(2,1)S(1)} fusion(f32[4,768,1536]{2,1,0:T(8,128)} %get-tuple-element.443, f32[4,768,1536]{2,1,0:T(8,128)} %copy-done.2, f32[4,768]{1,0:T(4,128)S(1)} %get-tuple-element.444, f32[4,768]{1,0:T(4,128)S(1)} %constant_dynamic-slice_fusion.18, pred[768,1536]{1,0:T(8,128)(4,1)S(1)} %broadcast_compare_fusion.5), kind=kLoop, calls=%fused_computation.18.clone.1 | loop fusion | flops 28311552 | bytes 48390144 | tf_op jit(solution)/shard_map/while/body/eval_jaxpr/convert_element_type | solution.py:113
  348.1 44.0 %all-reduce = (f32[768]{0:T(1024)}, f32[768]{0:T(1024)}, f32[768]{0:T(1024)}, f32[768]{0:T(1024)}) all-reduce(f32[768]{0:T(1024)S(1)} %copy-done.33, f32[768]{0:T(1024)S(1)} %copy-done.34, f32[768]{0:T(1024)S(1)} %copy-done.35, f32[768]{0:T(1024)S(1)} %copy-done.36), channel_id=1, replica_groups=mesh['seq'=16,'blk'=2] {'seq','blk'}, use_global_device_ids=true, to_apply=%region_20.21 | all-reduce | flops 3072 | bytes 24576 | tf_op jit(solution)/shard_map/psum | solution.py:217
  397.6 143.1 %all-reduce.4.cloned.1.call-done = (f32[3,4,192,192]{2,3,0,1:T(8,128)}, f32[768,768]{1,0:T(8,128)}, f32[4,192,768]{2,1,0:T(8,128)}, f32[4,768,192]{1,2,0:T(8,128)}) async-done(((f32[3,4,192,192]{2,3,0,1:T(8,128)}, f32[768,768]{1,0:T(8,128)}, f32[4,192,768]{2,1,0:T(8,128)}, f32[4,768,192]{1,2,0:T(8,128)}), (f32[3,4,192,192]{2,3,0,1:T(8,128)}, f32[768,768]{1,0:T(8,128)}, f32[4,192,768]{2,1,0:T(8,128)}, ...) | async-done | bytes 8847376 | tf_op jit(solution)/shard_map/psum | solution.py:217
  (220 shorter events, 140.3 us)
Async XLA Ops:
  7.2 88.9 %copy-start = (bf16[4,192,768]{2,1,0:T(8,128)(2,1)S(1)}, bf16[4,192,768]{2,1,0:T(8,128)(2,1)}, u32[]{:S(2)}) copy-start(bf16[4,192,768]{2,1,0:T(8,128)(2,1)} %param.19) | copy-start | bytes 3538948
  7.2 533.4 %all-reduce.4.cloned.1.call-start = ((), (), s32[]{:S(2)}) async-start(), calls=%async_computation | async-start | bytes 18874368 | tf_op jit(solution)/shard_map/psum | solution.py:217
  13.7 6.1 %collective-permute-start = (bf16[2,768,768]{1,2,0:T(8,128)(2,1)}, bf16[2,768,768]{1,2,0:T(8,128)(2,1)}, u32[]{:S(2)}, u32[]{:S(2)}) collective-permute-start(bf16[2,768,768]{1,2,0:T(8,128)(2,1)} %bitcast.5), channel_id=1, source_target_pairs={{0,1},{1,0},{2,3},{3,2},{4,5},{5,4},{6,7},{7,6},{8,9},{9,8},{10,11... | collective-permute-start | bytes 7077896 | tf_op jit(solution)/shard_map/ppermute | solution.py:17
  13.7 6.1 %collective-permute-start.1 = (s32[768]{0:T(1024)S(1)}, s32[768]{0:T(1024)S(1)}, u32[]{:S(2)}, u32[]{:S(2)}) collective-permute-start(s32[768]{0:T(1024)S(1)} %copy-done.29), channel_id=1, source_target_pairs={{0,1},{1,0},{2,3},{3,2},{4,5},{5,4},{6,7},{7,6},{8,9},{9,8},{10,11... | collective-permute-start | bytes 9224 | tf_op jit(solution)/shard_map/ppermute | solution.py:17
  28.1 5.7 %copy-start.3 = (pred[768,1536]{1,0:T(8,128)(4,1)}, pred[768,1536]{1,0:T(8,128)(4,1)S(1)}, u32[]{:S(2)}) copy-start(pred[768,1536]{1,0:T(8,128)(4,1)S(1)} %broadcast_compare_fusion.4) | copy-start | bytes 3538948 | tf_op jit(solution)/shard_map/while
  50.0 5.7 %copy-start.3 = (pred[768,1536]{1,0:T(8,128)(4,1)}, pred[768,1536]{1,0:T(8,128)(4,1)S(1)}, u32[]{:S(2)}) copy-start(pred[768,1536]{1,0:T(8,128)(4,1)S(1)} %broadcast_compare_fusion.4) | copy-start | bytes 3538948 | tf_op jit(solution)/shard_map/while
  71.9 5.7 %copy-start.3 = (pred[768,1536]{1,0:T(8,128)(4,1)}, pred[768,1536]{1,0:T(8,128)(4,1)S(1)}, u32[]{:S(2)}) copy-start(pred[768,1536]{1,0:T(8,128)(4,1)S(1)} %broadcast_compare_fusion.4) | copy-start | bytes 3538948 | tf_op jit(solution)/shard_map/while
  96.0 23.7 %copy-start.12 = (bf16[768,768]{0,1:T(8,128)(2,1)}, bf16[768,768]{0,1:T(8,128)(2,1)S(1)}, u32[]{:S(2)}) copy-start(bf16[768,768]{0,1:T(8,128)(2,1)S(1)} %fusion.59) | copy-start | bytes 3538948
  96.1 23.6 %copy-start.28 = (bf16[4,768,192]{1,2,0:T(8,128)(2,1)S(1)}, bf16[4,768,192]{1,2,0:T(8,128)(2,1)}, u32[]{:S(2)}) copy-start(bf16[4,768,192]{1,2,0:T(8,128)(2,1)} %param.20) | copy-start | bytes 3538948
  126.0 9.0 %copy-start.16 = (bf16[768,768]{0,1:T(8,128)(2,1)}, bf16[768,768]{0,1:T(8,128)(2,1)S(1)}, u32[]{:S(2)}) copy-start(bf16[768,768]{0,1:T(8,128)(2,1)S(1)} %fusion.66) | copy-start | bytes 3538948
  162.5 6.5 %copy-start.2 = (f32[4,768,1536]{2,1,0:T(8,128)}, f32[4,768,1536]{2,1,0:T(8,128)S(1)}, u32[]{:S(2)}) copy-start(f32[4,768,1536]{2,1,0:T(8,128)S(1)} %fusion.142) | copy-start | bytes 56623108 | tf_op jit(solution)/shard_map/while
  192.1 13.4 %copy-start.25 = (bf16[3,768,4,64]{1,3,2,0:T(8,128)(2,1)S(1)}, bf16[3,768,4,64]{1,3,2,0:T(8,128)(2,1)}, u32[]{:S(2)}) copy-start(bf16[3,768,4,64]{1,3,2,0:T(8,128)(2,1)} %get-tuple-element.505) | copy-start | bytes 3538948 | tf_op jit(solution)/shard_map/while
  219.5 6.5 %copy-start.2 = (f32[4,768,1536]{2,1,0:T(8,128)}, f32[4,768,1536]{2,1,0:T(8,128)S(1)}, u32[]{:S(2)}) copy-start(f32[4,768,1536]{2,1,0:T(8,128)S(1)} %fusion.142) | copy-start | bytes 56623108 | tf_op jit(solution)/shard_map/while
  249.1 13.4 %copy-start.25 = (bf16[3,768,4,64]{1,3,2,0:T(8,128)(2,1)S(1)}, bf16[3,768,4,64]{1,3,2,0:T(8,128)(2,1)}, u32[]{:S(2)}) copy-start(bf16[3,768,4,64]{1,3,2,0:T(8,128)(2,1)} %get-tuple-element.505) | copy-start | bytes 3538948 | tf_op jit(solution)/shard_map/while
  276.6 6.5 %copy-start.2 = (f32[4,768,1536]{2,1,0:T(8,128)}, f32[4,768,1536]{2,1,0:T(8,128)S(1)}, u32[]{:S(2)}) copy-start(f32[4,768,1536]{2,1,0:T(8,128)S(1)} %fusion.142) | copy-start | bytes 56623108 | tf_op jit(solution)/shard_map/while
  306.1 13.4 %copy-start.25 = (bf16[3,768,4,64]{1,3,2,0:T(8,128)(2,1)S(1)}, bf16[3,768,4,64]{1,3,2,0:T(8,128)(2,1)}, u32[]{:S(2)}) copy-start(bf16[3,768,4,64]{1,3,2,0:T(8,128)(2,1)} %get-tuple-element.505) | copy-start | bytes 3538948 | tf_op jit(solution)/shard_map/while
  325.6 4.3 copy-start.18
  329.6 5.6 %slice-start = ((s8[4718592]{0:T(1024)(128)(4,1)}), s8[524288]{0:T(1024)(128)(4,1)S(1)}, s32[]{:S(2)}) async-start(s8[4718592]{0:T(1024)(128)(4,1)} %bitcast.262), calls=%async_computation.1 | async-start | bytes 1048576
  329.8 10.4 %collective-permute-start.2 = (bf16[2,768,768]{1,2,0:T(8,128)(2,1)S(1)}, bf16[2,768,768]{1,2,0:T(8,128)(2,1)S(1)}, u32[]{:S(2)}, u32[]{:S(2)}) collective-permute-start(bf16[2,768,768]{1,2,0:T(8,128)(2,1)S(1)} %pad_maximum_fusion.3), channel_id=1, source_target_pairs={{0,1},{1,0},{2,3},{3,2},{4,5},{5,4},{6,7},{7,6},{8,9},{9,8},{10,11... | collective-permute-start | bytes 7077896 | tf_op jit(solution)/shard_map/ppermute | solution.py:17
  330.9 4.3 slice-start.1
  330.9 4.3 copy-start.17
  332.6 5.1 slice-start.2
  540.6 3.4 copy-start.22
  546.5 3.9 copy-start.1
  (33 other events, 65.1 us)
Sparse Core Ops, SparseCore 0:
  345.6 195.0 all-reduce.3
where the time goes:
time: 562 us; the launch traced here: 558 us
  matrix products  181 us (32%)
  waiting for transfers between devices  143 us (25%)
  local copies, waits for them, and re-layouts  81 us (14%)
  other arithmetic  76.5 us (14%)
  blocking collectives  44 us (8%)
  loops' own time  16.3 us (3%)
  between operations  14.8 us (3%)
    psum x1, waiting for transfers between devices, per_device(): lax.psum((grad_qkv, grad_out, grad_ffn_in, grad_ffn_out, grad_attn_gain,...  143 us
    dot_general x3, matrix products, one_block(): jnp.einsum('qhe,khe->hqk', grad_h, value_h, preferred_element_type=jnp.fl...  51 us
    psum x1, blocking collectives, per_device(): lax.psum((grad_qkv, grad_out, grad_ffn_in, grad_ffn_out, grad_attn_gain,...  44 us
    convert_element_type x3, other arithmetic, one_block(): (softmax * (grad_probs - row_dots[..., None])).astype(jnp.bfloat16)  40.2 us
    unnamed x91, local copies, waits for them, and re-layouts  26.8 us
    dot_general x2, matrix products, grouped(): jnp.einsum('ngi,gio->ngo', split_rows, weight, preferred_element_type=jnp...  25.3 us
    dot_general x3, matrix products, one_block(): jnp.einsum('hqk,khe->qhe', softmax, head_slice(value_set, block_index), p...  19.9 us
    dot_general x6, matrix products, masked_scores(): jnp.einsum('qhe,khe->hqk', query_h, key_h, preferred_element_type=jnp.flo...  19.4 us
  transfers between devices with their start and end apart: 4, of which 1 were waited for; matrix products, arithmetic and copies ran while one was open for 4% of the time, Pallas kernels for 0%

commit v1 on v0

v1 whole, which is shorter than its diff:
```python
from functools import partial

import jax
import jax.numpy as jnp
from jax import lax
from jax.experimental import pallas as pl
from jax.experimental.pallas import tpu as pltpu
from jax.sharding import Mesh, PartitionSpec as P

F32 = jnp.float32
BF16 = jnp.bfloat16
EPSILON = 1e-05
HEADS = 12
HEAD_DIM = 64
D = 768
GROUPS = 4
GD = D // GROUPS
FF = 3072
GF = FF // GROUPS
TOK = 768
BLK = 256
EXT = 512
ALL = TOK + EXT
UNITS = 16
CHUNK = (144, 384)
QCHUNK = (24, 640)
VMEM_LIMIT = 61 * 1024 * 1024


def nn(a, b):
    return lax.dot_general(a, b, (((1,), (0,)), ((), ())), preferred_element_type=F32)


def nt(a, b):
    return lax.dot_general(a, b, (((1,), (1,)), ((), ())), preferred_element_type=F32)


def tn(a, b):
    return lax.dot_general(a, b, (((0,), (0,)), ((), ())), preferred_element_type=F32)


def gelu_parts(u):
    a = jnp.abs(u) * 0.7071067811865476
    t = 1.0 / (1.0 + 0.3275911 * a)
    e = jnp.exp(-0.5 * (u * u))
    poly = t * (
        0.254829592
        + t * (-0.284496736 + t * (1.421413741 + t * (-1.453152027 + t * 1.061405429)))
    )
    tail = 0.5 * poly * e
    phi = jnp.where(u < 0, tail, 1.0 - tail)
    return u * phi, phi + u * (e * 0.3989422804014327)


def layer_kernel(
    code_ref, x_ref, xp_ref, segr_ref, segc_ref, wqkv_ref, wo_ref, w1_ref, w2t_ref, norm_ref, cot_ref,
    out_ref, xt_ref, q_ref, k_ref, v_ref, gctx_ref, lse_ref, gfirst_ref, keep_ref, send_ref, gvec_ref,
    bias, wot, w1t, w2, ctx, hid, act, gup, gpr, gfeed, gatt, nb, gacc,
):
    core, low, far = code_ref[0], code_ref[1], code_ref[3]
    two = code_ref[2]
    xt_ref[:, :TOK] = x_ref[...].T
    xt_ref[:, TOK:] = xp_ref[...].T
    for j in range(4):
        nb[j] = jnp.broadcast_to(norm_ref[:, j : j + 1], (D, 128))
    wot[...] = wo_ref[...].T
    for g in range(GROUPS):
        w1t[g] = w1_ref[g].T
        w2[g] = w2t_ref[g].T
        rows = slice(g * GD, (g + 1) * GD)
        xg = xt_ref[rows, :]
        q_ref[rows, :] = (tn(wqkv_ref[0, g], xg[:, :TOK]).astype(BF16).astype(F32) * 0.125).astype(BF16)
        k_ref[rows, :] = tn(wqkv_ref[1, g], xg).astype(BF16)
        v_ref[rows, :] = tn(wqkv_ref[2, g], xg).astype(BF16)

    off = jnp.where(two == 1, 2 * BLK + BLK + BLK, 2 * BLK)
    segr = segr_ref[...]
    segc = segc_ref[...]

    def same(kb, qb):
        a = segc[kb * BLK : (kb + 1) * BLK]
        b = segr[:, qb * BLK : (qb + 1) * BLK]
        return jnp.where(a == b, 0.0, -1e30).astype(F32)

    bias[0, :BLK] = same(1, 1)
    bias[0, BLK:] = jnp.where(two == 1, 0.0, same(2, 1))
    bias[1, :BLK] = same(2, 2)
    bias[1, BLK:] = same(1, 2)

    def head(h, carry):
        hr = pl.ds(pl.multiple_of(h * HEAD_DIM, HEAD_DIM), HEAD_DIM)
        for b in range(3):
            if b == 0:
                ec = slice(TOK, TOK + BLK)
            elif b == 1:
                ec = pl.ds(pl.multiple_of(off, BLK), BLK)
            else:
                ec = slice(BLK, 2 * BLK)
            qc = slice(b * BLK, (b + 1) * BLK)
            kt = jnp.concatenate([k_ref[hr, qc], k_ref[hr, ec]], 1)
            vt = jnp.concatenate([v_ref[hr, qc], v_ref[hr, ec]], 1)
            s = tn(kt, q_ref[hr, qc])
            if b:
                s = s + bias[b - 1]
            top = jnp.max(s, 0, keepdims=True)
            p = jnp.exp(s - top)
            total = jnp.sum(p, 0, keepdims=True)
            c = nn(vt, p.astype(BF16))
            ctx[hr, qc] = (c * (1.0 / total)).astype(BF16)
            lse_ref[h, :, qc] = top + jnp.log(total)
        return carry

    lax.fori_loop(0, HEADS, head, 0)

    gacc[...] = jnp.zeros_like(gacc)

    def wide(j):
        return jnp.concatenate([nb[j], nb[j]], 1)

    def tile(t, carry):
        tc = pl.ds(pl.multiple_of(t * BLK, BLK), BLK)
        r = xt_ref[:, tc].astype(F32) + nn(wot[...], ctx[:, tc])
        centre = r - jnp.mean(r, 0, keepdims=True)
        inv1 = lax.rsqrt(jnp.mean(centre * centre, 0, keepdims=True) + EPSILON)
        n1 = centre * inv1
        hidden = n1 * wide(0) + wide(1)
        hid[:, tc] = hidden.astype(BF16)
        feeds = []
        for g in range(GROUPS):
            hg = hid[g * GD : (g + 1) * GD, tc]
            for j in range(GF // BLK):
                fr = slice(j * BLK, (j + 1) * BLK)
                a, d = gelu_parts(nn(w1t[g, fr], hg))
                act[g, fr, tc] = a.astype(BF16)
                gpr[g, fr] = d
            feeds.append(nn(w2t_ref[g], act[g, :, tc]))
        r2 = hidden + jnp.concatenate(feeds, 0)
        centre2 = r2 - jnp.mean(r2, 0, keepdims=True)
        inv2 = lax.rsqrt(jnp.mean(centre2 * centre2, 0, keepdims=True) + EPSILON)
        n2 = centre2 * inv2
        out_ref[tc, :] = (n2 * wide(2) + wide(3)).astype(BF16).T
        c = cot_ref[tc, :].T.astype(F32)
        cn = c * n2
        gacc[2] += cn[:, :128] + cn[:, 128:]
        gacc[3] += c[:, :128] + c[:, 128:]
        cg = c * wide(2)
        gsec = inv2 * (
            cg - jnp.mean(cg, 0, keepdims=True) - n2 * jnp.mean(cg * n2, 0, keepdims=True)
        )
        gfeed[:, tc] = gsec.astype(BF16)
        gh = []
        for g in range(GROUPS):
            fg = gfeed[g * GD : (g + 1) * GD, tc]
            for j in range(GF // BLK):
                fr = slice(j * BLK, (j + 1) * BLK)
                gup[g, fr, tc] = (nn(w2[g, fr], fg) * gpr[g, fr]).astype(BF16)
            gh.append(nn(w1_ref[g], gup[g, :, tc]))
        ghid = gsec + jnp.concatenate(gh, 0)
        gn = ghid * n1
        gacc[0] += gn[:, :128] + gn[:, 128:]
        gacc[1] += ghid[:, :128] + ghid[:, 128:]
        sc = ghid * wide(0)
        gfirst = inv1 * (
            sc - jnp.mean(sc, 0, keepdims=True) - n1 * jnp.mean(sc * n1, 0, keepdims=True)
        )
        gfirst_ref[:, tc] = gfirst
        gatt[:, tc] = gfirst.astype(BF16)
        gctx_ref[:, tc] = nn(wo_ref[...], gatt[:, tc]).astype(BF16)
        return carry

    lax.fori_loop(0, TOK // BLK, tile, 0)
    for j in range(4):
        gvec_ref[:, j : j + 1] = jnp.sum(gacc[j], 1, keepdims=True)

    for jj in range(GROUPS):
        g = jj ^ (2 * core)
        gr = pl.ds(pl.multiple_of(g * GD, GD), GD)
        parts = (
            nt(hid[gr, :], gup[g]),
            nt(gfeed[gr, :], act[g]),
            nt(ctx[gr, :], gatt[...]),
        )
        for i, part in enumerate(parts):
            for r in range(4):
                for lh in range(2):
                    piece = part[48 * r : 48 * (r + 1), 384 * lh : 384 * (lh + 1)]
                    pos = ((g & 1) * 8 + r * 2 + lh) ^ (low if jj < 2 else far)
                    if jj < 2:
                        keep_ref[pos, 48 * i : 48 * (i + 1)] = piece
                    else:
                        send_ref[pos, 48 * i : 48 * (i + 1)] = piece.astype(BF16)


def back_kernel(
    code_ref, q_ref, k_ref, v_ref, gctx_ref, lse_ref, segr_ref, segc_ref,
    dq_ref, dk_ref, dv_ref, dkp_ref, dvp_ref, bias, dk, dv,
):
    two = code_ref[2]
    off = jnp.where(two == 1, 2 * BLK + BLK + BLK, 2 * BLK)
    segr = segr_ref[...]
    segc = segc_ref[...]

    def same(kb, qb):
        a = segc[kb * BLK : (kb + 1) * BLK]
        b = segr[:, qb * BLK : (qb + 1) * BLK]
        return jnp.where(a == b, 0.0, -1e30).astype(F32)

    bias[0, :BLK] = same(1, 1)
    bias[0, BLK:] = jnp.where(two == 1, 0.0, same(2, 1))
    bias[1, :BLK] = same(2, 2)
    bias[1, BLK:] = same(1, 2)
    dk[...] = jnp.zeros_like(dk)
    dv[...] = jnp.zeros_like(dv)

    def head(h, carry):
        hr = pl.ds(pl.multiple_of(h * HEAD_DIM, HEAD_DIM), HEAD_DIM)
        for b in range(3):
            if b == 0:
                ec = slice(TOK, TOK + BLK)
            elif b == 1:
                ec = pl.ds(pl.multiple_of(off, BLK), BLK)
            else:
                ec = slice(BLK, 2 * BLK)
            qc = slice(b * BLK, (b + 1) * BLK)
            kt = jnp.concatenate([k_ref[hr, qc], k_ref[hr, ec]], 1)
            vt = jnp.concatenate([v_ref[hr, qc], v_ref[hr, ec]], 1)
            qt = q_ref[hr, qc]
            gt = gctx_ref[hr, qc]
            s = tn(kt, qt)
            if b:
                s = s + bias[b - 1]
            p = jnp.exp(s - lse_ref[h, :, qc])
            dp = tn(vt, gt)
            dots = jnp.sum(p * dp, 0, keepdims=True)
            ds = (p * (dp - dots)).astype(BF16)
            dq_ref[hr, qc] = (nn(kt, ds) * 0.125).astype(BF16)
            gk = nt(qt, ds)
            gv = nt(gt, p.astype(BF16))
            dk[hr, qc] += gk[:, :BLK]
            dk[hr, ec] += gk[:, BLK:]
            dv[hr, qc] += gv[:, :BLK]
            dv[hr, ec] += gv[:, BLK:]
        return carry

    lax.fori_loop(0, HEADS, head, 0)
    dk_ref[...] = dk[:, :TOK]
    dv_ref[...] = dv[:, :TOK]
    dkp_ref[...] = dk[:, TOK:].astype(BF16)
    dvp_ref[...] = dv[:, TOK:].astype(BF16)


def final_kernel(
    code_ref, xt_ref, dq_ref, dk_ref, dv_ref, rk_ref, rv_ref, wqkv_ref, gfirst_ref, gvec_ref,
    gin_ref, keep_ref, send_ref, gk, gv,
):
    core, low, far = code_ref[0], code_ref[1], code_ref[3]
    gk[:, :EXT] = (dk_ref[:, :EXT] + rk_ref[...].astype(F32)).astype(BF16)
    gk[:, EXT:] = dk_ref[:, EXT:].astype(BF16)
    gv[:, :EXT] = (dv_ref[:, :EXT] + rv_ref[...].astype(F32)).astype(BF16)
    gv[:, EXT:] = dv_ref[:, EXT:].astype(BF16)
    for g in range(GROUPS):
        gr = slice(g * GD, (g + 1) * GD)
        through = (
            nn(wqkv_ref[0, g], dq_ref[gr, :]) + nn(wqkv_ref[1, g], gk[gr, :]) + nn(wqkv_ref[2, g], gv[gr, :])
        )
        gin_ref[:, gr] = (gfirst_ref[gr, :] + through).astype(BF16).T
    for jj in range(GROUPS):
        g = jj ^ (2 * core)
        gr = pl.ds(pl.multiple_of(g * GD, GD), GD)
        xg = xt_ref[gr, :]
        parts = [nt(xg, dq_ref[gr, :]), nt(xg, gk[gr, :]), nt(xg, gv[gr, :])]
        pad = jnp.zeros((GD, QCHUNK[1] - 3 * GD - 4), F32)
        row = jnp.concatenate(parts + [gvec_ref[gr, :], pad], 1)
        for r in range(8):
            piece = row[24 * r : 24 * (r + 1)]
            pos = ((g & 1) * 8 + r) ^ (low if jj < 2 else far)
            if jj < 2:
                keep_ref[pos] = piece
            else:
                send_ref[pos] = piece.astype(BF16)


def finish_kernel(code_ref, m_ref, q_ref, g1_ref, g2_ref, go_ref, gq_ref, gvec_ref):
    core, low, far = code_ref[0], code_ref[1], code_ref[3]
    for half in range(2):
        base = half ^ core
        low_of = far if half else low
        for a in range(16):
            part = m_ref[half * 16 + (a ^ low_of)].astype(F32)
            g = base * 2 + a // 8
            rows = slice(48 * (a % 8 // 2), 48 * (a % 8 // 2 + 1))
            lanes = slice(384 * (a % 2), 384 * (a % 2 + 1))
            g1_ref[g, rows, lanes] = part[:48]
            g2_ref[g, rows, lanes] = part[48:96]
            go_ref[g, rows, lanes] = part[96:]
        for a in range(16):
            part = q_ref[half * 16 + (a ^ low_of)].astype(F32)
            g = base * 2 + a // 8
            rows = slice(24 * (a % 8), 24 * (a % 8 + 1))
            for t in range(3):
                gq_ref[t, g, rows] = part[:, t * GD : (t + 1) * GD]
            gvec_ref[g, rows] = part[:, 3 * GD : 3 * GD + 4]


def call(kernel, outs, scratch, *args, flops=0, name=None):
    smem = pl.BlockSpec(memory_space=pltpu.SMEM)
    vmem = pl.BlockSpec(memory_space=pltpu.VMEM)
    return pl.pallas_call(
        kernel,
        out_shape=[jax.ShapeDtypeStruct(s, d) for s, d in outs],
        in_specs=[smem] + [vmem] * (len(args) - 1),
        out_specs=[vmem] * len(outs),
        scratch_shapes=[pltpu.VMEM(s, d) for s, d in scratch],
        compiler_params=pltpu.CompilerParams(vmem_limit_bytes=VMEM_LIMIT),
        name=name,
    )(*args)


class Links:
    def __init__(self, n_seq):
        bits = max(n_seq.bit_length() - 1, 0)
        self.n = n_seq * 2
        orders = [list(range(bits)), [1, 0] + list(range(2, bits))] if bits > 1 else [list(range(bits))] * 2
        self.orders = orders
        self.halving = min(4, bits)
        self.bits = bits

    def pairs(self, step):
        if step < 0:
            return [(i, i ^ 1) for i in range(self.n)]
        return [(i, i ^ (2 << self.orders[i & 1][step])) for i in range(self.n)]

    def code(self, seq, core):
        def of(order):
            value = 0
            for step in range(4):
                value = value * 2 + (((seq >> order[step]) & 1) if step < self.halving else 0)
            return value

        return jnp.where(core == 0, of(self.orders[0]), of(self.orders[1]))


def swap(x, links, step):
    return lax.ppermute(x, "dev", links.pairs(step))


def all_sum(keep, send, links):
    total = keep + swap(send, links, -1).astype(F32)
    for step in range(links.halving):
        half = total.shape[0] // 2
        total = total[:half] + swap(total[half:].astype(BF16), links, step).astype(F32)
    piece = total.astype(BF16)
    for step in range(links.halving, links.bits):
        piece = (piece.astype(F32) + swap(piece, links, step).astype(F32)).astype(BF16)
    for step in reversed(range(-1, links.halving)):
        piece = jnp.concatenate([piece, swap(piece, links, step)], 0)
    return piece


def per_device(
    links, inputs, segment_ids, qkv_weight, out_weight, ffn_in_weight, ffn_out_weight,
    attn_gain, attn_shift, ffn_gain, ffn_shift, out_cotangent,
):
    me = lax.axis_index("dev")
    seq, core = me >> 1, me & 1
    code = jnp.stack([core, links.code(seq, core), (segment_ids[BLK] == 1).astype(jnp.int32), links.code(seq, 1 - core)]).astype(jnp.int32)
    partner = swap(inputs[:EXT], links, -1)
    segr = segment_ids[None, :]
    segc = segment_ids[:, None]
    norms = jnp.stack((attn_gain, attn_shift, ffn_gain, ffn_shift), 1)
    (output, xt, q, k, v, gctx, lse, gfirst, keep, send, gvec) = call(
        layer_kernel,
        [
            ((TOK, D), BF16), ((D, ALL), BF16), ((D, TOK), BF16), ((D, ALL), BF16), ((D, ALL), BF16),
            ((D, TOK), BF16), ((HEADS, 1, TOK), F32), ((D, TOK), F32),
            ((16,) + CHUNK, F32), ((16,) + CHUNK, BF16), ((D, 4), F32),
        ],
        [
            ((2, 2 * BLK, BLK), F32), ((D, D), BF16), ((GROUPS, GF, GD), BF16), ((GROUPS, GF, GD), BF16),
            ((D, TOK), BF16), ((D, TOK), BF16), ((GROUPS, GF, TOK), BF16), ((GROUPS, GF, TOK), BF16),
            ((GROUPS, GF, BLK), F32), ((D, TOK), BF16), ((D, TOK), BF16), ((4, D, 128), F32), ((4, D, 128), F32),
        ],
        code, inputs, partner, segr, segc, qkv_weight, out_weight, ffn_in_weight, jnp.swapaxes(ffn_out_weight, 1, 2), norms, out_cotangent,
        name="layer",
    )
    dq, dk, dv, dkp, dvp = call(
        back_kernel,
        [((D, TOK), BF16), ((D, TOK), F32), ((D, TOK), F32), ((D, EXT), BF16), ((D, EXT), BF16)],
        [((2, 2 * BLK, BLK), F32), ((D, ALL), F32), ((D, ALL), F32)],
        code, q, k, v, gctx, lse, segr, segc,
        name="attention_back",
    )
    rk = swap(dkp, links, -1)
    rv = swap(dvp, links, -1)
    two = code[2] == 1
    rk = jnp.where(two | (jnp.arange(EXT) < BLK)[None, :], rk, 0)
    rv = jnp.where(two | (jnp.arange(EXT) < BLK)[None, :], rv, 0)
    grad_input, keep_q, send_q = call(
        final_kernel,
        [((TOK, D), BF16), ((16,) + QCHUNK, F32), ((16,) + QCHUNK, BF16)],
        [((D, TOK), BF16), ((D, TOK), BF16)],
        code, xt[:, :TOK], dq, dk, dv, rk, rv, qkv_weight, gfirst, gvec,
        name="through_qkv",
    )
    m = all_sum(keep, send, links)
    mq = all_sum(keep_q, send_q, links)
    g1, g2, go, gq, gv = call(
        finish_kernel,
        [((GROUPS, GD, GF), F32), ((GROUPS, GD, GF), F32), ((GROUPS, GD, D), F32), ((3, GROUPS, GD, GD), F32), ((GROUPS, GD, 4), F32)],
        [],
        code, m, mq,
        name="finish",
    )
    gv = gv.reshape(D, 4)
    return (output, grad_input, gq, go.reshape(D, D), g1, jnp.swapaxes(g2, 1, 2), gv[:, 0], gv[:, 1], gv[:, 2], gv[:, 3])


def solution(mesh):
    flat = Mesh(mesh.devices.reshape(-1), ("dev",))
    links = Links(mesh.shape["seq"])
    split, copied = P("dev"), P()
    return jax.shard_map(
        partial(per_device, links),
        mesh=flat,
        in_specs=(split, split) + (copied,) * 8 + (split,),
        out_specs=(split, split) + (copied,) * 8,
        check_vma=False,
    )
```

time: 562 us -> 208 us (0.37)
  matrix products: 181 us -> 0 us
  Pallas kernels: 0 us -> 97.7 us
  waiting for transfers between devices: 143 us -> 60.5 us
  other arithmetic: 76.5 us -> 6.18 us
  local copies, waits for them, and re-layouts: 81 us -> 17.1 us
  blocking collectives: 44 us -> 0 us
  starting transfers between devices: 0.67 us -> 24.5 us
  loops' own time: 16.3 us -> 0 us
  between operations: 14.8 us -> 1.61 us
    dot_general x33 -> x0, matrix products: 181 us -> none  [the longest x3 51 us: one_block(): jnp.einsum('qhe,khe->hqk', grad_h, value_h, preferred_element_type=jnp.fl...]
    psum x1 -> x0, waiting for transfers between devices: 143 us -> none  [per_device(): lax.psum((grad_qkv, grad_out, grad_ffn_in, grad_ffn_out, grad_attn_gain,...]
    pallas_call x0 -> x4, Pallas kernels: none -> 97.7 us  [call(): pl.pallas_call(kernel, out_shape=[jax.ShapeDtypeStruct(s, d) for s, d in...]
    ppermute x3 -> x23, waiting for transfers between devices: 0.01 us -> 60.5 us  [swap(): return lax.ppermute(x, 'dev', links.pairs(step))]
    psum x1 -> x0, blocking collectives: 44 us -> none  [per_device(): lax.psum((grad_qkv, grad_out, grad_ffn_in, grad_ffn_out, grad_attn_gain,...]
    convert_element_type x7 -> x0, other arithmetic: 42 us -> none  [the longest x3 40.2 us: one_block(): (softmax * (grad_probs - row_dots[..., None])).astype(jnp.bfloat16)]
    reduce_sum x8 -> x0, other arithmetic: 24.2 us -> none  [the longest x3 17.7 us: one_block(): jnp.sum(jnp.exp(scores - row_top), -1, keepdims=True)]
    ppermute x3 -> x23, starting transfers between devices: 0.63 us -> 24.5 us  [swap(): return lax.ppermute(x, 'dev', links.pairs(step))]
  transfers between devices with their start and end apart: 4 -> 23, of which waited for: 1 -> 14; matrix products, arithmetic and copies ran while one was open for 4% -> 7% of each run, Pallas kernels for 0% -> 18%
where the time goes in v1:
time: 208 us
  Pallas kernels  97.7 us (47%)
  waiting for transfers between devices  60.5 us (29%)
  starting transfers between devices  24.5 us (12%)
  local copies, waits for them, and re-layouts  17.1 us (8%)
  other arithmetic  6.18 us (3%)
    pallas_call x4, Pallas kernels, call(): pl.pallas_call(kernel, out_shape=[jax.ShapeDtypeStruct(s, d) for s, d in...  97.7 us
    ppermute x23, waiting for transfers between devices, swap(): return lax.ppermute(x, 'dev', links.pairs(step))  60.5 us
    ppermute x23, starting transfers between devices, swap(): return lax.ppermute(x, 'dev', links.pairs(step))  24.5 us
  transfers between devices with their start and end apart: 23, of which 14 were waited for; matrix products, arithmetic and copies ran while one was open for 7% of the time, Pallas kernels for 18%

profile of v1, /device:TPU:1, one launch (start us, length us, event | category | flops | bytes accessed | tf_op | source)
XLA Modules:
  0.0 207.6 jit_solution(3490753393539108155)
XLA Ops:
  4.5 1.6 broadcast_in_dim.28.segc_ref
  9.3 54.0 %layer.1 = (bf16[768,768]{1,0:T(8,128)(2,1)}, bf16[768,1280]{1,0:T(8,128)(2,1)}, bf16[768,768]{1,0:T(8,128)(2,1)}, bf16[768,1280]{1,0:T(8,128)(2,1)}, bf16[768,1...) custom-call(s32[4]{0:T(128)} %pad_add_fusion.code_ref, ...), custom_call_target="tpu_custom_call" | custom-call | tf_op jit(solution)/shard_map/layer/pallas_call | solution.py:308
  63.7 3.5 %collective-permute-done.3 = bf16[16,144,384]{2,1,0:T(8,128)(2,1)S(1)} collective-permute-done((bf16[16,144,384]{2,1,0:T(8,128)(2,1)}, bf16[16,144,384]{2,1,0:T(8,128)(2,1)S(1)}, u32[]{:S(2)}, u32[]{:S(2)}) %collective-permute-start.3) | collective-permute-done | bytes 1769504 | tf_op jit(solution)/shard_map/ppermute | solution.py:344
  67.3 2.3 %convert_add_fusion = f32[16,144,384]{2,1,0:T(8,128)S(1)} fusion(f32[16,144,384]{2,1,0:T(8,128)} %get-tuple-element.49, bf16[16,144,384]{2,1,0:T(8,128)(2,1)S(1)} %collective-permute-done.3), kind=kLoop, calls=%fused_computation | loop fusion | flops 1769472 | bytes 8847360 | tf_op jit(solution)/shard_map/add | solution.py:348
  69.7 2.6 %collective-permute-start.4 = (bf16[8,144,384]{2,1,0:T(8,128)(2,1)S(1)}, bf16[8,144,384]{2,1,0:T(8,128)(2,1)S(1)}, u32[]{:S(2)}, u32[]{:S(2)}) collective-permute-start(bf16[8,144,384]{2,1,0:T(8,128)(2,1)S(1)} %slice.144), channel_id=1, source_target_pairs={{0,2},{1,5},{2,0},{3,7},{4,6},{5,1},{6,4},{7,3},{8,10},{9,13},{10,... | collective-permute-start | bytes 2654216 | tf_op jit(solution)/shard_map/ppermute | solution.py:344
  72.3 10.7 %collective-permute-done.4 = bf16[8,144,384]{2,1,0:T(8,128)(2,1)S(1)} collective-permute-done((bf16[8,144,384]{2,1,0:T(8,128)(2,1)S(1)}, bf16[8,144,384]{2,1,0:T(8,128)(2,1)S(1)}, u32[]{:S(2)}, u32[]{:S(2)}) %collective-permute-start.4) | collective-permute-done | bytes 884768 | tf_op jit(solution)/shard_map/ppermute | solution.py:344
  84.8 29.3 %attention_back.1 = (bf16[768,768]{1,0:T(8,128)(2,1)}, f32[768,768]{1,0:T(8,128)}, f32[768,768]{1,0:T(8,128)}, bf16[768,512]{1,0:T(8,128)(2,1)}, bf16[768,512]{1,0:T(8,128)(2,1)}) custom-call(s32[4]{0:T(128)} %pad_add_fusion.code_ref, bf16[768,768]{1,0:T(8,128)(2,1)} %get-tuple-element.36.q_ref, bf16[768,1280]{1,0:T(8,128)(2,1)} %get-tuple-element.37.k_ref, ...), custom_call_target="tpu_custom_call" | custom-call | tf_op jit(solution)/shard_map/attention_back/pallas_call | solution.py:308
  118.2 4.0 %collective-permute-done.6 = bf16[2,144,384]{2,1,0:T(8,128)(2,1)S(1)} collective-permute-done((bf16[2,144,384]{2,1,0:T(8,128)(2,1)S(1)}, bf16[2,144,384]{2,1,0:T(8,128)(2,1)S(1)}, u32[]{:S(2)}, u32[]{:S(2)}) %collective-permute-start.6) | collective-permute-done | bytes 221216 | tf_op jit(solution)/shard_map/ppermute | solution.py:344
  122.3 2.5 %collective-permute-start.7 = (bf16[1,144,384]{2,1,0:T(8,128)(2,1)S(1)}, bf16[1,144,384]{2,1,0:T(8,128)(2,1)S(1)}, u32[]{:S(2)}, u32[]{:S(2)}) collective-permute-start(bf16[1,144,384]{2,1,0:T(8,128)(2,1)S(1)} %slice.149), channel_id=1, source_target_pairs={{0,16},{1,17},{2,18},{3,19},{4,20},{5,21},{6,22},{7,23},{8,24},{9,... | collective-permute-start | bytes 331784 | tf_op jit(solution)/shard_map/ppermute | solution.py:344
  126.1 8.0 %through_qkv.1 = (bf16[768,768]{1,0:T(8,128)(2,1)}, f32[16,24,640]{2,1,0:T(8,128)}, bf16[16,24,640]{2,1,0:T(8,128)(2,1)}) custom-call(s32[4]{0:T(128)} %pad_add_fusion.code_ref, bf16[768,768]{1,0:T(8,128)(2,1)} %slice.79.xt_ref, bf16[768,768]{1,0:T(8,128)(2,1)} %get-tuple-element.41.dq_ref, f32[768,768]{1,0:T(8,128)} %get-tuple-element.42.dk_ref, ...), custom_call_target="tpu_custom_call" | custom-call | tf_op jit(solution)/shard_map/through_qkv/pallas_call | solution.py:308
  134.1 1.6 collective-permute-start.13
  135.7 7.9 %collective-permute-done.8 = bf16[1,144,384]{2,1,0:T(8,128)(2,1)S(1)} collective-permute-done((bf16[1,144,384]{2,1,0:T(8,128)(2,1)S(1)}, bf16[1,144,384]{2,1,0:T(8,128)(2,1)S(1)}, u32[]{:S(2)}, u32[]{:S(2)}) %collective-permute-start.8) | collective-permute-done | bytes 110624 | tf_op jit(solution)/shard_map/ppermute | solution.py:344
  145.5 4.5 %collective-permute-done.9 = bf16[2,144,384]{2,1,0:T(8,128)(2,1)S(1)} collective-permute-done((bf16[2,144,384]{2,1,0:T(8,128)(2,1)S(1)}, bf16[2,144,384]{2,1,0:T(8,128)(2,1)S(1)}, u32[]{:S(2)}, u32[]{:S(2)}) %collective-permute-start.9) | collective-permute-done | bytes 221216 | tf_op jit(solution)/shard_map/ppermute | solution.py:344
  151.8 5.7 %collective-permute-done.10 = bf16[4,144,384]{2,1,0:T(8,128)(2,1)S(1)} collective-permute-done((bf16[4,144,384]{2,1,0:T(8,128)(2,1)S(1)}, bf16[4,144,384]{2,1,0:T(8,128)(2,1)S(1)}, u32[]{:S(2)}, u32[]{:S(2)}) %collective-permute-start.10) | collective-permute-done | bytes 442400 | tf_op jit(solution)/shard_map/ppermute | solution.py:344
  159.7 2.3 %collective-permute-done.16 = bf16[2,24,640]{2,1,0:T(8,128)(2,1)S(1)} collective-permute-done((bf16[2,24,640]{2,1,0:T(8,128)(2,1)S(1)}, bf16[2,24,640]{2,1,0:T(8,128)(2,1)S(1)}, u32[]{:S(2)}, u32[]{:S(2)}) %collective-permute-start.16) | collective-permute-done | bytes 61472 | tf_op jit(solution)/shard_map/ppermute | solution.py:344
  165.9 4.6 %collective-permute-done.11 = bf16[8,144,384]{2,1,0:T(8,128)(2,1)S(1)} collective-permute-done((bf16[8,144,384]{2,1,0:T(8,128)(2,1)S(1)}, bf16[8,144,384]{2,1,0:T(8,128)(2,1)S(1)}, u32[]{:S(2)}, u32[]{:S(2)}) %collective-permute-start.11) | collective-permute-done | bytes 884768 | tf_op jit(solution)/shard_map/ppermute | solution.py:344
  171.5 2.8 %collective-permute-start.12 = (bf16[16,144,384]{2,1,0:T(8,128)(2,1)S(1)}, bf16[16,144,384]{2,1,0:T(8,128)(2,1)S(1)}, u32[]{:S(2)}, u32[]{:S(2)}) collective-permute-start(bf16[16,144,384]{2,1,0:T(8,128)(2,1)S(1)} %get-tuple-element.66), channel_id=1, source_target_pairs={{0,1},{1,0},{2,3},{3,2},{4,5},{5,4},{6,7},{7,6},{8,9},{9,8},{10,11... | collective-permute-start | bytes 5308424 | tf_op jit(solution)/shard_map/ppermute | solution.py:344
  174.5 4.4 %collective-permute-done.18 = bf16[1,24,640]{2,1,0:T(8,128)(2,1)S(1)} collective-permute-done((bf16[1,24,640]{2,1,0:T(8,128)(2,1)S(1)}, bf16[1,24,640]{2,1,0:T(8,128)(2,1)S(1)}, u32[]{:S(2)}, u32[]{:S(2)}) %collective-permute-start.18) | collective-permute-done | bytes 30752 | tf_op jit(solution)/shard_map/ppermute | solution.py:344
  179.0 3.1 %collective-permute-done.19 = bf16[2,24,640]{2,1,0:T(8,128)(2,1)S(1)} collective-permute-done((bf16[2,24,640]{2,1,0:T(8,128)(2,1)S(1)}, bf16[2,24,640]{2,1,0:T(8,128)(2,1)S(1)}, u32[]{:S(2)}, u32[]{:S(2)}) %collective-permute-start.19) | collective-permute-done | bytes 61472 | tf_op jit(solution)/shard_map/ppermute | solution.py:344
  183.3 2.6 %collective-permute-done.20 = bf16[4,24,640]{2,1,0:T(8,128)(2,1)S(1)} collective-permute-done((bf16[4,24,640]{2,1,0:T(8,128)(2,1)S(1)}, bf16[4,24,640]{2,1,0:T(8,128)(2,1)S(1)}, u32[]{:S(2)}, u32[]{:S(2)}) %collective-permute-start.20) | collective-permute-done | bytes 122912 | tf_op jit(solution)/shard_map/ppermute | solution.py:344
  186.4 4.7 %collective-permute-done.21 = bf16[8,24,640]{2,1,0:T(8,128)(2,1)S(1)} collective-permute-done((bf16[8,24,640]{2,1,0:T(8,128)(2,1)S(1)}, bf16[8,24,640]{2,1,0:T(8,128)(2,1)S(1)}, u32[]{:S(2)}, u32[]{:S(2)}) %collective-permute-start.21) | collective-permute-done | bytes 245792 | tf_op jit(solution)/shard_map/ppermute | solution.py:344
  191.1 4.0 %collective-permute-start.22 = (bf16[16,24,640]{2,1,0:T(8,128)(2,1)S(1)}, bf16[16,24,640]{2,1,0:T(8,128)(2,1)S(1)}, u32[]{:S(2)}, u32[]{:S(2)}) collective-permute-start(bf16[16,24,640]{2,1,0:T(8,128)(2,1)S(1)} %get-tuple-element.70), channel_id=1, source_target_pairs={{0,1},{1,0},{2,3},{3,2},{4,5},{5,4},{6,7},{7,6},{8,9},{9,8},{10,11... | collective-permute-start | bytes 1474568 | tf_op jit(solution)/shard_map/ppermute | solution.py:344
  198.3 6.4 %finish.1 = (f32[4,192,768]{2,1,0:T(8,128)}, f32[4,192,768]{2,1,0:T(8,128)}, f32[4,192,768]{2,1,0:T(8,128)}, f32[3,4,192,192]{3,2,1,0:T(8,128)}, f32[4,192,4]{2,1,0:T(8,128)}) custom-call(s32[4]{0:T(128)} %pad_add_fusion.code_ref, bf16[32,144,384]{2,1,0:T(8,128)(2,1)} %constant_dynamic-update-slice_fusion.5.m_ref, bf16[32,24,640]{2,1,0:T(8,128)(2,1)} %copy-done), custom_call_target="tpu_custom_call" | custom-call | tf_op jit(solution)/shard_map/finish/pallas_call | solution.py:308
  204.7 2.9 %slice_reduce_fusion = (f32[768]{0:T(1024)}, f32[768]{0:T(1024)}, f32[768]{0:T(1024)}, f32[768]{0:T(1024)}) fusion(f32[768,4]{1,0:T(8,128)} %bitcast.8), kind=kLoop, calls=%fused_computation.14 | loop fusion | bytes 24576 | tf_op jit(solution)/shard_map/slice | solution.py:415
  (91 shorter events, 29.7 us)
Async XLA Ops:
  0.7 6.1 %copy-start.6 = (f32[768]{0:T(1024)S(1)}, f32[768]{0:T(1024)}, u32[]{:S(2)}) copy-start(f32[768]{0:T(1024)} %param.20) | copy-start | bytes 9220
  1.9 6.5 %collective-permute-start = (bf16[512,768]{1,0:T(8,128)(2,1)S(1)}, bf16[512,768]{1,0:T(8,128)(2,1)S(1)}, u32[]{:S(2)}, u32[]{:S(2)}) collective-permute-start(bf16[512,768]{1,0:T(8,128)(2,1)S(1)} %slice.78), channel_id=1, source_target_pairs={{0,1},{1,0},{2,3},{3,2},{4,5},{5,4},{6,7},{7,6},{8,9},{9,8},{10,11... | collective-permute-start | bytes 2359304 | tf_op jit(solution)/shard_map/ppermute | solution.py:344
  63.3 4.0 %collective-permute-start.3 = (bf16[16,144,384]{2,1,0:T(8,128)(2,1)}, bf16[16,144,384]{2,1,0:T(8,128)(2,1)S(1)}, u32[]{:S(2)}, u32[]{:S(2)}) collective-permute-start(bf16[16,144,384]{2,1,0:T(8,128)(2,1)} %get-tuple-element.50), channel_id=1, source_target_pairs={{0,1},{1,0},{2,3},{3,2},{4,5},{5,4},{6,7},{7,6},{8,9},{9,8},{10,11... | collective-permute-start | bytes 5308424 | tf_op jit(solution)/shard_map/ppermute | solution.py:344
  69.7 13.4 %collective-permute-start.4 = (bf16[8,144,384]{2,1,0:T(8,128)(2,1)S(1)}, bf16[8,144,384]{2,1,0:T(8,128)(2,1)S(1)}, u32[]{:S(2)}, u32[]{:S(2)}) collective-permute-start(bf16[8,144,384]{2,1,0:T(8,128)(2,1)S(1)} %slice.144), channel_id=1, source_target_pairs={{0,2},{1,5},{2,0},{3,7},{4,6},{5,1},{6,4},{7,3},{8,10},{9,13},{10,... | collective-permute-start | bytes 2654216 | tf_op jit(solution)/shard_map/ppermute | solution.py:344
  83.3 32.2 %collective-permute-start.5 = (bf16[4,144,384]{2,1,0:T(8,128)(2,1)S(1)}, bf16[4,144,384]{2,1,0:T(8,128)(2,1)S(1)}, u32[]{:S(2)}, u32[]{:S(2)}) collective-permute-start(bf16[4,144,384]{2,1,0:T(8,128)(2,1)S(1)} %slice.145), channel_id=1, source_target_pairs={{0,4},{1,3},{2,6},{3,1},{4,0},{5,7},{6,2},{7,5},{8,12},{9,11},{10,... | collective-permute-start | bytes 1327112 | tf_op jit(solution)/shard_map/ppermute | solution.py:344
  114.1 10.7 %collective-permute-start.1 = (bf16[768,512]{1,0:T(8,128)(2,1)}, bf16[768,512]{1,0:T(8,128)(2,1)S(1)}, u32[]{:S(2)}, u32[]{:S(2)}) collective-permute-start(bf16[768,512]{1,0:T(8,128)(2,1)} %get-tuple-element.44), channel_id=1, source_target_pairs={{0,1},{1,0},{2,3},{3,2},{4,5},{5,4},{6,7},{7,6},{8,9},{9,8},{10,11... | collective-permute-start | bytes 2359304 | tf_op jit(solution)/shard_map/ppermute | solution.py:344
  115.4 9.4 %collective-permute-start.2 = (bf16[768,512]{1,0:T(8,128)(2,1)}, bf16[768,512]{1,0:T(8,128)(2,1)S(1)}, u32[]{:S(2)}, u32[]{:S(2)}) collective-permute-start(bf16[768,512]{1,0:T(8,128)(2,1)} %get-tuple-element.45), channel_id=1, source_target_pairs={{0,1},{1,0},{2,3},{3,2},{4,5},{5,4},{6,7},{7,6},{8,9},{9,8},{10,11... | collective-permute-start | bytes 2359304 | tf_op jit(solution)/shard_map/ppermute | solution.py:344
  115.6 6.6 %collective-permute-start.6 = (bf16[2,144,384]{2,1,0:T(8,128)(2,1)S(1)}, bf16[2,144,384]{2,1,0:T(8,128)(2,1)S(1)}, u32[]{:S(2)}, u32[]{:S(2)}) collective-permute-start(bf16[2,144,384]{2,1,0:T(8,128)(2,1)S(1)} %slice.147), channel_id=1, source_target_pairs={{0,8},{1,9},{2,10},{3,11},{4,12},{5,13},{6,14},{7,15},{8,0},{9,1},... | collective-permute-start | bytes 663560 | tf_op jit(solution)/shard_map/ppermute | solution.py:344
  122.3 13.3 %collective-permute-start.7 = (bf16[1,144,384]{2,1,0:T(8,128)(2,1)S(1)}, bf16[1,144,384]{2,1,0:T(8,128)(2,1)S(1)}, u32[]{:S(2)}, u32[]{:S(2)}) collective-permute-start(bf16[1,144,384]{2,1,0:T(8,128)(2,1)S(1)} %slice.149), channel_id=1, source_target_pairs={{0,16},{1,17},{2,18},{3,19},{4,20},{5,21},{6,22},{7,23},{8,24},{9,... | collective-permute-start | bytes 331784 | tf_op jit(solution)/shard_map/ppermute | solution.py:344
  134.1 9.7 %collective-permute-start.13 = (bf16[16,24,640]{2,1,0:T(8,128)(2,1)}, bf16[16,24,640]{2,1,0:T(8,128)(2,1)S(1)}, u32[]{:S(2)}, u32[]{:S(2)}) collective-permute-start(bf16[16,24,640]{2,1,0:T(8,128)(2,1)} %get-tuple-element.52), channel_id=1, source_target_pairs={{0,1},{1,0},{2,3},{3,2},{4,5},{5,4},{6,7},{7,6},{8,9},{9,8},{10,11... | collective-permute-start | bytes 1474568 | tf_op jit(solution)/shard_map/ppermute | solution.py:344
  135.7 8.0 %collective-permute-start.8 = (bf16[1,144,384]{2,1,0:T(8,128)(2,1)S(1)}, bf16[1,144,384]{2,1,0:T(8,128)(2,1)S(1)}, u32[]{:S(2)}, u32[]{:S(2)}) collective-permute-start(bf16[1,144,384]{2,1,0:T(8,128)(2,1)S(1)} %get-tuple-element.65), channel_id=1, source_target_pairs={{0,16},{1,17},{2,18},{3,19},{4,20},{5,21},{6,22},{7,23},{8,24},{9,... | collective-permute-start | bytes 331784 | tf_op jit(solution)/shard_map/ppermute | solution.py:344
  143.7 6.2 %collective-permute-start.9 = (bf16[2,144,384]{2,1,0:T(8,128)(2,1)S(1)}, bf16[2,144,384]{2,1,0:T(8,128)(2,1)S(1)}, u32[]{:S(2)}, u32[]{:S(2)}) collective-permute-start(bf16[2,144,384]{2,1,0:T(8,128)(2,1)S(1)} %pad_maximum_fusion.3), channel_id=1, source_target_pairs={{0,8},{1,9},{2,10},{3,11},{4,12},{5,13},{6,14},{7,15},{8,0},{9,1},... | collective-permute-start | bytes 663560 | tf_op jit(solution)/shard_map/ppermute | solution.py:344
  145.1 6.1 %collective-permute-start.14 = (bf16[8,24,640]{2,1,0:T(8,128)(2,1)S(1)}, bf16[8,24,640]{2,1,0:T(8,128)(2,1)S(1)}, u32[]{:S(2)}, u32[]{:S(2)}) collective-permute-start(bf16[8,24,640]{2,1,0:T(8,128)(2,1)S(1)} %slice.146), channel_id=1, source_target_pairs={{0,2},{1,5},{2,0},{3,7},{4,6},{5,1},{6,4},{7,3},{8,10},{9,13},{10,... | collective-permute-start | bytes 737288 | tf_op jit(solution)/shard_map/ppermute | solution.py:344
  150.0 7.5 %collective-permute-start.10 = (bf16[4,144,384]{2,1,0:T(8,128)(2,1)S(1)}, bf16[4,144,384]{2,1,0:T(8,128)(2,1)S(1)}, u32[]{:S(2)}, u32[]{:S(2)}) collective-permute-start(bf16[4,144,384]{2,1,0:T(8,128)(2,1)S(1)} %pad_maximum_fusion.1), channel_id=1, source_target_pairs={{0,4},{1,3},{2,6},{3,1},{4,0},{5,7},{6,2},{7,5},{8,12},{9,11},{10,... | collective-permute-start | bytes 1327112 | tf_op jit(solution)/shard_map/ppermute | solution.py:344
  151.3 7.6 %collective-permute-start.15 = (bf16[4,24,640]{2,1,0:T(8,128)(2,1)S(1)}, bf16[4,24,640]{2,1,0:T(8,128)(2,1)S(1)}, u32[]{:S(2)}, u32[]{:S(2)}) collective-permute-start(bf16[4,24,640]{2,1,0:T(8,128)(2,1)S(1)} %slice.148), channel_id=1, source_target_pairs={{0,4},{1,3},{2,6},{3,1},{4,0},{5,7},{6,2},{7,5},{8,12},{9,11},{10,... | collective-permute-start | bytes 368648 | tf_op jit(solution)/shard_map/ppermute | solution.py:344
  157.6 12.8 %collective-permute-start.11 = (bf16[8,144,384]{2,1,0:T(8,128)(2,1)S(1)}, bf16[8,144,384]{2,1,0:T(8,128)(2,1)S(1)}, u32[]{:S(2)}, u32[]{:S(2)}) collective-permute-start(bf16[8,144,384]{2,1,0:T(8,128)(2,1)S(1)} %pad_maximum_fusion), channel_id=1, source_target_pairs={{0,2},{1,5},{2,0},{3,7},{4,6},{5,1},{6,4},{7,3},{8,10},{9,13},{10,... | collective-permute-start | bytes 2654216 | tf_op jit(solution)/shard_map/ppermute | solution.py:344
  158.9 3.1 %collective-permute-start.16 = (bf16[2,24,640]{2,1,0:T(8,128)(2,1)S(1)}, bf16[2,24,640]{2,1,0:T(8,128)(2,1)S(1)}, u32[]{:S(2)}, u32[]{:S(2)}) collective-permute-start(bf16[2,24,640]{2,1,0:T(8,128)(2,1)S(1)} %slice.150), channel_id=1, source_target_pairs={{0,8},{1,9},{2,10},{3,11},{4,12},{5,13},{6,14},{7,15},{8,0},{9,1},... | collective-permute-start | bytes 184328 | tf_op jit(solution)/shard_map/ppermute | solution.py:344
  162.1 12.3 %collective-permute-start.17 = (bf16[1,24,640]{2,1,0:T(8,128)(2,1)S(1)}, bf16[1,24,640]{2,1,0:T(8,128)(2,1)S(1)}, u32[]{:S(2)}, u32[]{:S(2)}) collective-permute-start(bf16[1,24,640]{2,1,0:T(8,128)(2,1)S(1)} %slice.151), channel_id=1, source_target_pairs={{0,16},{1,17},{2,18},{3,19},{4,20},{5,21},{6,22},{7,23},{8,24},{9,... | collective-permute-start | bytes 92168 | tf_op jit(solution)/shard_map/ppermute | solution.py:344
  171.5 25.2 %collective-permute-start.12 = (bf16[16,144,384]{2,1,0:T(8,128)(2,1)S(1)}, bf16[16,144,384]{2,1,0:T(8,128)(2,1)S(1)}, u32[]{:S(2)}, u32[]{:S(2)}) collective-permute-start(bf16[16,144,384]{2,1,0:T(8,128)(2,1)S(1)} %get-tuple-element.66), channel_id=1, source_target_pairs={{0,1},{1,0},{2,3},{3,2},{4,5},{5,4},{6,7},{7,6},{8,9},{9,8},{10,11... | collective-permute-start | bytes 5308424 | tf_op jit(solution)/shard_map/ppermute | solution.py:344
  174.4 4.6 %collective-permute-start.18 = (bf16[1,24,640]{2,1,0:T(8,128)(2,1)S(1)}, bf16[1,24,640]{2,1,0:T(8,128)(2,1)S(1)}, u32[]{:S(2)}, u32[]{:S(2)}) collective-permute-start(bf16[1,24,640]{2,1,0:T(8,128)(2,1)S(1)} %get-tuple-element.63), channel_id=1, source_target_pairs={{0,16},{1,17},{2,18},{3,19},{4,20},{5,21},{6,22},{7,23},{8,24},{9,... | collective-permute-start | bytes 92168 | tf_op jit(solution)/shard_map/ppermute | solution.py:344
  179.0 3.1 %collective-permute-start.19 = (bf16[2,24,640]{2,1,0:T(8,128)(2,1)S(1)}, bf16[2,24,640]{2,1,0:T(8,128)(2,1)S(1)}, u32[]{:S(2)}, u32[]{:S(2)}) collective-permute-start(bf16[2,24,640]{2,1,0:T(8,128)(2,1)S(1)} %pad_maximum_fusion.5), channel_id=1, source_target_pairs={{0,8},{1,9},{2,10},{3,11},{4,12},{5,13},{6,14},{7,15},{8,0},{9,1},... | collective-permute-start | bytes 184328 | tf_op jit(solution)/shard_map/ppermute | solution.py:344
  182.1 3.8 %collective-permute-start.20 = (bf16[4,24,640]{2,1,0:T(8,128)(2,1)S(1)}, bf16[4,24,640]{2,1,0:T(8,128)(2,1)S(1)}, u32[]{:S(2)}, u32[]{:S(2)}) collective-permute-start(bf16[4,24,640]{2,1,0:T(8,128)(2,1)S(1)} %pad_maximum_fusion.4), channel_id=1, source_target_pairs={{0,4},{1,3},{2,6},{3,1},{4,0},{5,7},{6,2},{7,5},{8,12},{9,11},{10,... | collective-permute-start | bytes 368648 | tf_op jit(solution)/shard_map/ppermute | solution.py:344
  186.0 5.1 %collective-permute-start.21 = (bf16[8,24,640]{2,1,0:T(8,128)(2,1)S(1)}, bf16[8,24,640]{2,1,0:T(8,128)(2,1)S(1)}, u32[]{:S(2)}, u32[]{:S(2)}) collective-permute-start(bf16[8,24,640]{2,1,0:T(8,128)(2,1)S(1)} %pad_maximum_fusion.2), channel_id=1, source_target_pairs={{0,2},{1,5},{2,0},{3,7},{4,6},{5,1},{6,4},{7,3},{8,10},{9,13},{10,... | collective-permute-start | bytes 737288 | tf_op jit(solution)/shard_map/ppermute | solution.py:344
  191.1 5.5 %collective-permute-start.22 = (bf16[16,24,640]{2,1,0:T(8,128)(2,1)S(1)}, bf16[16,24,640]{2,1,0:T(8,128)(2,1)S(1)}, u32[]{:S(2)}, u32[]{:S(2)}) collective-permute-start(bf16[16,24,640]{2,1,0:T(8,128)(2,1)S(1)} %get-tuple-element.70), channel_id=1, source_target_pairs={{0,1},{1,0},{2,3},{3,2},{4,5},{5,4},{6,7},{7,6},{8,9},{9,8},{10,11... | collective-permute-start | bytes 1474568 | tf_op jit(solution)/shard_map/ppermute | solution.py:344
  (6 other events, 23.7 us)

commit v2 on v1

v2 whole, which is shorter than its diff:
```python
from functools import partial

import jax
import jax.numpy as jnp
from jax import lax
from jax.experimental import pallas as pl
from jax.experimental.pallas import tpu as pltpu
from jax.sharding import Mesh, PartitionSpec as P

F32 = jnp.float32
BF16 = jnp.bfloat16
EPSILON = 1e-05
HEADS = 12
HEAD_DIM = 64
D = 768
GROUPS = 4
GD = D // GROUPS
FF = 3072
GF = FF // GROUPS
TOK = 768
BLK = 256
EXT = 512
QCHUNK = (24, 640)
HALF = D // 2


def nn(a, b):
    return lax.dot_general(a, b, (((1,), (0,)), ((), ())), preferred_element_type=F32)


def nt(a, b):
    return lax.dot_general(a, b, (((1,), (1,)), ((), ())), preferred_element_type=F32)


def tn(a, b):
    return lax.dot_general(a, b, (((0,), (0,)), ((), ())), preferred_element_type=F32)


def gelu_parts(u):
    a = jnp.abs(u) * 0.7071067811865476
    t = 1.0 / (1.0 + 0.3275911 * a)
    e = jnp.exp(-0.5 * (u * u))
    poly = t * (
        0.254829592
        + t * (-0.284496736 + t * (1.421413741 + t * (-1.453152027 + t * 1.061405429)))
    )
    tail = 0.5 * poly * e
    phi = jnp.where(u < 0, tail, 1.0 - tail)
    return u * phi, phi + u * (e * 0.3989422804014327)


def pipelined(items, first, second, third, lag, last):
    n = len(items)
    for t in range(n + last):
        if t < n:
            first(items[t])
        if 0 <= t - lag < n:
            second(items[t - lag])
        if 0 <= t - last < n:
            third(items[t - last])


def project_kernel(
    seg_ref, x_ref, ids_ref, wqkv_ref,
    xt_ref, q_ref, k_ref, v_ref, bias_ref,
):
    two = seg_ref[BLK] == 1
    xt_ref[...] = x_ref[...].T
    for g in range(GROUPS):
        rows = slice(g * GD, (g + 1) * GD)
        xg = xt_ref[rows, :]
        q_ref[rows, :] = (tn(wqkv_ref[0, g], xg).astype(BF16).astype(F32) * 0.125).astype(BF16)
        k_ref[rows, :] = tn(wqkv_ref[1, g], xg).astype(BF16)
        v_ref[rows, :] = tn(wqkv_ref[2, g], xg).astype(BF16)
    row = ids_ref[...].reshape(1, TOK)

    def lanes(b):
        return jnp.broadcast_to(row[:, b * BLK : (b + 1) * BLK], (BLK, BLK))

    def same(kb, qb):
        return jnp.where(lanes(kb).T == lanes(qb), 0.0, -1e30).astype(BF16)

    bias_ref[0, :BLK] = same(1, 1)
    bias_ref[0, BLK:] = jnp.where(two, jnp.zeros((BLK, BLK), BF16), same(2, 1))
    bias_ref[1, :BLK] = same(2, 2)
    bias_ref[1, BLK:] = same(1, 2)


def pick(ref, far_ref, hr, b, two):
    if b == 0:
        other = far_ref[hr, :BLK]
    elif b == 1:
        other = jnp.where(two, far_ref[hr, BLK:], ref[hr, 2 * BLK :])
    else:
        other = ref[hr, BLK : 2 * BLK]
    return jnp.concatenate([ref[hr, b * BLK : (b + 1) * BLK], other], 1)


def attend_kernel(
    seg_ref, xp_ref, wqkv_ref, q_ref, k_ref, v_ref, bias_ref,
    kp_ref, vp_ref, ctx_ref, lse_ref,
):
    two = seg_ref[BLK] == 1
    xpt = xp_ref[:EXT, :].T
    for g in range(GROUPS):
        rows = slice(g * GD, (g + 1) * GD)
        kp_ref[rows, :] = tn(wqkv_ref[1, g], xpt[rows]).astype(BF16)
        vp_ref[rows, :] = tn(wqkv_ref[2, g], xpt[rows]).astype(BF16)

    def heads(i, carry):
        items = []
        for u in range(4):
            h = i * 4 + u
            hr = pl.ds(pl.multiple_of(h * HEAD_DIM, HEAD_DIM), HEAD_DIM)
            items += [{"h": h, "hr": hr, "b": b, "qc": slice(b * BLK, (b + 1) * BLK)} for b in range(3)]

        def scores(d):
            s = tn(pick(k_ref, kp_ref, d["hr"], d["b"], two), q_ref[d["hr"], d["qc"]])
            if d["b"]:
                s = s + bias_ref[d["b"] - 1].astype(F32)
            d["s"] = s

        def weights(d):
            s = d.pop("s")
            d["top"] = jnp.max(s, 0, keepdims=True)
            p = jnp.exp(s - d["top"])
            d["total"] = jnp.sum(p, 0, keepdims=True)
            d["p"] = p.astype(BF16)

        def mix(d):
            c = nn(pick(v_ref, vp_ref, d["hr"], d["b"], two), d.pop("p"))
            ctx_ref[d["hr"], d["qc"]] = (c * (1.0 / d["total"])).astype(BF16)
            lse_ref[d["h"], :, d["qc"]] = d["top"] + jnp.log(d["total"])

        pipelined(items, scores, weights, mix, 2, 3)
        return carry

    lax.fori_loop(0, HEADS // 4, heads, 0)


PARTS = [(g, slice(j * BLK, (j + 1) * BLK)) for g in range(GROUPS) for j in range(GF // BLK)]


def columns(ref):
    wide = jnp.broadcast_to(ref[...].reshape(1, D), (128, D)).T
    return jnp.concatenate([wide, wide], 1)


def halves(x):
    return x[:, :128] + x[:, 128:]


def scatter(part, jj, g, keep_ref, send_ref, at, low, far):
    for r in range(4):
        for lh in range(2):
            piece = part[48 * r : 48 * (r + 1), 384 * lh : 384 * (lh + 1)].astype(BF16)
            pos = ((g & 1) * 8 + r * 2 + lh) ^ (low if jj < 2 else far)
            ref = keep_ref if jj < 2 else send_ref
            ref[pos, at : at + 48] = piece


def forward_kernel(
    code_ref, xt_ref, ctx_ref, wo_ref, w1_ref, w2t_ref, cot_ref, ag_ref, as_ref, fg_ref, fs_ref,
    out_ref, hid_ref, n1_ref, inv1_ref, gpr_ref, gsec_ref, gfeed_ref, keep_ref, send_ref, gvec_ref,
    wot, w1t, act, nb, gacc,
):
    core, low, far = code_ref[0], code_ref[1], code_ref[2]
    for j, ref in enumerate((ag_ref, as_ref, fg_ref, fs_ref)):
        nb[j] = columns(ref)
    wot[...] = wo_ref[...].T
    for g in range(GROUPS):
        w1t[g] = w1_ref[g].T
    gacc[...] = jnp.zeros_like(gacc)

    def tile(t, carry):
        tc = pl.ds(pl.multiple_of(t * BLK, BLK), BLK)
        r = xt_ref[:, tc].astype(F32) + nn(wot[...], ctx_ref[:, tc])
        centre = r - jnp.mean(r, 0, keepdims=True)
        inv1 = lax.rsqrt(jnp.mean(centre * centre, 0, keepdims=True) + EPSILON)
        n1 = centre * inv1
        n1_ref[:, tc] = n1
        inv1_ref[:, tc] = inv1
        hidden = n1 * nb[0] + nb[1]
        hid_ref[:, tc] = hidden.astype(BF16)
        up, feeds = {}, []

        def rise(p):
            g, fr = p
            up[g, fr.start] = nn(w1t[g, fr], hid_ref[g * GD : (g + 1) * GD, tc])

        def bend(p):
            g, fr = p
            a, d = gelu_parts(up.pop((g, fr.start)))
            act[g, fr, tc] = a.astype(BF16)
            gpr_ref[g, fr, tc] = d.astype(BF16)

        def fall(p):
            if p[1].stop == GF:
                feeds.append(nn(w2t_ref[p[0]], act[p[0], :, tc]))

        pipelined(PARTS, rise, bend, fall, 2, 3)
        r2 = hidden + jnp.concatenate(feeds, 0)
        centre2 = r2 - jnp.mean(r2, 0, keepdims=True)
        inv2 = lax.rsqrt(jnp.mean(centre2 * centre2, 0, keepdims=True) + EPSILON)
        n2 = centre2 * inv2
        out_ref[tc, :] = (n2 * nb[2] + nb[3]).astype(BF16).T
        c = cot_ref[tc, :].T.astype(F32)
        gacc[0] += halves(c * n2)
        gacc[1] += halves(c)
        cg = c * nb[2]
        gsec = inv2 * (
            cg - jnp.mean(cg, 0, keepdims=True) - n2 * jnp.mean(cg * n2, 0, keepdims=True)
        )
        gsec_ref[:, tc] = gsec
        gfeed_ref[:, tc] = gsec.astype(BF16)
        return carry

    lax.fori_loop(0, TOK // BLK, tile, 0)
    for j in range(2):
        gvec_ref[:, j : j + 1] = jnp.sum(gacc[j], 1, keepdims=True)
    for jj in (2, 3, 0, 1):
        g = jj ^ (2 * core)
        gr = pl.ds(pl.multiple_of(g * GD, GD), GD)
        scatter(nt(gfeed_ref[gr, :], act[g]), jj, g, keep_ref, send_ref, 0, low, far)


def backward_kernel(
    code_ref, ctx_ref, wo_ref, w1_ref, w2t_ref, hid_ref, n1_ref, inv1_ref, gpr_ref, gsec_ref, gfeed_ref, ag_ref,
    gctx_ref, gfirst_ref, keep_ref, send_ref, gvec_ref,
    w2, gup, gatt, nb, gacc,
):
    core, low, far = code_ref[0], code_ref[1], code_ref[2]
    nb[...] = columns(ag_ref)
    for g in range(GROUPS):
        w2[g] = w2t_ref[g].T
    gacc[...] = jnp.zeros_like(gacc)

    def tile(t, carry):
        tc = pl.ds(pl.multiple_of(t * BLK, BLK), BLK)
        back, gh = {}, []

        def lift(p):
            g, fr = p
            back[g, fr.start] = nn(w2[g, fr], gfeed_ref[g * GD : (g + 1) * GD, tc])

        def scale(p):
            g, fr = p
            gup[g, fr, tc] = (back.pop((g, fr.start)) * gpr_ref[g, fr, tc].astype(F32)).astype(BF16)

        def drop(p):
            if p[1].stop == GF:
                gh.append(nn(w1_ref[p[0]], gup[p[0], :, tc]))

        pipelined(PARTS, lift, scale, drop, 2, 3)
        ghid = gsec_ref[:, tc] + jnp.concatenate(gh, 0)
        n1 = n1_ref[:, tc]
        gacc[0] += halves(ghid * n1)
        gacc[1] += halves(ghid)
        sc = ghid * nb[...]
        gfirst = inv1_ref[:, tc] * (
            sc - jnp.mean(sc, 0, keepdims=True) - n1 * jnp.mean(sc * n1, 0, keepdims=True)
        )
        gfirst_ref[:, tc] = gfirst
        gatt[:, tc] = gfirst.astype(BF16)
        gctx_ref[:, tc] = nn(wo_ref[...], gatt[:, tc]).astype(BF16)
        return carry

    lax.fori_loop(0, TOK // BLK, tile, 0)
    for j in range(2):
        gvec_ref[:, j : j + 1] = jnp.sum(gacc[j], 1, keepdims=True)
    for jj in (2, 3, 0, 1):
        g = jj ^ (2 * core)
        gr = pl.ds(pl.multiple_of(g * GD, GD), GD)
        scatter(nt(hid_ref[gr, :], gup[g]), jj, g, keep_ref, send_ref, 0, low, far)
        scatter(nt(ctx_ref[gr, :], gatt[...]), jj, g, keep_ref, send_ref, 48, low, far)


def back_kernel(
    seg_ref, q_ref, k_ref, v_ref, kp_ref, vp_ref, gctx_ref, lse_ref, bias_ref,
    dq_ref, dk_ref, dv_ref, far_ref, dk, dv,
):
    two = seg_ref[BLK] == 1
    scale = jnp.where(two, 1.0, 0.0)
    dk[...] = jnp.zeros_like(dk)
    dv[...] = jnp.zeros_like(dv)

    items = []
    for h in range(3):
        hr = slice(h * HEAD_DIM, (h + 1) * HEAD_DIM)
        items += [{"h": h, "hr": hr, "b": b, "qc": slice(b * BLK, (b + 1) * BLK)} for b in range(3)]

    def scores(d):
        hr, qc, b = d["hr"], d["qc"], d["b"]
        s = tn(pick(k_ref, kp_ref, hr, b, two), q_ref[hr, qc])
        if b:
            s = s + bias_ref[b - 1].astype(F32)
        d["s"] = s
        d["dp"] = tn(pick(v_ref, vp_ref, hr, b, two), gctx_ref[hr, qc])

    def weights(d):
        p = jnp.exp(d.pop("s") - lse_ref[d["h"], :, d["qc"]])
        dp = d.pop("dp")
        dots = jnp.sum(p * dp, 0, keepdims=True)
        d["ds"] = (p * (dp - dots)).astype(BF16)
        d["p"] = p.astype(BF16)

    def mix(d):
        hr, qc, b = d["hr"], d["qc"], d["b"]
        ds = d.pop("ds")
        dq_ref[hr, qc] = (nn(pick(k_ref, kp_ref, hr, b, two), ds) * 0.125).astype(BF16)
        gk = nt(q_ref[hr, qc], ds)
        gv = nt(gctx_ref[hr, qc], d.pop("p"))
        for acc, grad, slot in ((dk, gk, 0), (dv, gv, 1)):
            acc[hr, qc] += grad[:, :BLK]
            other = grad[:, BLK:]
            if b == 0:
                far_ref[slot, hr, :BLK] = other.astype(BF16)
            elif b == 1:
                far_ref[slot, hr, BLK:] = (other * scale).astype(BF16)
                acc[hr, 2 * BLK :] += other * (1.0 - scale)
            else:
                acc[hr, BLK : 2 * BLK] += other

    pipelined(items, scores, weights, mix, 1, 2)
    dk_ref[...] = dk[...]
    dv_ref[...] = dv[...]


def through_kernel(
    code_ref, xt_ref, dqa_ref, dka_ref, dva_ref, ba_ref, dqb_ref, dkb_ref, dvb_ref, bb_ref, wqkv_ref,
    gfirst_ref, gvec1_ref, gvec2_ref, *refs, half,
):
    core = code_ref[0]
    order = jnp.where(core == half, code_ref[1], code_ref[2])
    if half:
        first_ref, _, gin_ref, keep_ref, send_ref, piece_ref = refs
    else:
        gin_ref, piece_ref = refs
    through = []
    groups = ((dqa_ref, dka_ref, dva_ref, ba_ref), (dqb_ref, dkb_ref, dvb_ref, bb_ref))
    for i, (dq_ref, dk_ref, dv_ref, b_ref) in enumerate(groups):
        rows = slice(i * GD, (i + 1) * GD)
        grads = [dq_ref[...]]
        for slot, ref in ((0, dk_ref), (1, dv_ref)):
            own = ref[...]
            own = jnp.concatenate([own[:, :EXT] + b_ref[slot].astype(F32), own[:, EXT:]], 1)
            grads.append(own.astype(BF16))
        through.append(sum(nn(wqkv_ref[t, i], grads[t]) for t in range(3)))
        row = jnp.concatenate(
            [nt(xt_ref[rows], grad) for grad in grads]
            + [gvec1_ref[rows], gvec2_ref[rows], jnp.zeros((GD, QCHUNK[1] - 3 * GD - 4), F32)],
            1,
        )
        for r in range(8):
            piece_ref[(i * 8 + r) ^ order] = row[24 * r : 24 * (r + 1)]
    if half:
        mine, other = piece_ref[...], first_ref[...]
        keep_ref[...] = jnp.where(core == 1, mine, other)
        send_ref[...] = jnp.where(core == 1, other, mine).astype(BF16)
    gin_ref[...] = (gfirst_ref[...] + jnp.concatenate(through, 0)).astype(BF16).T


def finish_kernel(code_ref, m_ref, *outs):
    core, low, far = code_ref[0], code_ref[1], code_ref[2]
    for half in range(2):
        for a in range(16):
            part = m_ref[half * 16 + (a ^ (far if half else low))].astype(F32)
            g = (half ^ core) * 2 + a // 8
            rows = slice(48 * (a % 8 // 2), 48 * (a % 8 // 2 + 1))
            lanes = slice(384 * (a % 2), 384 * (a % 2 + 1))
            for i, ref in enumerate(outs):
                ref[g, rows, lanes] = part[48 * i : 48 * (i + 1)]


def finish_qkv_kernel(code_ref, m_ref, gq_ref, ag_ref, as_ref, fg_ref, fs_ref, vec):
    core, low, far = code_ref[0], code_ref[1], code_ref[2]
    for half in range(2):
        for a in range(16):
            part = m_ref[half * 16 + (a ^ (far if half else low))].astype(F32)
            g = (half ^ core) * 2 + a // 8
            rows = slice(24 * (a % 8), 24 * (a % 8 + 1))
            for t in range(3):
                gq_ref[t, g, rows] = part[:, t * GD : (t + 1) * GD]
            vec[g, rows] = part[:, 512:640]
    turned = vec[...].reshape(D, 128).T
    for i, ref in enumerate((ag_ref, as_ref, fg_ref, fs_ref)):
        ref[...] = turned[64 + i : 65 + i].reshape(D)


SMEM = pl.BlockSpec(memory_space=pltpu.SMEM)
VMEM = pl.BlockSpec(memory_space=pltpu.VMEM)
ANY = pl.BlockSpec(memory_space=pl.ANY)


def call(kernel, name, ins, outs, scratch, limit, work, grid=(), aliases=None):
    return pl.pallas_call(
        kernel,
        grid=grid,
        out_shape=[jax.ShapeDtypeStruct(s, d) for s, d, _ in outs],
        in_specs=[spec for _, spec in ins],
        out_specs=[spec for _, _, spec in outs],
        scratch_shapes=scratch,
        compiler_params=pltpu.CompilerParams(vmem_limit_bytes=limit << 20),
        cost_estimate=pl.CostEstimate(flops=work[0], bytes_accessed=work[1], transcendentals=0),
        input_output_aliases=aliases or {},
        name=name,
    )(*[array for array, _ in ins])


def block(shape, *at):
    return pl.BlockSpec(shape, lambda _: at)


class Links:
    def __init__(self, n_seq):
        bits = max(n_seq.bit_length() - 1, 0)
        self.n = n_seq * 2
        orders = [list(range(bits)), [1, 0] + list(range(2, bits))] if bits > 1 else [list(range(bits))] * 2
        self.orders = orders
        self.halving = min(4, bits)
        self.bits = bits

    def pairs(self, step):
        if step < 0:
            return [(i, i ^ 1) for i in range(self.n)]
        return [(i, i ^ (2 << self.orders[i & 1][step])) for i in range(self.n)]

    def code(self, seq, core):
        def of(order):
            value = 0
            for step in range(4):
                value = value * 2 + (((seq >> order[step]) & 1) if step < self.halving else 0)
            return value

        return jnp.where(core == 0, of(self.orders[0]), of(self.orders[1]))


def swap(x, links, step):
    return lax.ppermute(x, "dev", links.pairs(step))


def all_sum(keep, came, links):
    total = keep.astype(F32) + came.astype(F32)
    for step in range(links.halving):
        half = total.shape[0] // 2
        total = total[:half] + swap(total[half:].astype(BF16), links, step).astype(F32)
    piece = total.astype(BF16)
    for step in range(links.halving, links.bits):
        piece = (piece.astype(F32) + swap(piece, links, step).astype(F32)).astype(BF16)
    for step in reversed(range(-1, links.halving)):
        piece = jnp.concatenate([piece, swap(piece, links, step)], 0)
    return piece


def per_device(
    links, inputs, segment_ids, qkv_weight, out_weight, ffn_in_weight, ffn_out_weight,
    attn_gain, attn_shift, ffn_gain, ffn_shift, out_cotangent,
):
    me = lax.axis_index("dev")
    seq, core = me >> 1, me & 1
    code = jnp.stack([core, links.code(seq, core), links.code(seq, 1 - core)]).astype(jnp.int32)
    partner = swap(inputs, links, -1)
    square = (D, TOK)
    large = (GROUPS, GF, TOK)
    xt, q, k, v, bias = call(
        project_kernel,
        "project",
        [(segment_ids, SMEM), (inputs, VMEM), (segment_ids, VMEM), (qkv_weight, VMEM)],
        [(square, BF16, VMEM)] * 4 + [((2, 2 * BLK, BLK), BF16, VMEM)],
        [],
        12,
        (2_000_000_000, 7_000_000),
    )
    kp, vp, ctx, lse = call(
        attend_kernel,
        "attend",
        [(segment_ids, SMEM), (partner, VMEM), (qkv_weight, VMEM), (q, VMEM), (k, VMEM), (v, VMEM), (bias, VMEM)],
        [((D, EXT), BF16, VMEM), ((D, EXT), BF16, VMEM), (square, BF16, VMEM), ((HEADS, 1, TOK), F32, VMEM)],
        [],
        12,
        (8_000_000_000, 9_000_000),
    )
    weight2t = jnp.swapaxes(ffn_out_weight, 1, 2)
    output, hid, n1, inv1, gpr, gsec, gfeed, keep, send, gvec2 = call(
        forward_kernel,
        "forward",
        [(code, SMEM), (xt, VMEM), (ctx, VMEM), (out_weight, VMEM), (ffn_in_weight, VMEM), (weight2t, VMEM)]
        + [(out_cotangent, VMEM), (attn_gain, VMEM), (attn_shift, VMEM), (ffn_gain, VMEM), (ffn_shift, VMEM)],
        [((TOK, D), BF16, VMEM), (square, BF16, VMEM), (square, F32, VMEM), ((1, TOK), F32, VMEM), (large, BF16, VMEM)]
        + [(square, F32, VMEM), (square, BF16, VMEM), ((16, 48, 384), BF16, VMEM), ((16, 48, 384), BF16, VMEM)]
        + [((D, 2), F32, VMEM)],
        [
            pltpu.VMEM((D, D), BF16), pltpu.VMEM((GROUPS, GF, GD), BF16), pltpu.VMEM(large, BF16),
            pltpu.VMEM((4, D, BLK), F32), pltpu.VMEM((2, D, 128), F32),
        ],
        20,
        (10_000_000_000, 20_000_000),
    )
    came = swap(send, links, -1)
    gctx, gfirst, keep1, send1, gvec1 = call(
        backward_kernel,
        "backward",
        [(code, SMEM), (ctx, VMEM), (out_weight, VMEM), (ffn_in_weight, VMEM), (weight2t, VMEM), (hid, VMEM)]
        + [(n1, VMEM), (inv1, VMEM), (gpr, VMEM), (gsec, VMEM), (gfeed, VMEM), (attn_gain, VMEM)],
        [(square, BF16, VMEM), (square, F32, VMEM), ((16, 96, 384), BF16, VMEM), ((16, 96, 384), BF16, VMEM)]
        + [((D, 2), F32, VMEM)],
        [
            pltpu.VMEM((GROUPS, GF, GD), BF16), pltpu.VMEM(large, BF16), pltpu.VMEM(square, BF16),
            pltpu.VMEM((D, BLK), F32), pltpu.VMEM((2, D, 128), F32),
        ],
        18,
        (10_000_000_000, 20_000_000),
    )
    came1 = swap(send1, links, -1)

    def attention_back(g):
        rows = partial(lambda width: block((GD, width), g, 0))
        return call(
            back_kernel,
            "attention_back",
            [(segment_ids, SMEM), (q, rows(TOK)), (k, rows(TOK)), (v, rows(TOK)), (kp, rows(EXT)), (vp, rows(EXT))]
            + [(gctx, rows(TOK)), (lse, block((3, 1, TOK), g, 0, 0)), (bias, VMEM)],
            [((GD, TOK), BF16, VMEM), ((GD, TOK), F32, VMEM), ((GD, TOK), F32, VMEM), ((2, GD, EXT), BF16, VMEM)],
            [pltpu.VMEM((GD, TOK), F32), pltpu.VMEM((GD, TOK), F32)],
            10,
            (4_000_000_000, 4_000_000),
            (1,),
        )

    def through(half, parts, first):
        ins = [(code, SMEM), (xt, block((HALF, TOK), half, 0))]
        for dq, dk, dv, far in parts:
            ins += [(dq, VMEM), (dk, VMEM), (dv, VMEM), (swap(far, links, -1), VMEM)]
        ins += [(qkv_weight, block((3, 2, GD, GD), 0, half, 0, 0))]
        ins += [(gfirst, block((HALF, TOK), half, 0)), (gvec1, block((HALF, 2), half, 0))]
        ins += [(gvec2, block((HALF, 2), half, 0))]
        shape = (16,) + QCHUNK
        outs = [((TOK, D), BF16, block((TOK, HALF), 0, half))]
        if half:
            ins += [(first[1], VMEM), (first[0], ANY)]
            outs += [(shape, F32, VMEM), (shape, BF16, VMEM)]
        else:
            outs += [(shape, F32, VMEM)]
        return call(
            partial(through_kernel, half=half),
            "through_qkv",
            ins,
            outs,
            [pltpu.VMEM(shape, F32)] if half else [],
            10,
            (2_000_000_000, 6_000_000),
            (1,),
            {len(ins) - 1: 0} if half else None,
        )

    parts = [attention_back(g) for g in range(GROUPS)]
    first = through(0, parts[:2], None)
    grad_input, keep_q, send_q = through(1, parts[2:], first)
    m2 = all_sum(keep, came, links)
    m1 = all_sum(keep1, came1, links)
    mq = all_sum(keep_q, swap(send_q, links, -1), links)
    rows = (GROUPS, GD, D)
    (g2,) = call(finish_kernel, "finish", [(code, SMEM), (m2, VMEM)], [(rows, F32, VMEM)], [], 10, (0, 4_000_000))
    g1, go = call(
        finish_kernel, "finish", [(code, SMEM), (m1, VMEM)], [(rows, F32, VMEM)] * 2, [], 16, (0, 8_000_000)
    )
    gq, *vectors = call(
        finish_qkv_kernel,
        "finish_qkv",
        [(code, SMEM), (mq, VMEM)],
        [((3, GROUPS, GD, GD), F32, VMEM)] + [((D,), F32, VMEM)] * 4,
        [pltpu.VMEM((GROUPS, GD, 128), F32)],
        8,
        (0, 4_000_000),
    )
    return (output, grad_input, gq, go.reshape(D, D), g1, jnp.swapaxes(g2, 1, 2)) + tuple(vectors)


def solution(mesh):
    flat = Mesh(mesh.devices.reshape(-1), ("dev",))
    links = Links(mesh.shape["seq"])
    split, copied = P("dev"), P()
    return jax.shard_map(
        partial(per_device, links),
        mesh=flat,
        in_specs=(split, split) + (copied,) * 8 + (split,),
        out_specs=(split, split) + (copied,) * 8,
        check_vma=False,
    )
```

time: 208 us -> 159 us (0.76)
  Pallas kernels: 97.7 us -> 67.8 us
  waiting for transfers between devices: 60.5 us -> 40.8 us
  starting transfers between devices: 24.5 us -> 42.7 us
  local copies, waits for them, and re-layouts: 17.1 us -> 4.64 us
  other arithmetic: 6.18 us -> 1.37 us
    pallas_call x4 -> x13, Pallas kernels: 97.7 us -> 67.8 us  [call(): pl.pallas_call(kernel, grid=grid, out_shape=[jax.ShapeDtypeStruct(s, d) f...]
    ppermute x23 -> x35, waiting for transfers between devices: 60.5 us -> 40.8 us  [swap(): return lax.ppermute(x, 'dev', links.pairs(step))]
    ppermute x23 -> x35, starting transfers between devices: 24.5 us -> 42.7 us  [swap(): return lax.ppermute(x, 'dev', links.pairs(step))]
    slice x4 -> x0, local copies, waits for them, and re-layouts: 6.41 us -> none  [the longest x1 2.91 us: per_device(): gv[:, 3]]
    add x2 -> x3, other arithmetic: 3.58 us -> 0.55 us  [all_sum(): total = keep.astype(F32) + came.astype(F32)]
    broadcast_in_dim x2 -> x0, local copies, waits for them, and re-layouts: 2.86 us -> none  [the longest x1 1.59 us: per_device(): segc = segment_ids[:, None]]
  transfers between devices with their start and end apart: 23 -> 35, of which waited for: 14 -> 14; matrix products, arithmetic and copies ran while one was open for 7% -> 2% of each run, Pallas kernels for 18% -> 12%
where the time goes in v2:
time: 159 us; the launch traced here: 158 us
  Pallas kernels  67.8 us (43%)
  starting transfers between devices  42.7 us (27%)
  waiting for transfers between devices  40.8 us (26%)
  local copies, waits for them, and re-layouts  4.64 us (3%)
    pallas_call x13, Pallas kernels, call(): pl.pallas_call(kernel, grid=grid, out_shape=[jax.ShapeDtypeStruct(s, d) f...  67.8 us
    ppermute x35, starting transfers between devices, swap(): return lax.ppermute(x, 'dev', links.pairs(step))  42.7 us
    ppermute x35, waiting for transfers between devices, swap(): return lax.ppermute(x, 'dev', links.pairs(step))  40.8 us
    unnamed x38, local copies, waits for them, and re-layouts  3.62 us
  transfers between devices with their start and end apart: 35, of which 14 were waited for; matrix products, arithmetic and copies ran while one was open for 2% of the time, Pallas kernels for 12%

profile of v2, /device:TPU:1, one launch (start us, length us, event | category | flops | bytes accessed | tf_op | source)
XLA Modules:
  0.0 158.3 jit_solution(16927653798630838539)
XLA Ops:
  6.0 8.2 %attend.1 = (bf16[768,512]{1,0:T(8,128)(2,1)S(1)}, bf16[768,512]{1,0:T(8,128)(2,1)S(1)}, bf16[768,768]{1,0:T(8,128)(2,1)S(1)}, f32[12,1,768]{2,1,0:T(1,128)S(1)}) custom-call(s32[768]{0:T(1024)S(1)} %copy-done.11, bf16[768,768]{1,0:T(8,128)(2,1)S(1)} %collective-permute-done.xp_ref, bf16[3,4,192,192]{3,2,1,0:T(8,128)(2,1)S(1)} %copy-done.1, ...), custom_call_target="tpu_custom_call" | custom-call | flops 8000000000 | bytes 9000000 | tf_op jit(solution)/shard_map/attend/pallas_call | solution.py:396
  14.3 19.7 %forward.1 = (bf16[768,768]{1,0:T(8,128)(2,1)}, bf16[768,768]{1,0:T(8,128)(2,1)S(1)}, f32[768,768]{1,0:T(8,128)S(1)}, f32[1,768]{1,0:T(1,128)S(1)}, bf16[4,768,7...) custom-call(s32[3]{0:T(128)S(1)} %pad_add_fusion.code_ref, ...), custom_call_target="tpu_custom_call" | custom-call | flops 10000000000 | bytes 20000000 | tf_op jit(solution)/shard_map/forward/pallas_call | solution.py:396
  34.0 9.8 %backward.1 = (bf16[768,768]{1,0:T(8,128)(2,1)S(1)}, f32[768,768]{1,0:T(8,128)S(1)}, bf16[16,96,384]{2,1,0:T(8,128)(2,1)S(1)}, bf16[16,96,384]{2,1,0:T(8,128)(2,1)S(1)}, f32[768,2]{1,0:T(8,128)S(1)}) custom-call(s32[3]{0:T(128)S(1)} %pad_add_fusion.code_ref, bf16[768,768]{1,0:T(8,128)(2,1)S(1)} %get-tuple-element.67.ctx_ref, bf16[768,768]{1,0:T(8,128)(2,1)S(1)} %copy-done.4, ...), custom_call_target="tpu_custom_call" | custom-call | flops 10000000000 | bytes 20000000 | tf_op jit(solution)/shard_map/backward/pallas_call | solution.py:396
  43.9 3.8 %attention_back.6 = (bf16[192,768]{1,0:T(8,128)(2,1)S(1)}, f32[192,768]{1,0:T(8,128)S(1)}, f32[192,768]{1,0:T(8,128)S(1)}, bf16[2,192,512]{2,1,0:T(8,128)(2,1)S(1)}) custom-call(s32[768]{0:T(1024)S(1)} %copy-done.12, bf16[768,768]{1,0:T(8,128)(2,1)S(1)} %get-tuple-element.63.q_ref, bf16[768,768]{1,0:T(8,128)(2,1)S(1)} %get-tuple-element.64.k_ref, ...), custom_call_target="tpu_custom_call" | custom-call | flops 4000000000 | bytes 4000000 | tf_op jit(solution)/shard_map/attention_back/pallas_call | solution.py:396
  47.6 3.8 %attention_back.7 = (bf16[192,768]{1,0:T(8,128)(2,1)S(1)}, f32[192,768]{1,0:T(8,128)S(1)}, f32[192,768]{1,0:T(8,128)S(1)}, bf16[2,192,512]{2,1,0:T(8,128)(2,1)S(1)}) custom-call(s32[768]{0:T(1024)S(1)} %copy-done.12, bf16[768,768]{1,0:T(8,128)(2,1)S(1)} %get-tuple-element.63.q_ref, bf16[768,768]{1,0:T(8,128)(2,1)S(1)} %get-tuple-element.64.k_ref, ...), custom_call_target="tpu_custom_call" | custom-call | flops 4000000000 | bytes 4000000 | tf_op jit(solution)/shard_map/attention_back/pallas_call | solution.py:396
  52.4 3.8 %attention_back.4 = (bf16[192,768]{1,0:T(8,128)(2,1)S(1)}, f32[192,768]{1,0:T(8,128)S(1)}, f32[192,768]{1,0:T(8,128)S(1)}, bf16[2,192,512]{2,1,0:T(8,128)(2,1)S(1)}) custom-call(s32[768]{0:T(1024)S(1)} %copy-done.12, bf16[768,768]{1,0:T(8,128)(2,1)S(1)} %get-tuple-element.63.q_ref, bf16[768,768]{1,0:T(8,128)(2,1)S(1)} %get-tuple-element.64.k_ref, ...), custom_call_target="tpu_custom_call" | custom-call | flops 4000000000 | bytes 4000000 | tf_op jit(solution)/shard_map/attention_back/pallas_call | solution.py:396
  56.2 4.0 %attention_back.5 = (bf16[192,768]{1,0:T(8,128)(2,1)S(1)}, f32[192,768]{1,0:T(8,128)S(1)}, f32[192,768]{1,0:T(8,128)S(1)}, bf16[2,192,512]{2,1,0:T(8,128)(2,1)S(1)}) custom-call(s32[768]{0:T(1024)S(1)} %copy-done.12, bf16[768,768]{1,0:T(8,128)(2,1)S(1)} %get-tuple-element.63.q_ref, bf16[768,768]{1,0:T(8,128)(2,1)S(1)} %get-tuple-element.64.k_ref, ...), custom_call_target="tpu_custom_call" | custom-call | flops 4000000000 | bytes 4000000 | tf_op jit(solution)/shard_map/attention_back/pallas_call | solution.py:396
  61.0 2.7 %collective-permute-start.26 = (bf16[8,48,384]{2,1,0:T(8,128)(2,1)S(1)}, bf16[8,48,384]{2,1,0:T(8,128)(2,1)S(1)}, u32[]{:S(2)}, u32[]{:S(2)}) collective-permute-start(bf16[8,48,384]{2,1,0:T(8,128)(2,1)S(1)} %slice.163), channel_id=1, source_target_pairs={{0,2},{1,5},{2,0},{3,7},{4,6},{5,1},{6,4},{7,3},{8,10},{9,13},{10,... | collective-permute-start | bytes 884744 | tf_op jit(solution)/shard_map/ppermute | solution.py:439
  63.8 2.6 %through_qkv.2 = (bf16[768,768]{1,0:T(8,128)(2,1)}, f32[16,24,640]{2,1,0:T(8,128)S(1)}) custom-call(s32[3]{0:T(128)S(1)} %pad_add_fusion.code_ref, bf16[768,768]{1,0:T(8,128)(2,1)S(1)} %get-tuple-element.62.xt_ref, bf16[192,768]{1,0:T(8,128)(2,1)S(1)} %get-tuple-element.90.dqa_ref, f32[192,768]{1,0:T(8,128)S(1)} %get-tuple-element.91.dka_ref, ...), custom_call_target="tpu_custom_call" | custom-call | flops 2000000000 | bytes 6000000 | tf_op jit(solution)/shard_map/through_qkv/pallas_call | solution.py:396
  66.4 2.9 %through_qkv.3 = (bf16[768,768]{1,0:T(8,128)(2,1)}, f32[16,24,640]{2,1,0:T(8,128)S(1)}, bf16[16,24,640]{2,1,0:T(8,128)(2,1)S(1)}) custom-call(s32[3]{0:T(128)S(1)} %pad_add_fusion.code_ref, bf16[768,768]{1,0:T(8,128)(2,1)S(1)} %get-tuple-element.62.xt_ref, bf16[192,768]{1,0:T(8,128)(2,1)S(1)} %get-tuple-element.79.dqa_ref, ...), custom_call_target="tpu_custom_call", output_to_operand_aliasing={{0}: (15, {})} | custom-call | flops 2000000000 | bytes 6000000 | tf_op jit(solution)/shard_map/through_qkv/pallas_call | solution.py:396
  70.7 3.4 %collective-permute-done.27 = bf16[4,48,384]{2,1,0:T(8,128)(2,1)S(1)} collective-permute-done((bf16[4,48,384]{2,1,0:T(8,128)(2,1)S(1)}, bf16[4,48,384]{2,1,0:T(8,128)(2,1)S(1)}, u32[]{:S(2)}, u32[]{:S(2)}) %collective-permute-start.27) | collective-permute-done | bytes 147488 | tf_op jit(solution)/shard_map/ppermute | solution.py:439
  77.5 2.4 %collective-permute-start.29 = (bf16[1,48,384]{2,1,0:T(8,128)(2,1)S(1)}, bf16[1,48,384]{2,1,0:T(8,128)(2,1)S(1)}, u32[]{:S(2)}, u32[]{:S(2)}) collective-permute-start(bf16[1,48,384]{2,1,0:T(8,128)(2,1)S(1)} %slice.172), channel_id=1, source_target_pairs={{0,16},{1,17},{2,18},{3,19},{4,20},{5,21},{6,22},{7,23},{8,24},{9,... | collective-permute-start | bytes 110600 | tf_op jit(solution)/shard_map/ppermute | solution.py:439
  82.1 2.4 %collective-permute-start.30 = (bf16[1,48,384]{2,1,0:T(8,128)(2,1)S(1)}, bf16[1,48,384]{2,1,0:T(8,128)(2,1)S(1)}, u32[]{:S(2)}, u32[]{:S(2)}) collective-permute-start(bf16[1,48,384]{2,1,0:T(8,128)(2,1)S(1)} %get-tuple-element.115), channel_id=1, source_target_pairs={{0,16},{1,17},{2,18},{3,19},{4,20},{5,21},{6,22},{7,23},{8,24},{9,... | collective-permute-start | bytes 110600 | tf_op jit(solution)/shard_map/ppermute | solution.py:439
  87.1 3.5 %collective-permute-done.16 = bf16[8,96,384]{2,1,0:T(8,128)(2,1)S(1)} collective-permute-done((bf16[8,96,384]{2,1,0:T(8,128)(2,1)S(1)}, bf16[8,96,384]{2,1,0:T(8,128)(2,1)S(1)}, u32[]{:S(2)}, u32[]{:S(2)}) %collective-permute-start.16) | collective-permute-done | bytes 589856 | tf_op jit(solution)/shard_map/ppermute | solution.py:439
  92.5 4.3 %collective-permute-done.17 = bf16[4,96,384]{2,1,0:T(8,128)(2,1)S(1)} collective-permute-done((bf16[4,96,384]{2,1,0:T(8,128)(2,1)S(1)}, bf16[4,96,384]{2,1,0:T(8,128)(2,1)S(1)}, u32[]{:S(2)}, u32[]{:S(2)}) %collective-permute-start.17) | collective-permute-done | bytes 294944 | tf_op jit(solution)/shard_map/ppermute | solution.py:439
  98.5 2.4 %collective-permute-done.18 = bf16[2,96,384]{2,1,0:T(8,128)(2,1)S(1)} collective-permute-done((bf16[2,96,384]{2,1,0:T(8,128)(2,1)S(1)}, bf16[2,96,384]{2,1,0:T(8,128)(2,1)S(1)}, u32[]{:S(2)}, u32[]{:S(2)}) %collective-permute-start.18) | collective-permute-done | bytes 147488 | tf_op jit(solution)/shard_map/ppermute | solution.py:439
  107.7 2.5 %collective-permute-done.20 = bf16[1,96,384]{2,1,0:T(8,128)(2,1)S(1)} collective-permute-done((bf16[1,96,384]{2,1,0:T(8,128)(2,1)S(1)}, bf16[1,96,384]{2,1,0:T(8,128)(2,1)S(1)}, u32[]{:S(2)}, u32[]{:S(2)}) %collective-permute-start.20) | collective-permute-done | bytes 73760 | tf_op jit(solution)/shard_map/ppermute | solution.py:439
  110.3 2.3 %collective-permute-start.21 = (bf16[2,96,384]{2,1,0:T(8,128)(2,1)S(1)}, bf16[2,96,384]{2,1,0:T(8,128)(2,1)S(1)}, u32[]{:S(2)}, u32[]{:S(2)}) collective-permute-start(bf16[2,96,384]{2,1,0:T(8,128)(2,1)S(1)} %pad_maximum_fusion.4), channel_id=1, source_target_pairs={{0,8},{1,9},{2,10},{3,11},{4,12},{5,13},{6,14},{7,15},{8,0},{9,1},... | collective-permute-start | bytes 442376 | tf_op jit(solution)/shard_map/ppermute | solution.py:439
  113.2 2.8 %collective-permute-done.21 = bf16[2,96,384]{2,1,0:T(8,128)(2,1)S(1)} collective-permute-done((bf16[2,96,384]{2,1,0:T(8,128)(2,1)S(1)}, bf16[2,96,384]{2,1,0:T(8,128)(2,1)S(1)}, u32[]{:S(2)}, u32[]{:S(2)}) %collective-permute-start.21) | collective-permute-done | bytes 147488 | tf_op jit(solution)/shard_map/ppermute | solution.py:439
  118.4 3.6 %collective-permute-done.22 = bf16[4,96,384]{2,1,0:T(8,128)(2,1)S(1)} collective-permute-done((bf16[4,96,384]{2,1,0:T(8,128)(2,1)S(1)}, bf16[4,96,384]{2,1,0:T(8,128)(2,1)S(1)}, u32[]{:S(2)}, u32[]{:S(2)}) %collective-permute-start.22) | collective-permute-done | bytes 294944 | tf_op jit(solution)/shard_map/ppermute | solution.py:439
  124.5 10.1 %collective-permute-done.23 = bf16[8,96,384]{2,1,0:T(8,128)(2,1)S(1)} collective-permute-done((bf16[8,96,384]{2,1,0:T(8,128)(2,1)S(1)}, bf16[8,96,384]{2,1,0:T(8,128)(2,1)S(1)}, u32[]{:S(2)}, u32[]{:S(2)}) %collective-permute-start.23) | collective-permute-done | bytes 589856 | tf_op jit(solution)/shard_map/ppermute | solution.py:439
  134.8 9.3 %collective-permute-start.24 = (bf16[16,96,384]{2,1,0:T(8,128)(2,1)S(1)}, bf16[16,96,384]{2,1,0:T(8,128)(2,1)S(1)}, u32[]{:S(2)}, u32[]{:S(2)}) collective-permute-start(bf16[16,96,384]{2,1,0:T(8,128)(2,1)S(1)} %get-tuple-element.120), channel_id=1, source_target_pairs={{0,1},{1,0},{2,3},{3,2},{4,5},{5,4},{6,7},{7,6},{8,9},{9,8},{10,11... | collective-permute-start | bytes 3538952 | tf_op jit(solution)/shard_map/ppermute | solution.py:439
  146.2 3.6 %collective-permute-done.13 = bf16[8,24,640]{2,1,0:T(8,128)(2,1)S(1)} collective-permute-done((bf16[8,24,640]{2,1,0:T(8,128)(2,1)S(1)}, bf16[8,24,640]{2,1,0:T(8,128)(2,1)S(1)}, u32[]{:S(2)}, u32[]{:S(2)}) %collective-permute-start.13) | collective-permute-done | bytes 245792 | tf_op jit(solution)/shard_map/ppermute | solution.py:439
  155.3 3.0 %finish.2 = (f32[4,192,768]{2,1,0:T(8,128)}, f32[4,192,768]{2,1,0:T(8,128)}) custom-call(s32[3]{0:T(128)S(1)} %pad_add_fusion.code_ref, bf16[32,96,384]{2,1,0:T(8,128)(2,1)S(1)} %constant_dynamic-update-slice_fusion.16.m_ref), custom_call_target="tpu_custom_call" | custom-call | bytes 8000000 | tf_op jit(solution)/shard_map/finish/pallas_call | solution.py:396
  (140 shorter events, 40.1 us)
Async XLA Ops:
  0.6 5.3 %collective-permute-start = (bf16[768,768]{1,0:T(8,128)(2,1)}, bf16[768,768]{1,0:T(8,128)(2,1)S(1)}, u32[]{:S(2)}, u32[]{:S(2)}) collective-permute-start(bf16[768,768]{1,0:T(8,128)(2,1)} %x_ref.1), channel_id=1, source_target_pairs={{0,1},{1,0},{2,3},{3,2},{4,5},{5,4},{6,7},{7,6},{8,9},{9,8},{10,11... | collective-permute-start | bytes 3538952 | tf_op jit(solution)/shard_map/ppermute | solution.py:439
  51.4 9.6 %collective-permute-start.3 = (bf16[2,192,512]{2,1,0:T(8,128)(2,1)S(1)}, bf16[2,192,512]{2,1,0:T(8,128)(2,1)S(1)}, u32[]{:S(2)}, u32[]{:S(2)}) collective-permute-start(bf16[2,192,512]{2,1,0:T(8,128)(2,1)S(1)} %get-tuple-element.93), channel_id=1, source_target_pairs={{0,1},{1,0},{2,3},{3,2},{4,5},{5,4},{6,7},{7,6},{8,9},{9,8},{10,11... | collective-permute-start | bytes 1179656 | tf_op jit(solution)/shard_map/ppermute | solution.py:439
  51.9 11.8 %collective-permute-start.4 = (bf16[2,192,512]{2,1,0:T(8,128)(2,1)S(1)}, bf16[2,192,512]{2,1,0:T(8,128)(2,1)S(1)}, u32[]{:S(2)}, u32[]{:S(2)}) collective-permute-start(bf16[2,192,512]{2,1,0:T(8,128)(2,1)S(1)} %get-tuple-element.97), channel_id=1, source_target_pairs={{0,1},{1,0},{2,3},{3,2},{4,5},{5,4},{6,7},{7,6},{8,9},{9,8},{10,11... | collective-permute-start | bytes 1179656 | tf_op jit(solution)/shard_map/ppermute | solution.py:439
  52.0 8.8 %collective-permute-start.25 = (bf16[16,48,384]{2,1,0:T(8,128)(2,1)S(1)}, bf16[16,48,384]{2,1,0:T(8,128)(2,1)S(1)}, u32[]{:S(2)}, u32[]{:S(2)}) collective-permute-start(bf16[16,48,384]{2,1,0:T(8,128)(2,1)S(1)} %get-tuple-element.109), channel_id=1, source_target_pairs={{0,1},{1,0},{2,3},{3,2},{4,5},{5,4},{6,7},{7,6},{8,9},{9,8},{10,11... | collective-permute-start | bytes 1769480 | tf_op jit(solution)/shard_map/ppermute | solution.py:439
  60.2 6.2 %collective-permute-start.1 = (bf16[2,192,512]{2,1,0:T(8,128)(2,1)S(1)}, bf16[2,192,512]{2,1,0:T(8,128)(2,1)S(1)}, u32[]{:S(2)}, u32[]{:S(2)}) collective-permute-start(bf16[2,192,512]{2,1,0:T(8,128)(2,1)S(1)} %get-tuple-element.82), channel_id=1, source_target_pairs={{0,1},{1,0},{2,3},{3,2},{4,5},{5,4},{6,7},{7,6},{8,9},{9,8},{10,11... | collective-permute-start | bytes 1179656 | tf_op jit(solution)/shard_map/ppermute | solution.py:439
  60.3 6.1 %collective-permute-start.2 = (bf16[2,192,512]{2,1,0:T(8,128)(2,1)S(1)}, bf16[2,192,512]{2,1,0:T(8,128)(2,1)S(1)}, u32[]{:S(2)}, u32[]{:S(2)}) collective-permute-start(bf16[2,192,512]{2,1,0:T(8,128)(2,1)S(1)} %get-tuple-element.86), channel_id=1, source_target_pairs={{0,1},{1,0},{2,3},{3,2},{4,5},{5,4},{6,7},{7,6},{8,9},{9,8},{10,11... | collective-permute-start | bytes 1179656 | tf_op jit(solution)/shard_map/ppermute | solution.py:439
  60.7 19.1 %collective-permute-start.15 = (bf16[16,96,384]{2,1,0:T(8,128)(2,1)S(1)}, bf16[16,96,384]{2,1,0:T(8,128)(2,1)S(1)}, u32[]{:S(2)}, u32[]{:S(2)}) collective-permute-start(bf16[16,96,384]{2,1,0:T(8,128)(2,1)S(1)} %get-tuple-element.105), channel_id=1, source_target_pairs={{0,1},{1,0},{2,3},{3,2},{4,5},{5,4},{6,7},{7,6},{8,9},{9,8},{10,11... | collective-permute-start | bytes 3538952 | tf_op jit(solution)/shard_map/ppermute | solution.py:439
  61.0 8.6 %collective-permute-start.26 = (bf16[8,48,384]{2,1,0:T(8,128)(2,1)S(1)}, bf16[8,48,384]{2,1,0:T(8,128)(2,1)S(1)}, u32[]{:S(2)}, u32[]{:S(2)}) collective-permute-start(bf16[8,48,384]{2,1,0:T(8,128)(2,1)S(1)} %slice.163), channel_id=1, source_target_pairs={{0,2},{1,5},{2,0},{3,7},{4,6},{5,1},{6,4},{7,3},{8,10},{9,13},{10,... | collective-permute-start | bytes 884744 | tf_op jit(solution)/shard_map/ppermute | solution.py:439
  69.3 6.2 %collective-permute-start.5 = (bf16[16,24,640]{2,1,0:T(8,128)(2,1)S(1)}, bf16[16,24,640]{2,1,0:T(8,128)(2,1)S(1)}, u32[]{:S(2)}, u32[]{:S(2)}) collective-permute-start(bf16[16,24,640]{2,1,0:T(8,128)(2,1)S(1)} %get-tuple-element.102), channel_id=1, source_target_pairs={{0,1},{1,0},{2,3},{3,2},{4,5},{5,4},{6,7},{7,6},{8,9},{9,8},{10,11... | collective-permute-start | bytes 1474568 | tf_op jit(solution)/shard_map/ppermute | solution.py:439
  75.7 5.9 %collective-permute-start.6 = (bf16[8,24,640]{2,1,0:T(8,128)(2,1)S(1)}, bf16[8,24,640]{2,1,0:T(8,128)(2,1)S(1)}, u32[]{:S(2)}, u32[]{:S(2)}) collective-permute-start(bf16[8,24,640]{2,1,0:T(8,128)(2,1)S(1)} %slice.165), channel_id=1, source_target_pairs={{0,2},{1,5},{2,0},{3,7},{4,6},{5,1},{6,4},{7,3},{8,10},{9,13},{10,... | collective-permute-start | bytes 737288 | tf_op jit(solution)/shard_map/ppermute | solution.py:439
  80.2 10.4 %collective-permute-start.16 = (bf16[8,96,384]{2,1,0:T(8,128)(2,1)S(1)}, bf16[8,96,384]{2,1,0:T(8,128)(2,1)S(1)}, u32[]{:S(2)}, u32[]{:S(2)}) collective-permute-start(bf16[8,96,384]{2,1,0:T(8,128)(2,1)S(1)} %slice.162), channel_id=1, source_target_pairs={{0,2},{1,5},{2,0},{3,7},{4,6},{5,1},{6,4},{7,3},{8,10},{9,13},{10,... | collective-permute-start | bytes 1769480 | tf_op jit(solution)/shard_map/ppermute | solution.py:439
  81.6 16.6 %collective-permute-start.7 = (bf16[4,24,640]{2,1,0:T(8,128)(2,1)S(1)}, bf16[4,24,640]{2,1,0:T(8,128)(2,1)S(1)}, u32[]{:S(2)}, u32[]{:S(2)}) collective-permute-start(bf16[4,24,640]{2,1,0:T(8,128)(2,1)S(1)} %slice.168), channel_id=1, source_target_pairs={{0,4},{1,3},{2,6},{3,1},{4,0},{5,7},{6,2},{7,5},{8,12},{9,11},{10,... | collective-permute-start | bytes 368648 | tf_op jit(solution)/shard_map/ppermute | solution.py:439
  85.9 5.8 %collective-permute-start.31 = (bf16[2,48,384]{2,1,0:T(8,128)(2,1)S(1)}, bf16[2,48,384]{2,1,0:T(8,128)(2,1)S(1)}, u32[]{:S(2)}, u32[]{:S(2)}) collective-permute-start(bf16[2,48,384]{2,1,0:T(8,128)(2,1)S(1)} %pad_maximum_fusion.7), channel_id=1, source_target_pairs={{0,8},{1,9},{2,10},{3,11},{4,12},{5,13},{6,14},{7,15},{8,0},{9,1},... | collective-permute-start | bytes 221192 | tf_op jit(solution)/shard_map/ppermute | solution.py:439
  90.8 5.9 %collective-permute-start.17 = (bf16[4,96,384]{2,1,0:T(8,128)(2,1)S(1)}, bf16[4,96,384]{2,1,0:T(8,128)(2,1)S(1)}, u32[]{:S(2)}, u32[]{:S(2)}) collective-permute-start(bf16[4,96,384]{2,1,0:T(8,128)(2,1)S(1)} %slice.164), channel_id=1, source_target_pairs={{0,4},{1,3},{2,6},{3,1},{4,0},{5,7},{6,2},{7,5},{8,12},{9,11},{10,... | collective-permute-start | bytes 884744 | tf_op jit(solution)/shard_map/ppermute | solution.py:439
  91.8 24.5 %collective-permute-start.32 = (bf16[4,48,384]{2,1,0:T(8,128)(2,1)S(1)}, bf16[4,48,384]{2,1,0:T(8,128)(2,1)S(1)}, u32[]{:S(2)}, u32[]{:S(2)}) collective-permute-start(bf16[4,48,384]{2,1,0:T(8,128)(2,1)S(1)} %pad_maximum_fusion.5), channel_id=1, source_target_pairs={{0,4},{1,3},{2,6},{3,1},{4,0},{5,7},{6,2},{7,5},{8,12},{9,11},{10,... | collective-permute-start | bytes 442376 | tf_op jit(solution)/shard_map/ppermute | solution.py:439
  105.9 7.2 %collective-permute-start.10 = (bf16[1,24,640]{2,1,0:T(8,128)(2,1)S(1)}, bf16[1,24,640]{2,1,0:T(8,128)(2,1)S(1)}, u32[]{:S(2)}, u32[]{:S(2)}) collective-permute-start(bf16[1,24,640]{2,1,0:T(8,128)(2,1)S(1)} %get-tuple-element.119), channel_id=1, source_target_pairs={{0,16},{1,17},{2,18},{3,19},{4,20},{5,21},{6,22},{7,23},{8,24},{9,... | collective-permute-start | bytes 92168 | tf_op jit(solution)/shard_map/ppermute | solution.py:439
  110.3 5.7 %collective-permute-start.21 = (bf16[2,96,384]{2,1,0:T(8,128)(2,1)S(1)}, bf16[2,96,384]{2,1,0:T(8,128)(2,1)S(1)}, u32[]{:S(2)}, u32[]{:S(2)}) collective-permute-start(bf16[2,96,384]{2,1,0:T(8,128)(2,1)S(1)} %pad_maximum_fusion.4), channel_id=1, source_target_pairs={{0,8},{1,9},{2,10},{3,11},{4,12},{5,13},{6,14},{7,15},{8,0},{9,1},... | collective-permute-start | bytes 442376 | tf_op jit(solution)/shard_map/ppermute | solution.py:439
  113.1 11.1 %collective-permute-start.11 = (bf16[2,24,640]{2,1,0:T(8,128)(2,1)S(1)}, bf16[2,24,640]{2,1,0:T(8,128)(2,1)S(1)}, u32[]{:S(2)}, u32[]{:S(2)}) collective-permute-start(bf16[2,24,640]{2,1,0:T(8,128)(2,1)S(1)} %pad_maximum_fusion.8), channel_id=1, source_target_pairs={{0,8},{1,9},{2,10},{3,11},{4,12},{5,13},{6,14},{7,15},{8,0},{9,1},... | collective-permute-start | bytes 184328 | tf_op jit(solution)/shard_map/ppermute | solution.py:439
  116.1 5.9 %collective-permute-start.22 = (bf16[4,96,384]{2,1,0:T(8,128)(2,1)S(1)}, bf16[4,96,384]{2,1,0:T(8,128)(2,1)S(1)}, u32[]{:S(2)}, u32[]{:S(2)}) collective-permute-start(bf16[4,96,384]{2,1,0:T(8,128)(2,1)S(1)} %pad_maximum_fusion.1), channel_id=1, source_target_pairs={{0,4},{1,3},{2,6},{3,1},{4,0},{5,7},{6,2},{7,5},{8,12},{9,11},{10,... | collective-permute-start | bytes 884744 | tf_op jit(solution)/shard_map/ppermute | solution.py:439
  116.4 29.6 %collective-permute-start.33 = (bf16[8,48,384]{2,1,0:T(8,128)(2,1)S(1)}, bf16[8,48,384]{2,1,0:T(8,128)(2,1)S(1)}, u32[]{:S(2)}, u32[]{:S(2)}) collective-permute-start(bf16[8,48,384]{2,1,0:T(8,128)(2,1)S(1)} %pad_maximum_fusion.2), channel_id=1, source_target_pairs={{0,2},{1,5},{2,0},{3,7},{4,6},{5,1},{6,4},{7,3},{8,10},{9,13},{10,... | collective-permute-start | bytes 884744 | tf_op jit(solution)/shard_map/ppermute | solution.py:439
  122.1 12.5 %collective-permute-start.23 = (bf16[8,96,384]{2,1,0:T(8,128)(2,1)S(1)}, bf16[8,96,384]{2,1,0:T(8,128)(2,1)S(1)}, u32[]{:S(2)}, u32[]{:S(2)}) collective-permute-start(bf16[8,96,384]{2,1,0:T(8,128)(2,1)S(1)} %pad_maximum_fusion), channel_id=1, source_target_pairs={{0,2},{1,5},{2,0},{3,7},{4,6},{5,1},{6,4},{7,3},{8,10},{9,13},{10,... | collective-permute-start | bytes 1769480 | tf_op jit(solution)/shard_map/ppermute | solution.py:439
  124.2 19.9 %collective-permute-start.12 = (bf16[4,24,640]{2,1,0:T(8,128)(2,1)S(1)}, bf16[4,24,640]{2,1,0:T(8,128)(2,1)S(1)}, u32[]{:S(2)}, u32[]{:S(2)}) collective-permute-start(bf16[4,24,640]{2,1,0:T(8,128)(2,1)S(1)} %pad_maximum_fusion.6), channel_id=1, source_target_pairs={{0,4},{1,3},{2,6},{3,1},{4,0},{5,7},{6,2},{7,5},{8,12},{9,11},{10,... | collective-permute-start | bytes 368648 | tf_op jit(solution)/shard_map/ppermute | solution.py:439
  134.8 20.3 %collective-permute-start.24 = (bf16[16,96,384]{2,1,0:T(8,128)(2,1)S(1)}, bf16[16,96,384]{2,1,0:T(8,128)(2,1)S(1)}, u32[]{:S(2)}, u32[]{:S(2)}) collective-permute-start(bf16[16,96,384]{2,1,0:T(8,128)(2,1)S(1)} %get-tuple-element.120), channel_id=1, source_target_pairs={{0,1},{1,0},{2,3},{3,2},{4,5},{5,4},{6,7},{7,6},{8,9},{9,8},{10,11... | collective-permute-start | bytes 3538952 | tf_op jit(solution)/shard_map/ppermute | solution.py:439
  144.2 5.7 %collective-permute-start.13 = (bf16[8,24,640]{2,1,0:T(8,128)(2,1)S(1)}, bf16[8,24,640]{2,1,0:T(8,128)(2,1)S(1)}, u32[]{:S(2)}, u32[]{:S(2)}) collective-permute-start(bf16[8,24,640]{2,1,0:T(8,128)(2,1)S(1)} %pad_maximum_fusion.3), channel_id=1, source_target_pairs={{0,2},{1,5},{2,0},{3,7},{4,6},{5,1},{6,4},{7,3},{8,10},{9,13},{10,... | collective-permute-start | bytes 737288 | tf_op jit(solution)/shard_map/ppermute | solution.py:439
  (24 other events, 126.0 us)

commit v3 on v2

--- a/solution.py
+++ b/solution.py
@@ -20,8 +20,9 @@
 TOK = 768
 BLK = 256
 EXT = 512
-QCHUNK = (24, 640)
+WIDTH = 640
 HALF = D // 2
+COST = dict(project=3, attend=9, forward=19, backward=6, weights=4, attention=4, through=3, sum=9, finish=3)
 
 
 def nn(a, b):
@@ -61,9 +62,18 @@
 
 
 def project_kernel(
-    seg_ref, x_ref, ids_ref, wqkv_ref,
+    seg_ref, x_hbm, ids_hbm, wqkv_hbm,
     xt_ref, q_ref, k_ref, v_ref, bias_ref,
+    x_ref, ids_ref, wqkv_ref, sem,
 ):
+    loads = [
+        pltpu.make_async_copy(source, ref, sem.at[i])
+        for i, (source, ref) in enumerate(((x_hbm, x_ref), (wqkv_hbm, wqkv_ref), (ids_hbm, ids_ref)))
+    ]
+    for copy in loads:
+        copy.start()
+    for copy in loads:
+        copy.wait()
     two = seg_ref[BLK] == 1
     xt_ref[...] = x_ref[...].T
     for g in range(GROUPS):
@@ -152,11 +162,10 @@
 
 def scatter(part, jj, g, keep_ref, send_ref, at, low, far):
     for r in range(4):
-        for lh in range(2):
-            piece = part[48 * r : 48 * (r + 1), 384 * lh : 384 * (lh + 1)].astype(BF16)
-            pos = ((g & 1) * 8 + r * 2 + lh) ^ (low if jj < 2 else far)
-            ref = keep_ref if jj < 2 else send_ref
-            ref[pos, at : at + 48] = piece
+        piece = part[48 * r : 48 * (r + 1)].astype(BF16)
+        pos = ((g & 1) * 4 + r) ^ (low if jj < 2 else far)
+        ref = keep_ref if jj < 2 else send_ref
+        ref[pos, at : at + 48] = piece
 
 
 def forward_kernel(
@@ -164,7 +173,7 @@
     out_ref, hid_ref, n1_ref, inv1_ref, gpr_ref, gsec_ref, gfeed_ref, keep_ref, send_ref, gvec_ref,
     wot, w1t, act, nb, gacc,
 ):
-    core, low, far = code_ref[0], code_ref[1], code_ref[2]
+    core, low, far = code_ref[0], code_ref[3], code_ref[4]
     for j, ref in enumerate((ag_ref, as_ref, fg_ref, fs_ref)):
         nb[j] = columns(ref)
     wot[...] = wo_ref[...].T
@@ -225,11 +234,10 @@
 
 
 def backward_kernel(
-    code_ref, ctx_ref, wo_ref, w1_ref, w2t_ref, hid_ref, n1_ref, inv1_ref, gpr_ref, gsec_ref, gfeed_ref, ag_ref,
-    gctx_ref, gfirst_ref, keep_ref, send_ref, gvec_ref,
-    w2, gup, gatt, nb, gacc,
+    wo_ref, w1_ref, w2t_ref, n1_ref, inv1_ref, gpr_ref, gsec_ref, gfeed_ref, ag_ref,
+    gctx_ref, gfirst_ref, gup, gatt, gvec_ref,
+    w2, nb, gacc,
 ):
-    core, low, far = code_ref[0], code_ref[1], code_ref[2]
     nb[...] = columns(ag_ref)
     for g in range(GROUPS):
         w2[g] = w2t_ref[g].T
@@ -268,11 +276,15 @@
     lax.fori_loop(0, TOK // BLK, tile, 0)
     for j in range(2):
         gvec_ref[:, j : j + 1] = jnp.sum(gacc[j], 1, keepdims=True)
+
+
+def weights_kernel(code_ref, ctx_ref, hid_ref, gup_ref, gatt_ref, keep_ref, send_ref):
+    core, low, far = code_ref[0], code_ref[1], code_ref[2]
     for jj in (2, 3, 0, 1):
         g = jj ^ (2 * core)
         gr = pl.ds(pl.multiple_of(g * GD, GD), GD)
-        scatter(nt(hid_ref[gr, :], gup[g]), jj, g, keep_ref, send_ref, 0, low, far)
-        scatter(nt(ctx_ref[gr, :], gatt[...]), jj, g, keep_ref, send_ref, 48, low, far)
+        scatter(nt(hid_ref[gr, :], gup_ref[g]), jj, g, keep_ref, send_ref, 0, low, far)
+        scatter(nt(ctx_ref[gr, :], gatt_ref[...]), jj, g, keep_ref, send_ref, 48, low, far)
 
 
 def back_kernel(
@@ -348,11 +360,11 @@
         through.append(sum(nn(wqkv_ref[t, i], grads[t]) for t in range(3)))
         row = jnp.concatenate(
             [nt(xt_ref[rows], grad) for grad in grads]
-            + [gvec1_ref[rows], gvec2_ref[rows], jnp.zeros((GD, QCHUNK[1] - 3 * GD - 4), F32)],
+            + [gvec1_ref[rows], gvec2_ref[rows], jnp.zeros((GD, WIDTH - 3 * GD - 4), F32)],
             1,
         )
-        for r in range(8):
-            piece_ref[(i * 8 + r) ^ order] = row[24 * r : 24 * (r + 1)]
+        for r in range(4):
+            piece_ref[(i * 4 + r) ^ order] = row[48 * r : 48 * (r + 1)]
     if half:
         mine, other = piece_ref[...], first_ref[...]
         keep_ref[...] = jnp.where(core == 1, mine, other)
@@ -360,51 +372,89 @@
     gin_ref[...] = (gfirst_ref[...] + jnp.concatenate(through, 0)).astype(BF16).T
 
 
-def finish_kernel(code_ref, m_ref, *outs):
+def chunks(code_ref, near_ref, far_ref):
     core, low, far = code_ref[0], code_ref[1], code_ref[2]
-    for half in range(2):
-        for a in range(16):
-            part = m_ref[half * 16 + (a ^ (far if half else low))].astype(F32)
-            g = (half ^ core) * 2 + a // 8
-            rows = slice(48 * (a % 8 // 2), 48 * (a % 8 // 2 + 1))
-            lanes = slice(384 * (a % 2), 384 * (a % 2 + 1))
-            for i, ref in enumerate(outs):
-                ref[g, rows, lanes] = part[48 * i : 48 * (i + 1)]
-
-
-def finish_qkv_kernel(code_ref, m_ref, gq_ref, ag_ref, as_ref, fg_ref, fs_ref, vec):
-    core, low, far = code_ref[0], code_ref[1], code_ref[2]
-    for half in range(2):
-        for a in range(16):
-            part = m_ref[half * 16 + (a ^ (far if half else low))].astype(F32)
-            g = (half ^ core) * 2 + a // 8
-            rows = slice(24 * (a % 8), 24 * (a % 8 + 1))
-            for t in range(3):
-                gq_ref[t, g, rows] = part[:, t * GD : (t + 1) * GD]
-            vec[g, rows] = part[:, 512:640]
+    for other, ref in ((0, near_ref), (1, far_ref)):
+        for a in range(8):
+            g = (other ^ core) * 2 + a // 4
+            rows = slice(48 * (a % 4), 48 * (a % 4 + 1))
+            yield g, rows, ref[a ^ (far if other else low)].astype(F32)
+
+
+def finish_kernel(code_ref, half_ref, *refs, far, way, outs):
+    *refs, token_ref = refs
+    token_ref[...] = jnp.zeros_like(token_ref)
+    order = code_ref[1 + 2 * way + far]
+    for a in range(8):
+        part = half_ref[a ^ order].astype(F32)
+        rows = slice(48 * (a % 4), 48 * (a % 4 + 1))
+        for i, ref in enumerate(refs[-outs:]):
+            ref[a // 4, rows] = part[48 * i : 48 * (i + 1)]
+
+
+def finish_qkv_kernel(code_ref, near_ref, far_ref, gq_ref, ag_ref, as_ref, fg_ref, fs_ref, vec):
+    for g, rows, part in chunks(code_ref, near_ref, far_ref):
+        for t in range(3):
+            gq_ref[t, g, rows] = part[:, t * GD : (t + 1) * GD]
+        vec[g, rows] = part[:, 512:640]
     turned = vec[...].reshape(D, 128).T
     for i, ref in enumerate((ag_ref, as_ref, fg_ref, fs_ref)):
         ref[...] = turned[64 + i : 65 + i].reshape(D)
 
 
+def fold_kernel(keep_ref, came_ref, kept_ref, send_ref):
+    n = kept_ref.shape[0]
+    kept_ref[...] = keep_ref[:n].astype(F32) + came_ref[:n].astype(F32)
+    send_ref[...] = (keep_ref[n:].astype(F32) + came_ref[n:].astype(F32)).astype(BF16)
+
+
+def meet_kernel(*refs):
+    *ins, out_ref = refs
+    at = 0
+    for keep_ref, came_ref in zip(ins[::2], ins[1::2]):
+        rows = keep_ref.shape[1]
+        out_ref[:, at : at + rows] = (keep_ref[...].astype(F32) + came_ref[...].astype(F32)).astype(BF16)
+        at += rows
+
+
+def join_kernel(near_ref, far_ref, out_ref):
+    n = near_ref.shape[0]
+    out_ref[:n] = near_ref[...]
+    out_ref[n:] = far_ref[...]
+
+
 SMEM = pl.BlockSpec(memory_space=pltpu.SMEM)
 VMEM = pl.BlockSpec(memory_space=pltpu.VMEM)
 ANY = pl.BlockSpec(memory_space=pl.ANY)
 
 
-def call(kernel, name, ins, outs, scratch, limit, work, grid=(), aliases=None):
-    return pl.pallas_call(
-        kernel,
-        grid=grid,
-        out_shape=[jax.ShapeDtypeStruct(s, d) for s, d, _ in outs],
-        in_specs=[spec for _, spec in ins],
-        out_specs=[spec for _, _, spec in outs],
-        scratch_shapes=scratch,
-        compiler_params=pltpu.CompilerParams(vmem_limit_bytes=limit << 20),
-        cost_estimate=pl.CostEstimate(flops=work[0], bytes_accessed=work[1], transcendentals=0),
-        input_output_aliases=aliases or {},
-        name=name,
-    )(*[array for array, _ in ins])
+class Steps:
+    def __init__(self):
+        self.last = None
+
+    def __call__(self, kernel, name, ins, outs, scratch, limit, grid=(), code=None, aliases=None):
+        n, free = len(ins) + (code is not None), self.last is None
+        if not free:
+            ins = ins + [(self.last, ANY)]
+        specs = dict(
+            grid=grid,
+            in_specs=[spec for _, spec in ins],
+            out_specs=[spec for _, _, spec in outs],
+            scratch_shapes=scratch,
+        )
+        if code is not None:
+            specs = dict(grid_spec=pltpu.PrefetchScalarGridSpec(num_scalar_prefetch=1, **specs))
+        results = pl.pallas_call(
+            kernel if free else lambda *refs: kernel(*refs[:n], *refs[n + 1 :]),
+            out_shape=[jax.ShapeDtypeStruct(s, d) for s, d, _ in outs],
+            compiler_params=pltpu.CompilerParams(vmem_limit_bytes=limit << 20),
+            cost_estimate=pl.CostEstimate(flops=int(COST[name.split('_')[0]] * 1e9), bytes_accessed=1024, transcendentals=0),
+            input_output_aliases=aliases or {},
+            name=name,
+            **specs,
+        )(*([] if code is None else [code]), *[array for array, _ in ins])
+        self.last = results[-1]
+        return results
 
 
 def block(shape, *at):
@@ -412,12 +462,10 @@
 
 
 class Links:
-    def __init__(self, n_seq):
-        bits = max(n_seq.bit_length() - 1, 0)
+    def __init__(self, n_seq, orders):
+        bits = n_seq.bit_length() - 1
         self.n = n_seq * 2
-        orders = [list(range(bits)), [1, 0] + list(range(2, bits))] if bits > 1 else [list(range(bits))] * 2
-        self.orders = orders
-        self.halving = min(4, bits)
+        self.orders = [order + list(range(3, bits)) for order in orders]
         self.bits = bits
 
     def pairs(self, step):
@@ -426,96 +474,124 @@
         return [(i, i ^ (2 << self.orders[i & 1][step])) for i in range(self.n)]
 
     def code(self, seq, core):
-        def of(order):
-            value = 0
-            for step in range(4):
-                value = value * 2 + (((seq >> order[step]) & 1) if step < self.halving else 0)
-            return value
-
-        return jnp.where(core == 0, of(self.orders[0]), of(self.orders[1]))
+        first, second = [sum(((seq >> order[step]) & 1) << (2 - step) for step in range(3)) for order in self.orders]
+        return jnp.where(core == 0, first, second)
 
 
 def swap(x, links, step):
     return lax.ppermute(x, "dev", links.pairs(step))
 
 
-def all_sum(keep, came, links):
-    total = keep.astype(F32) + came.astype(F32)
-    for step in range(links.halving):
-        half = total.shape[0] // 2
-        total = total[:half] + swap(total[half:].astype(BF16), links, step).astype(F32)
-    piece = total.astype(BF16)
-    for step in range(links.halving, links.bits):
-        piece = (piece.astype(F32) + swap(piece, links, step).astype(F32)).astype(BF16)
-    for step in reversed(range(-1, links.halving)):
-        piece = jnp.concatenate([piece, swap(piece, links, step)], 0)
-    return piece
+class Total:
+    def __init__(self, run, links, name, keep, came):
+        self.run, self.links, self.name = run, links, name
+        self.keep, self.came = keep, came
+        self.step = 0
+
+    def small(self, kernel, ins, outs):
+        spec = [(x, VMEM) for x in ins]
+        return self.run(kernel, self.name, spec, [o + (VMEM,) for o in outs], [], 4)
+
+    def fold(self):
+        shape = (self.keep.shape[0] // 2,) + self.keep.shape[1:]
+        self.keep, send = self.small(fold_kernel, [self.keep, self.came], [(shape, F32), (shape, BF16)])
+        self.came = swap(send, self.links, self.step)
+        self.step += 1
+
+    def meet(self, *others):
+        parts = [*others, self]
+        shape = (1, sum(p.keep.shape[1] for p in parts), self.keep.shape[2])
+        ins = [x for p in parts for x in (p.keep, p.came)]
+        (self.near,) = self.small(meet_kernel, ins, [(shape, BF16)])
+        for step in range(3, self.links.bits - 1):
+            (self.near,) = self.small(meet_kernel, [self.near, swap(self.near, self.links, step)], [(shape, BF16)])
+        self.far = swap(self.near, self.links, self.links.bits - 1)
+
+    def whole(self):
+        (self.near,) = self.small(meet_kernel, [self.near, self.far], [(self.near.shape, BF16)])
+        self.step = 2
+        self.far = swap(self.near, self.links, self.step)
+
+    def join(self):
+        shape = (self.near.shape[0] * 2,) + self.near.shape[1:]
+        (self.near,) = self.small(join_kernel, [self.near, self.far], [(shape, BF16)])
+        self.step -= 1
+        self.far = swap(self.near, self.links, self.step)
 
 
 def per_device(
-    links, inputs, segment_ids, qkv_weight, out_weight, ffn_in_weight, ffn_out_weight,
+    links, upright, inputs, segment_ids, qkv_weight, out_weight, ffn_in_weight, ffn_out_weight,
     attn_gain, attn_shift, ffn_gain, ffn_shift, out_cotangent,
 ):
     me = lax.axis_index("dev")
     seq, core = me >> 1, me & 1
-    code = jnp.stack([core, links.code(seq, core), links.code(seq, 1 - core)]).astype(jnp.int32)
+    codes = [core]
+    for way in (links, upright):
+        codes += [way.code(seq, core), way.code(seq, 1 - core)]
+    code = jnp.stack(codes).astype(jnp.int32)
     partner = swap(inputs, links, -1)
     square = (D, TOK)
     large = (GROUPS, GF, TOK)
-    xt, q, k, v, bias = call(
+    run = Steps()
+    xt, q, k, v, bias = run(
         project_kernel,
         "project",
-        [(segment_ids, SMEM), (inputs, VMEM), (segment_ids, VMEM), (qkv_weight, VMEM)],
+        [(segment_ids, SMEM), (inputs, ANY), (segment_ids, ANY), (qkv_weight, ANY)],
         [(square, BF16, VMEM)] * 4 + [((2, 2 * BLK, BLK), BF16, VMEM)],
-        [],
+        [
+            pltpu.VMEM((TOK, D), BF16), pltpu.VMEM((TOK,), jnp.int32), pltpu.VMEM((3, GROUPS, GD, GD), BF16),
+            pltpu.SemaphoreType.DMA((3,)),
+        ],
         12,
-        (2_000_000_000, 7_000_000),
     )
-    kp, vp, ctx, lse = call(
+    kp, vp, ctx, lse = run(
         attend_kernel,
         "attend",
         [(segment_ids, SMEM), (partner, VMEM), (qkv_weight, VMEM), (q, VMEM), (k, VMEM), (v, VMEM), (bias, VMEM)],
         [((D, EXT), BF16, VMEM), ((D, EXT), BF16, VMEM), (square, BF16, VMEM), ((HEADS, 1, TOK), F32, VMEM)],
         [],
         12,
-        (8_000_000_000, 9_000_000),
     )
     weight2t = jnp.swapaxes(ffn_out_weight, 1, 2)
-    output, hid, n1, inv1, gpr, gsec, gfeed, keep, send, gvec2 = call(
+    output, hid, n1, inv1, gpr, gsec, gfeed, keep, send, gvec2 = run(
         forward_kernel,
         "forward",
         [(code, SMEM), (xt, VMEM), (ctx, VMEM), (out_weight, VMEM), (ffn_in_weight, VMEM), (weight2t, VMEM)]
         + [(out_cotangent, VMEM), (attn_gain, VMEM), (attn_shift, VMEM), (ffn_gain, VMEM), (ffn_shift, VMEM)],
         [((TOK, D), BF16, VMEM), (square, BF16, VMEM), (square, F32, VMEM), ((1, TOK), F32, VMEM), (large, BF16, VMEM)]
-        + [(square, F32, VMEM), (square, BF16, VMEM), ((16, 48, 384), BF16, VMEM), ((16, 48, 384), BF16, VMEM)]
+        + [(square, F32, VMEM), (square, BF16, VMEM), ((8, 48, D), BF16, VMEM), ((8, 48, D), BF16, VMEM)]
         + [((D, 2), F32, VMEM)],
         [
             pltpu.VMEM((D, D), BF16), pltpu.VMEM((GROUPS, GF, GD), BF16), pltpu.VMEM(large, BF16),
             pltpu.VMEM((4, D, BLK), F32), pltpu.VMEM((2, D, 128), F32),
         ],
         20,
-        (10_000_000_000, 20_000_000),
     )
-    came = swap(send, links, -1)
-    gctx, gfirst, keep1, send1, gvec1 = call(
+    ffn_out = Total(run, upright, "sum_ffn_out", keep, swap(send, links, -1))
+    gctx, gfirst, gup, gatt, gvec1 = run(
         backward_kernel,
         "backward",
-        [(code, SMEM), (ctx, VMEM), (out_weight, VMEM), (ffn_in_weight, VMEM), (weight2t, VMEM), (hid, VMEM)]
+        [(out_weight, VMEM), (ffn_in_weight, VMEM), (weight2t, VMEM)]
         + [(n1, VMEM), (inv1, VMEM), (gpr, VMEM), (gsec, VMEM), (gfeed, VMEM), (attn_gain, VMEM)],
-        [(square, BF16, VMEM), (square, F32, VMEM), ((16, 96, 384), BF16, VMEM), ((16, 96, 384), BF16, VMEM)]
-        + [((D, 2), F32, VMEM)],
-        [
-            pltpu.VMEM((GROUPS, GF, GD), BF16), pltpu.VMEM(large, BF16), pltpu.VMEM(square, BF16),
-            pltpu.VMEM((D, BLK), F32), pltpu.VMEM((2, D, 128), F32),
-        ],
-        18,
-        (10_000_000_000, 20_000_000),
+        [(square, BF16, VMEM), (square, F32, VMEM), (large, BF16, VMEM), (square, BF16, VMEM), ((D, 2), F32, VMEM)],
+        [pltpu.VMEM((GROUPS, GF, GD), BF16), pltpu.VMEM((D, BLK), F32), pltpu.VMEM((2, D, 128), F32)],
+        12,
     )
-    came1 = swap(send1, links, -1)
+    ffn_out.fold()
+    message = ((8, 96, D), BF16, VMEM)
+    keep, send = run(
+        weights_kernel,
+        "weights",
+        [(code, SMEM), (ctx, VMEM), (hid, VMEM), (gup, VMEM), (gatt, VMEM)],
+        [message, message],
+        [],
+        12,
+    )
+    others = Total(run, links, "sum_others", keep, swap(send, links, -1))
 
     def attention_back(g):
         rows = partial(lambda width: block((GD, width), g, 0))
-        return call(
+        return run(
             back_kernel,
             "attention_back",
             [(segment_ids, SMEM), (q, rows(TOK)), (k, rows(TOK)), (v, rows(TOK)), (kp, rows(EXT)), (vp, rows(EXT))]
@@ -523,7 +599,6 @@
             [((GD, TOK), BF16, VMEM), ((GD, TOK), F32, VMEM), ((GD, TOK), F32, VMEM), ((2, GD, EXT), BF16, VMEM)],
             [pltpu.VMEM((GD, TOK), F32), pltpu.VMEM((GD, TOK), F32)],
             10,
-            (4_000_000_000, 4_000_000),
             (1,),
         )
 
@@ -534,54 +609,90 @@
         ins += [(qkv_weight, block((3, 2, GD, GD), 0, half, 0, 0))]
         ins += [(gfirst, block((HALF, TOK), half, 0)), (gvec1, block((HALF, 2), half, 0))]
         ins += [(gvec2, block((HALF, 2), half, 0))]
-        shape = (16,) + QCHUNK
+        shape = (8, 48, WIDTH)
         outs = [((TOK, D), BF16, block((TOK, HALF), 0, half))]
         if half:
             ins += [(first[1], VMEM), (first[0], ANY)]
             outs += [(shape, F32, VMEM), (shape, BF16, VMEM)]
         else:
             outs += [(shape, F32, VMEM)]
-        return call(
+        return run(
             partial(through_kernel, half=half),
             "through_qkv",
             ins,
             outs,
             [pltpu.VMEM(shape, F32)] if half else [],
             10,
-            (2_000_000_000, 6_000_000),
             (1,),
+            None,
             {len(ins) - 1: 0} if half else None,
         )
 
-    parts = [attention_back(g) for g in range(GROUPS)]
+    rows = (GROUPS, GD, D)
+
+    def finish(total, far, into, way, n):
+        def half(c):
+            return (c[0] ^ far, 0, 0)
+
+        outs = [(rows, F32, pl.BlockSpec((2, GD, D), lambda _, c: half(c)))] * n
+        outs += [((8, 128), F32, pl.BlockSpec((8, 128), lambda _, c: (0, 0)))]
+        ins = [(total.far if far else total.near, pl.BlockSpec((8, 48 * n, D), lambda _, c: (0, 0, 0)))]
+        ins += [(x, ANY) for x in into]
+        kernel = partial(finish_kernel, far=far, way=way, outs=n)
+        return run(kernel, "finish", ins, outs, [], 12, (1,), code, {2 + i: i for i in range(len(into))})[:n]
+
+    parts = [attention_back(0)]
+    ffn_out.fold()
+    others.fold()
+    parts += [attention_back(1)]
+    ffn_out.fold()
+    parts += [attention_back(2)]
+    others.fold()
     first = through(0, parts[:2], None)
-    grad_input, keep_q, send_q = through(1, parts[2:], first)
-    m2 = all_sum(keep, came, links)
-    m1 = all_sum(keep1, came1, links)
-    mq = all_sum(keep_q, swap(send_q, links, -1), links)
-    rows = (GROUPS, GD, D)
-    (g2,) = call(finish_kernel, "finish", [(code, SMEM), (m2, VMEM)], [(rows, F32, VMEM)], [], 10, (0, 4_000_000))
-    g1, go = call(
-        finish_kernel, "finish", [(code, SMEM), (m1, VMEM)], [(rows, F32, VMEM)] * 2, [], 16, (0, 8_000_000)
-    )
-    gq, *vectors = call(
+    ffn_out.meet()
+    parts += [attention_back(3)]
+    others.fold()
+    grad_input, keep, send = through(1, parts[2:], first)
+    others.meet()
+    qkv = Total(run, links, "sum_qkv", keep, swap(send, links, -1))
+    qkv.fold()
+    ffn_out.whole()
+    qkv.fold()
+    ffn_out.join()
+    others.whole()
+    qkv.fold()
+    ffn_out.join()
+    others.join()
+    qkv.meet()
+    others.join()
+    qkv.whole()
+    ffn_out.join()
+    qkv.join()
+    near_out = finish(ffn_out, 0, [], 1, 1)
+    qkv.join()
+    (g2,) = finish(ffn_out, 1, near_out, 1, 1)
+    others.join()
+    half_way = finish(others, 0, [], 0, 2)
+    qkv.join()
+    g1, go = finish(others, 1, half_way, 0, 2)
+    gq, *vectors = run(
         finish_qkv_kernel,
         "finish_qkv",
-        [(code, SMEM), (mq, VMEM)],
+        [(code, SMEM), (qkv.near, VMEM), (qkv.far, VMEM)],
         [((3, GROUPS, GD, GD), F32, VMEM)] + [((D,), F32, VMEM)] * 4,
         [pltpu.VMEM((GROUPS, GD, 128), F32)],
         8,
-        (0, 4_000_000),
     )
     return (output, grad_input, gq, go.reshape(D, D), g1, jnp.swapaxes(g2, 1, 2)) + tuple(vectors)
 
 
 def solution(mesh):
     flat = Mesh(mesh.devices.reshape(-1), ("dev",))
-    links = Links(mesh.shape["seq"])
+    links = Links(mesh.shape["seq"], [[0, 1, 2], [1, 2, 0]])
+    upright = Links(mesh.shape["seq"], [[2, 0, 1], [0, 2, 1]])
     split, copied = P("dev"), P()
     return jax.shard_map(
-        partial(per_device, links),
+        partial(per_device, links, upright),
         mesh=flat,
         in_specs=(split, split) + (copied,) * 8 + (split,),
         out_specs=(split, split) + (copied,) * 8,

time: 159 us -> 126 us (0.79)
  waiting for transfers between devices: 40.8 us -> 22.6 us
  starting transfers between devices: 42.7 us -> 27.5 us
  Pallas kernels: 67.8 us -> 71.8 us
    ppermute x35 -> x32, waiting for transfers between devices: 40.8 us -> 22.6 us  [swap(): return lax.ppermute(x, 'dev', links.pairs(step))]
    ppermute x35 -> x32, starting transfers between devices: 42.7 us -> 27.5 us  [swap(): return lax.ppermute(x, 'dev', links.pairs(step))]
    pallas_call x13 -> x40, Pallas kernels: 67.8 us -> 71.8 us  [__call__(): pl.pallas_call(kernel if free else lambda *refs: kernel(*refs[:n], *refs[...]
    unnamed x38 -> x26, local copies, waits for them, and re-layouts: 3.62 us -> 3.28 us
  transfers between devices with their start and end apart: 35 -> 32, of which waited for: 14 -> 11; matrix products, arithmetic and copies ran while one was open for 2% -> 0% of each run, Pallas kernels for 12% -> 33%
where the time goes in v3:
time: 126 us
  Pallas kernels  71.8 us (57%)
  starting transfers between devices  27.5 us (22%)
  waiting for transfers between devices  22.6 us (18%)
  local copies, waits for them, and re-layouts  3.37 us (3%)
    pallas_call x40, Pallas kernels, __call__(): pl.pallas_call(kernel if free else lambda *refs: kernel(*refs[:n], *refs[...  71.8 us
    ppermute x32, starting transfers between devices, swap(): return lax.ppermute(x, 'dev', links.pairs(step))  27.5 us
    ppermute x32, waiting for transfers between devices, swap(): return lax.ppermute(x, 'dev', links.pairs(step))  22.6 us
    unnamed x26, local copies, waits for them, and re-layouts  3.28 us
  transfers between devices with their start and end apart: 32, of which 11 were waited for; matrix products, arithmetic and copies ran while one was open for 0% of the time, Pallas kernels for 33%

profile of v3, /device:TPU:1, one launch (start us, length us, event | category | flops | bytes accessed | tf_op | source)
XLA Modules:
  0.0 126.3 jit_solution(3343458248267555291)
XLA Ops:
  4.1 2.3 %project.1 = (bf16[768,768]{1,0:T(8,128)(2,1)S(1)}, bf16[768,768]{1,0:T(8,128)(2,1)S(1)}, bf16[768,768]{1,0:T(8,128)(2,1)S(1)}, bf16[768,768]{1,0:T(8,128)(2,1)S(1)}, bf16[2,512,256]{2,1,0:T(8,128)(2,1)S(1)}) custom-call(s32[768]{0:T(1024)S(1)} %copy-done.11, bf16[768,768]{1,0:T(8,128)(2,1)S(1)} %copy-done.2, s32[768]{0:T(1024)S(1)} %copy-done.11, ...), custom_call_target="tpu_custom_call" | custom-call | flops 3000000000 | bytes 1024 | tf_op jit(solution)/shard_map/project/pallas_call | solution.py:447
  6.5 8.3 %attend.1 = (bf16[768,512]{1,0:T(8,128)(2,1)S(1)}, bf16[768,512]{1,0:T(8,128)(2,1)S(1)}, bf16[768,768]{1,0:T(8,128)(2,1)S(1)}, f32[12,1,768]{2,1,0:T(1,128)S(1)}) custom-call(s32[768]{0:T(1024)S(1)} %copy-done.11, bf16[768,768]{1,0:T(8,128)(2,1)S(1)} %collective-permute-done.refs_1_, bf16[3,4,192,192]{3,2,1,0:T(8,128)(2,1)S(1)} %copy-done.1, ...), custom_call_target="tpu_custom_call" | custom-call | flops 8999999488 | bytes 1024 | tf_op jit(solution)/shard_map/attend/pallas_call | solution.py:447
  14.9 19.4 %forward.1 = (bf16[768,768]{1,0:T(8,128)(2,1)}, bf16[768,768]{1,0:T(8,128)(2,1)S(1)}, f32[768,768]{1,0:T(8,128)S(1)}, f32[1,768]{1,0:T(1,128)S(1)}, bf16[4,768,7...) custom-call(s32[5]{0:T(128)S(1)} %stack.23.refs_0_, ...), custom_call_target="tpu_custom_call" | custom-call | flops 19000000512 | bytes 1024 | tf_op jit(solution)/shard_map/forward/pallas_call | solution.py:447
  34.8 6.3 %backward.1 = (bf16[768,768]{1,0:T(8,128)(2,1)S(1)}, f32[768,768]{1,0:T(8,128)S(1)}, bf16[4,768,768]{2,1,0:T(8,128)(2,1)S(1)}, bf16[768,768]{1,0:T(8,128)(2,1)S(1)}, f32[768,2]{1,0:T(8,128)S(1)}) custom-call(bf16[768,768]{1,0:T(8,128)(2,1)S(1)} %copy-done.4, bf16[4,192,768]{2,1,0:T(8,128)(2,1)S(1)} %copy-done.5, bf16[4,192,768]{2,1,0:T(8,128)(2,1)S(1)} %bitcast.9, ...), custom_call_target="tpu_custom_call" | custom-call | flops 6000000000 | bytes 1024 | tf_op jit(solution)/shard_map/backward/pallas_call | solution.py:447
  41.3 2.3 %collective-permute-start.2 = (bf16[4,48,768]{2,1,0:T(8,128)(2,1)S(1)}, bf16[4,48,768]{2,1,0:T(8,128)(2,1)S(1)}, u32[]{:S(2)}, u32[]{:S(2)}) collective-permute-start(bf16[4,48,768]{2,1,0:T(8,128)(2,1)S(1)} %get-tuple-element.111.refs_5_), channel_id=1, source_target_pairs={{0,8},{1,3},{2,10},{3,1},{4,12},{5,7},{6,14},{7,5},{8,0},{9,11},{1... | collective-permute-start | bytes 884744 | tf_op jit(solution)/shard_map/ppermute | solution.py:482
  43.6 3.7 %weights.1 = (bf16[8,96,768]{2,1,0:T(8,128)(2,1)S(1)}, bf16[8,96,768]{2,1,0:T(8,128)(2,1)S(1)}) custom-call(s32[5]{0:T(128)S(1)} %stack.23.refs_0_, bf16[768,768]{1,0:T(8,128)(2,1)S(1)} %get-tuple-element.95.refs_2_.refs_1_, bf16[768,768]{1,0:T(8,128)(2,1)S(1)} %get-tuple-element.112.refs_2_, bf16[4,768,768]{2,1,0:T(8,128)(2,1)S(1)} %get-tuple-element.113.refs_3_, ...), custom_call_target="tpu_custom_call" | custom-call | flops 4000000000 | bytes 1024 | tf_op jit(solution)/shard_map/weights/pallas_call | solution.py:447
  48.2 3.8 %attention_back.4 = (bf16[192,768]{1,0:T(8,128)(2,1)S(1)}, f32[192,768]{1,0:T(8,128)S(1)}, f32[192,768]{1,0:T(8,128)S(1)}, bf16[2,192,512]{2,1,0:T(8,128)(2,1)S(1)}) custom-call(s32[768]{0:T(1024)S(1)} %copy-done.12, bf16[768,768]{1,0:T(8,128)(2,1)S(1)} %get-tuple-element.91.refs_3_.refs_1_, bf16[768,768]{1,0:T(8,128)(2,1)S(1)} %get-tuple-element.92.refs_4_.refs_2_, ...), custom_call_target="tpu_custom_call" | custom-call | flops 4000000000 | bytes 1024 | tf_op jit(solution)/shard_map/attention_back/pallas_call | solution.py:447
  54.7 3.8 %attention_back.5 = (bf16[192,768]{1,0:T(8,128)(2,1)S(1)}, f32[192,768]{1,0:T(8,128)S(1)}, f32[192,768]{1,0:T(8,128)S(1)}, bf16[2,192,512]{2,1,0:T(8,128)(2,1)S(1)}) custom-call(s32[768]{0:T(1024)S(1)} %copy-done.12, bf16[768,768]{1,0:T(8,128)(2,1)S(1)} %get-tuple-element.91.refs_3_.refs_1_, bf16[768,768]{1,0:T(8,128)(2,1)S(1)} %get-tuple-element.92.refs_4_.refs_2_, ...), custom_call_target="tpu_custom_call" | custom-call | flops 4000000000 | bytes 1024 | tf_op jit(solution)/shard_map/attention_back/pallas_call | solution.py:447
  60.2 3.8 %attention_back.6 = (bf16[192,768]{1,0:T(8,128)(2,1)S(1)}, f32[192,768]{1,0:T(8,128)S(1)}, f32[192,768]{1,0:T(8,128)S(1)}, bf16[2,192,512]{2,1,0:T(8,128)(2,1)S(1)}) custom-call(s32[768]{0:T(1024)S(1)} %copy-done.12, bf16[768,768]{1,0:T(8,128)(2,1)S(1)} %get-tuple-element.91.refs_3_.refs_1_, bf16[768,768]{1,0:T(8,128)(2,1)S(1)} %get-tuple-element.92.refs_4_.refs_2_, ...), custom_call_target="tpu_custom_call" | custom-call | flops 4000000000 | bytes 1024 | tf_op jit(solution)/shard_map/attention_back/pallas_call | solution.py:447
  65.0 2.9 %through_qkv.2 = (bf16[768,768]{1,0:T(8,128)(2,1)}, f32[8,48,640]{2,1,0:T(8,128)S(1)}) custom-call(s32[5]{0:T(128)S(1)} %stack.23.refs_0_, bf16[768,768]{1,0:T(8,128)(2,1)S(1)} %get-tuple-element.90.refs_1_, bf16[192,768]{1,0:T(8,128)(2,1)S(1)} %get-tuple-element.128.refs_2_, f32[192,768]{1,0:T(8,128)S(1)} %get-tuple-element.129.refs_3_, ...), custom_call_target="tpu_custom_call" | custom-call | flops 3000000000 | bytes 1024 | tf_op jit(solution)/shard_map/through_qkv/pallas_call | solution.py:447
  67.9 2.4 %collective-permute-start.15 = (bf16[1,48,768]{2,1,0:T(8,128)(2,1)S(1)}, bf16[1,48,768]{2,1,0:T(8,128)(2,1)S(1)}, u32[]{:S(2)}, u32[]{:S(2)}) collective-permute-start(bf16[1,48,768]{2,1,0:T(8,128)(2,1)S(1)} %sum_ffn_out.11.refs_9_.refs_0_), channel_id=1, source_target_pairs={{0,16},{1,17},{2,18},{3,19},{4,20},{5,21},{6,22},{7,23},{8,24},{9,... | collective-permute-start | bytes 221192 | tf_op jit(solution)/shard_map/ppermute | solution.py:482
  70.3 3.8 %attention_back.7 = (bf16[192,768]{1,0:T(8,128)(2,1)S(1)}, f32[192,768]{1,0:T(8,128)S(1)}, f32[192,768]{1,0:T(8,128)S(1)}, bf16[2,192,512]{2,1,0:T(8,128)(2,1)S(1)}) custom-call(s32[768]{0:T(1024)S(1)} %copy-done.12, bf16[768,768]{1,0:T(8,128)(2,1)S(1)} %get-tuple-element.91.refs_3_.refs_1_, bf16[768,768]{1,0:T(8,128)(2,1)S(1)} %get-tuple-element.92.refs_4_.refs_2_, ...), custom_call_target="tpu_custom_call" | custom-call | flops 4000000000 | bytes 1024 | tf_op jit(solution)/shard_map/attention_back/pallas_call | solution.py:447
  76.9 2.9 %through_qkv.3 = (bf16[768,768]{1,0:T(8,128)(2,1)}, f32[8,48,640]{2,1,0:T(8,128)S(1)}, bf16[8,48,640]{2,1,0:T(8,128)(2,1)S(1)}) custom-call(s32[5]{0:T(128)S(1)} %stack.23.refs_0_, bf16[768,768]{1,0:T(8,128)(2,1)S(1)} %get-tuple-element.90.refs_1_, bf16[192,768]{1,0:T(8,128)(2,1)S(1)} %get-tuple-element.123.refs_2_, ...), custom_call_target="tpu_custom_call", output_to_operand_aliasing={{0}: (15, {})} | custom-call | flops 3000000000 | bytes 1024 | tf_op jit(solution)/shard_map/through_qkv/pallas_call | solution.py:447
  83.3 4.1 %collective-permute-done.14.refs_1_ = bf16[4,48,640]{2,1,0:T(8,128)(2,1)S(1)} collective-permute-done((bf16[4,48,640]{2,1,0:T(8,128)(2,1)S(1)}, bf16[4,48,640]{2,1,0:T(8,128)(2,1)S(1)}, u32[]{:S(2)}, u32[]{:S(2)}) %collective-permute-start.14) | collective-permute-done | bytes 245792 | tf_op jit(solution)/shard_map/ppermute | solution.py:482
  91.3 1.8 %collective-permute-start.19 = (bf16[1,48,640]{2,1,0:T(8,128)(2,1)S(1)}, bf16[1,48,640]{2,1,0:T(8,128)(2,1)S(1)}, u32[]{:S(2)}, u32[]{:S(2)}) collective-permute-start(bf16[1,48,640]{2,1,0:T(8,128)(2,1)S(1)} %get-tuple-element.154.refs_2_), channel_id=1, source_target_pairs={{0,8},{1,3},{2,10},{3,1},{4,12},{5,7},{6,14},{7,5},{8,0},{9,11},{1... | collective-permute-start | bytes 184328 | tf_op jit(solution)/shard_map/ppermute | solution.py:482
  96.5 9.1 %collective-permute-done.23.refs_1_ = bf16[2,96,768]{2,1,0:T(8,128)(2,1)S(1)} collective-permute-done((bf16[2,96,768]{2,1,0:T(8,128)(2,1)S(1)}, bf16[2,96,768]{2,1,0:T(8,128)(2,1)S(1)}, u32[]{:S(2)}, u32[]{:S(2)}) %collective-permute-start.23) | collective-permute-done | bytes 294944 | tf_op jit(solution)/shard_map/ppermute | solution.py:482
  107.3 2.5 %collective-permute-done.24.refs_1_ = bf16[1,48,640]{2,1,0:T(8,128)(2,1)S(1)} collective-permute-done((bf16[1,48,640]{2,1,0:T(8,128)(2,1)S(1)}, bf16[1,48,640]{2,1,0:T(8,128)(2,1)S(1)}, u32[]{:S(2)}, u32[]{:S(2)}) %collective-permute-start.24) | collective-permute-done | bytes 61472 | tf_op jit(solution)/shard_map/ppermute | solution.py:482
  110.0 1.6 %finish.4 = (f32[4,192,768]{2,1,0:T(8,128)}, f32[8,128]{1,0:T(8,128)S(1)}) custom-call(s32[5]{0:T(128)S(1)} %stack.23.refs_0_, bf16[8,48,768]{2,1,0:T(8,128)(2,1)S(1)} %sum_ffn_out.15.refs_2_.refs_1_, bf16[2,48,640]{2,1,0:T(8,128)(2,1)S(1)} %sum_qkv.13.refs_2_.refs_0_), custom_call_target="tpu_custom_call" | custom-call | flops 3000000000 | bytes 1024 | tf_op jit(solution)/shard_map/finish/pallas_call | solution.py:447
  111.6 2.4 %collective-permute-done.26.refs_1_ = bf16[2,48,640]{2,1,0:T(8,128)(2,1)S(1)} collective-permute-done((bf16[2,48,640]{2,1,0:T(8,128)(2,1)S(1)}, bf16[2,48,640]{2,1,0:T(8,128)(2,1)S(1)}, u32[]{:S(2)}, u32[]{:S(2)}) %collective-permute-start.26) | collective-permute-done | bytes 122912 | tf_op jit(solution)/shard_map/ppermute | solution.py:482
  114.0 1.5 %collective-permute-start.27 = (bf16[4,48,640]{2,1,0:T(8,128)(2,1)S(1)}, bf16[4,48,640]{2,1,0:T(8,128)(2,1)S(1)}, u32[]{:S(2)}, u32[]{:S(2)}) collective-permute-start(bf16[4,48,640]{2,1,0:T(8,128)(2,1)S(1)} %sum_qkv.14.refs_3_.refs_0_), channel_id=1, source_target_pairs={{0,2},{1,5},{2,0},{3,7},{4,6},{5,1},{6,4},{7,3},{8,10},{9,13},{10,... | collective-permute-start | bytes 737288 | tf_op jit(solution)/shard_map/ppermute | solution.py:482
  115.5 1.6 %finish.5 = (f32[4,192,768]{2,1,0:T(8,128)}, f32[8,128]{1,0:T(8,128)S(1)}) custom-call(s32[5]{0:T(128)S(1)} %stack.23.refs_0_, bf16[8,48,768]{2,1,0:T(8,128)(2,1)S(1)} %collective-permute-done.29.refs_1_, f32[4,192,768]{2,1,0:T(8,128)} %get-tuple-element.156.refs_2_, bf16[4,48,640]{2,1,0:T(8,128)(2,1)S(1)} %sum_qkv.14.refs_3_.refs_0_), custom_call_target="tpu_custom_call", output_to_operand_aliasing={{0}: (2, {})} | custom-call | flops 3000000000 | bytes 1024 | tf_op jit(solution)/shard_map/finish/pallas_call | solution.py:447
  118.7 2.1 %finish.6 = (f32[4,192,768]{2,1,0:T(8,128)}, f32[4,192,768]{2,1,0:T(8,128)}, f32[8,128]{1,0:T(8,128)S(1)}) custom-call(s32[5]{0:T(128)S(1)} %stack.23.refs_0_, bf16[8,96,768]{2,1,0:T(8,128)(2,1)S(1)} %sum_others.15.refs_1_.refs_2_, bf16[8,96,768]{2,1,0:T(8,128)(2,1)S(1)} %sum_others.15.refs_1_.refs_2_), custom_call_target="tpu_custom_call" | custom-call | flops 3000000000 | bytes 1024 | tf_op jit(solution)/shard_map/finish/pallas_call | solution.py:447
  122.0 2.1 %finish.7 = (f32[4,192,768]{2,1,0:T(8,128)}, f32[4,192,768]{2,1,0:T(8,128)}, f32[8,128]{1,0:T(8,128)S(1)}) custom-call(s32[5]{0:T(128)S(1)} %stack.23.refs_0_, bf16[8,96,768]{2,1,0:T(8,128)(2,1)S(1)} %collective-permute-done.31.refs_1_, f32[4,192,768]{2,1,0:T(8,128)} %get-tuple-element.159.refs_2_, ...), custom_call_target="tpu_custom_call", output_to_operand_aliasing={{0}: (2, {}), {1}: (3, {})} | custom-call | flops 3000000000 | bytes 1024 | tf_op jit(solution)/shard_map/finish/pallas_call | solution.py:447
  124.0 2.2 %finish_qkv.1 = (f32[3,4,192,192]{3,2,1,0:T(8,128)}, f32[768]{0:T(1024)}, f32[768]{0:T(1024)}, f32[768]{0:T(1024)}, f32[768]{0:T(1024)}) custom-call(s32[5]{0:T(128)S(1)} %stack.23.refs_0_, bf16[8,48,640]{2,1,0:T(8,128)(2,1)S(1)} %sum_qkv.15.refs_4_.refs_1_, bf16[8,48,640]{2,1,0:T(8,128)(2,1)S(1)} %collective-permute-done.30.refs_2_, ...), custom_call_target="tpu_custom_call" | custom-call | flops 3000000000 | bytes 1024 | tf_op jit(solution)/shard_map/finish_qkv/pallas_call | solution.py:447
  (107 shorter events, 28.6 us)
Async XLA Ops:
  0.6 5.8 %collective-permute-start = (bf16[768,768]{1,0:T(8,128)(2,1)}, bf16[768,768]{1,0:T(8,128)(2,1)S(1)}, u32[]{:S(2)}, u32[]{:S(2)}) collective-permute-start(bf16[768,768]{1,0:T(8,128)(2,1)} %x_hbm.1), channel_id=1, source_target_pairs={{0,1},{1,0},{2,3},{3,2},{4,5},{5,4},{6,7},{7,6},{8,9},{9,8},{10,11... | collective-permute-start | bytes 3538952 | tf_op jit(solution)/shard_map/ppermute | solution.py:482
  34.3 6.8 %collective-permute-start.1 = (bf16[8,48,768]{2,1,0:T(8,128)(2,1)S(1)}, bf16[8,48,768]{2,1,0:T(8,128)(2,1)S(1)}, u32[]{:S(2)}, u32[]{:S(2)}) collective-permute-start(bf16[8,48,768]{2,1,0:T(8,128)(2,1)S(1)} %get-tuple-element.108), channel_id=1, source_target_pairs={{0,1},{1,0},{2,3},{3,2},{4,5},{5,4},{6,7},{7,6},{8,9},{9,8},{10,11... | collective-permute-start | bytes 1769480 | tf_op jit(solution)/shard_map/ppermute | solution.py:482
  41.3 10.8 %collective-permute-start.2 = (bf16[4,48,768]{2,1,0:T(8,128)(2,1)S(1)}, bf16[4,48,768]{2,1,0:T(8,128)(2,1)S(1)}, u32[]{:S(2)}, u32[]{:S(2)}) collective-permute-start(bf16[4,48,768]{2,1,0:T(8,128)(2,1)S(1)} %get-tuple-element.111.refs_5_), channel_id=1, source_target_pairs={{0,8},{1,3},{2,10},{3,1},{4,12},{5,7},{6,14},{7,5},{8,0},{9,11},{1... | collective-permute-start | bytes 884744 | tf_op jit(solution)/shard_map/ppermute | solution.py:482
  47.3 5.9 %collective-permute-start.4 = (bf16[8,96,768]{2,1,0:T(8,128)(2,1)S(1)}, bf16[8,96,768]{2,1,0:T(8,128)(2,1)S(1)}, u32[]{:S(2)}, u32[]{:S(2)}) collective-permute-start(bf16[8,96,768]{2,1,0:T(8,128)(2,1)S(1)} %get-tuple-element.115.refs_9_), channel_id=1, source_target_pairs={{0,1},{1,0},{2,3},{3,2},{4,5},{5,4},{6,7},{7,6},{8,9},{9,8},{10,11... | collective-permute-start | bytes 3538952 | tf_op jit(solution)/shard_map/ppermute | solution.py:482
  52.0 13.0 %collective-permute-start.7 = (bf16[2,192,512]{2,1,0:T(8,128)(2,1)S(1)}, bf16[2,192,512]{2,1,0:T(8,128)(2,1)S(1)}, u32[]{:S(2)}, u32[]{:S(2)}) collective-permute-start(bf16[2,192,512]{2,1,0:T(8,128)(2,1)S(1)} %get-tuple-element.116.refs_2_), channel_id=1, source_target_pairs={{0,1},{1,0},{2,3},{3,2},{4,5},{5,4},{6,7},{7,6},{8,9},{9,8},{10,11... | collective-permute-start | bytes 1179656 | tf_op jit(solution)/shard_map/ppermute | solution.py:482
  52.2 6.7 %collective-permute-start.3 = (bf16[2,48,768]{2,1,0:T(8,128)(2,1)S(1)}, bf16[2,48,768]{2,1,0:T(8,128)(2,1)S(1)}, u32[]{:S(2)}, u32[]{:S(2)}) collective-permute-start(bf16[2,48,768]{2,1,0:T(8,128)(2,1)S(1)} %get-tuple-element.118.refs_2_), channel_id=1, source_target_pairs={{0,2},{1,9},{2,0},{3,11},{4,6},{5,13},{6,4},{7,15},{8,10},{9,1},{1... | collective-permute-start | bytes 442376 | tf_op jit(solution)/shard_map/ppermute | solution.py:482
  53.4 11.0 %collective-permute-start.9 = (bf16[4,96,768]{2,1,0:T(8,128)(2,1)S(1)}, bf16[4,96,768]{2,1,0:T(8,128)(2,1)S(1)}, u32[]{:S(2)}, u32[]{:S(2)}) collective-permute-start(bf16[4,96,768]{2,1,0:T(8,128)(2,1)S(1)} %get-tuple-element.120.refs_9_), channel_id=1, source_target_pairs={{0,2},{1,5},{2,0},{3,7},{4,6},{5,1},{6,4},{7,3},{8,10},{9,13},{10,... | collective-permute-start | bytes 1769480 | tf_op jit(solution)/shard_map/ppermute | solution.py:482
  58.5 6.5 %collective-permute-start.8 = (bf16[2,192,512]{2,1,0:T(8,128)(2,1)S(1)}, bf16[2,192,512]{2,1,0:T(8,128)(2,1)S(1)}, u32[]{:S(2)}, u32[]{:S(2)}) collective-permute-start(bf16[2,192,512]{2,1,0:T(8,128)(2,1)S(1)} %get-tuple-element.121.refs_2_), channel_id=1, source_target_pairs={{0,1},{1,0},{2,3},{3,2},{4,5},{5,4},{6,7},{7,6},{8,9},{9,8},{10,11... | collective-permute-start | bytes 1179656 | tf_op jit(solution)/shard_map/ppermute | solution.py:482
  58.9 9.0 %collective-permute-start.6 = (bf16[1,48,768]{2,1,0:T(8,128)(2,1)S(1)}, bf16[1,48,768]{2,1,0:T(8,128)(2,1)S(1)}, u32[]{:S(2)}, u32[]{:S(2)}) collective-permute-start(bf16[1,48,768]{2,1,0:T(8,128)(2,1)S(1)} %get-tuple-element.122.refs_9_), channel_id=1, source_target_pairs={{0,4},{1,5},{2,6},{3,7},{4,0},{5,1},{6,2},{7,3},{8,12},{9,13},{10,... | collective-permute-start | bytes 221192 | tf_op jit(solution)/shard_map/ppermute | solution.py:482
  64.0 12.6 %collective-permute-start.5 = (bf16[2,192,512]{2,1,0:T(8,128)(2,1)S(1)}, bf16[2,192,512]{2,1,0:T(8,128)(2,1)S(1)}, u32[]{:S(2)}, u32[]{:S(2)}) collective-permute-start(bf16[2,192,512]{2,1,0:T(8,128)(2,1)S(1)} %get-tuple-element.126.refs_2_), channel_id=1, source_target_pairs={{0,1},{1,0},{2,3},{3,2},{4,5},{5,4},{6,7},{7,6},{8,9},{9,8},{10,11... | collective-permute-start | bytes 1179656 | tf_op jit(solution)/shard_map/ppermute | solution.py:482
  64.5 11.0 %collective-permute-start.11 = (bf16[2,96,768]{2,1,0:T(8,128)(2,1)S(1)}, bf16[2,96,768]{2,1,0:T(8,128)(2,1)S(1)}, u32[]{:S(2)}, u32[]{:S(2)}) collective-permute-start(bf16[2,96,768]{2,1,0:T(8,128)(2,1)S(1)} %get-tuple-element.136.refs_14_), channel_id=1, source_target_pairs={{0,4},{1,9},{2,6},{3,11},{4,0},{5,13},{6,2},{7,15},{8,12},{9,1},{1... | collective-permute-start | bytes 884744 | tf_op jit(solution)/shard_map/ppermute | solution.py:482
  67.9 14.2 %collective-permute-start.15 = (bf16[1,48,768]{2,1,0:T(8,128)(2,1)S(1)}, bf16[1,48,768]{2,1,0:T(8,128)(2,1)S(1)}, u32[]{:S(2)}, u32[]{:S(2)}) collective-permute-start(bf16[1,48,768]{2,1,0:T(8,128)(2,1)S(1)} %sum_ffn_out.11.refs_9_.refs_0_), channel_id=1, source_target_pairs={{0,16},{1,17},{2,18},{3,19},{4,20},{5,21},{6,22},{7,23},{8,24},{9,... | collective-permute-start | bytes 221192 | tf_op jit(solution)/shard_map/ppermute | solution.py:482
  80.1 9.9 %collective-permute-start.17 = (bf16[1,96,768]{2,1,0:T(8,128)(2,1)S(1)}, bf16[1,96,768]{2,1,0:T(8,128)(2,1)S(1)}, u32[]{:S(2)}, u32[]{:S(2)}) collective-permute-start(bf16[1,96,768]{2,1,0:T(8,128)(2,1)S(1)} %sum_others.11.refs_2_.refs_0_), channel_id=1, source_target_pairs={{0,16},{1,17},{2,18},{3,19},{4,20},{5,21},{6,22},{7,23},{8,24},{9,... | collective-permute-start | bytes 442376 | tf_op jit(solution)/shard_map/ppermute | solution.py:482
  81.7 5.8 %collective-permute-start.14 = (bf16[4,48,640]{2,1,0:T(8,128)(2,1)S(1)}, bf16[4,48,640]{2,1,0:T(8,128)(2,1)S(1)}, u32[]{:S(2)}, u32[]{:S(2)}) collective-permute-start(bf16[4,48,640]{2,1,0:T(8,128)(2,1)S(1)} %get-tuple-element.150.refs_2_), channel_id=1, source_target_pairs={{0,2},{1,5},{2,0},{3,7},{4,6},{5,1},{6,4},{7,3},{8,10},{9,13},{10,... | collective-permute-start | bytes 737288 | tf_op jit(solution)/shard_map/ppermute | solution.py:482
  82.2 6.5 %collective-permute-start.18 = (bf16[1,48,768]{2,1,0:T(8,128)(2,1)S(1)}, bf16[1,48,768]{2,1,0:T(8,128)(2,1)S(1)}, u32[]{:S(2)}, u32[]{:S(2)}) collective-permute-start(bf16[1,48,768]{2,1,0:T(8,128)(2,1)S(1)} %sum_ffn_out.12.refs_2_.refs_0_), channel_id=1, source_target_pairs={{0,4},{1,5},{2,6},{3,7},{4,0},{5,1},{6,2},{7,3},{8,12},{9,13},{10,... | collective-permute-start | bytes 221192 | tf_op jit(solution)/shard_map/ppermute | solution.py:482
  90.1 5.5 %collective-permute-start.20 = (bf16[1,96,768]{2,1,0:T(8,128)(2,1)S(1)}, bf16[1,96,768]{2,1,0:T(8,128)(2,1)S(1)}, u32[]{:S(2)}, u32[]{:S(2)}) collective-permute-start(bf16[1,96,768]{2,1,0:T(8,128)(2,1)S(1)} %sum_others.12.refs_2_.refs_0_), channel_id=1, source_target_pairs={{0,8},{1,3},{2,10},{3,1},{4,12},{5,7},{6,14},{7,5},{8,0},{9,11},{1... | collective-permute-start | bytes 442376 | tf_op jit(solution)/shard_map/ppermute | solution.py:482
  91.3 4.6 %collective-permute-start.19 = (bf16[1,48,640]{2,1,0:T(8,128)(2,1)S(1)}, bf16[1,48,640]{2,1,0:T(8,128)(2,1)S(1)}, u32[]{:S(2)}, u32[]{:S(2)}) collective-permute-start(bf16[1,48,640]{2,1,0:T(8,128)(2,1)S(1)} %get-tuple-element.154.refs_2_), channel_id=1, source_target_pairs={{0,8},{1,3},{2,10},{3,1},{4,12},{5,7},{6,14},{7,5},{8,0},{9,11},{1... | collective-permute-start | bytes 184328 | tf_op jit(solution)/shard_map/ppermute | solution.py:482
  93.2 14.0 %collective-permute-start.25 = (bf16[4,48,768]{2,1,0:T(8,128)(2,1)S(1)}, bf16[4,48,768]{2,1,0:T(8,128)(2,1)S(1)}, u32[]{:S(2)}, u32[]{:S(2)}) collective-permute-start(bf16[4,48,768]{2,1,0:T(8,128)(2,1)S(1)} %sum_ffn_out.14.refs_2_.refs_0_), channel_id=1, source_target_pairs={{0,8},{1,3},{2,10},{3,1},{4,12},{5,7},{6,14},{7,5},{8,0},{9,11},{1... | collective-permute-start | bytes 884744 | tf_op jit(solution)/shard_map/ppermute | solution.py:482
  95.5 10.0 %collective-permute-start.23 = (bf16[2,96,768]{2,1,0:T(8,128)(2,1)S(1)}, bf16[2,96,768]{2,1,0:T(8,128)(2,1)S(1)}, u32[]{:S(2)}, u32[]{:S(2)}) collective-permute-start(bf16[2,96,768]{2,1,0:T(8,128)(2,1)S(1)} %sum_others.13.refs_2_.refs_0_), channel_id=1, source_target_pairs={{0,4},{1,9},{2,6},{3,11},{4,0},{5,13},{6,2},{7,15},{8,12},{9,1},{1... | collective-permute-start | bytes 884744 | tf_op jit(solution)/shard_map/ppermute | solution.py:482
  95.9 9.8 %collective-permute-start.22 = (bf16[1,48,640]{2,1,0:T(8,128)(2,1)S(1)}, bf16[1,48,640]{2,1,0:T(8,128)(2,1)S(1)}, u32[]{:S(2)}, u32[]{:S(2)}) collective-permute-start(bf16[1,48,640]{2,1,0:T(8,128)(2,1)S(1)} %sum_qkv.11.refs_2_.refs_0_), channel_id=1, source_target_pairs={{0,16},{1,17},{2,18},{3,19},{4,20},{5,21},{6,22},{7,23},{8,24},{9,... | collective-permute-start | bytes 184328 | tf_op jit(solution)/shard_map/ppermute | solution.py:482
  105.6 11.5 %collective-permute-start.28 = (bf16[4,96,768]{2,1,0:T(8,128)(2,1)S(1)}, bf16[4,96,768]{2,1,0:T(8,128)(2,1)S(1)}, u32[]{:S(2)}, u32[]{:S(2)}) collective-permute-start(bf16[4,96,768]{2,1,0:T(8,128)(2,1)S(1)} %sum_others.14.refs_2_.refs_0_), channel_id=1, source_target_pairs={{0,2},{1,5},{2,0},{3,7},{4,6},{5,1},{6,4},{7,3},{8,10},{9,13},{10,... | collective-permute-start | bytes 1769480 | tf_op jit(solution)/shard_map/ppermute | solution.py:482
  107.3 8.3 %collective-permute-start.29 = (bf16[8,48,768]{2,1,0:T(8,128)(2,1)S(1)}, bf16[8,48,768]{2,1,0:T(8,128)(2,1)S(1)}, u32[]{:S(2)}, u32[]{:S(2)}) collective-permute-start(bf16[8,48,768]{2,1,0:T(8,128)(2,1)S(1)} %sum_ffn_out.15.refs_2_.refs_1_), channel_id=1, source_target_pairs={{0,1},{1,0},{2,3},{3,2},{4,5},{5,4},{6,7},{7,6},{8,9},{9,8},{10,11... | collective-permute-start | bytes 1769480 | tf_op jit(solution)/shard_map/ppermute | solution.py:482
  114.0 6.8 %collective-permute-start.27 = (bf16[4,48,640]{2,1,0:T(8,128)(2,1)S(1)}, bf16[4,48,640]{2,1,0:T(8,128)(2,1)S(1)}, u32[]{:S(2)}, u32[]{:S(2)}) collective-permute-start(bf16[4,48,640]{2,1,0:T(8,128)(2,1)S(1)} %sum_qkv.14.refs_3_.refs_0_), channel_id=1, source_target_pairs={{0,2},{1,5},{2,0},{3,7},{4,6},{5,1},{6,4},{7,3},{8,10},{9,13},{10,... | collective-permute-start | bytes 737288 | tf_op jit(solution)/shard_map/ppermute | solution.py:482
  117.2 4.7 %collective-permute-start.31 = (bf16[8,96,768]{2,1,0:T(8,128)(2,1)S(1)}, bf16[8,96,768]{2,1,0:T(8,128)(2,1)S(1)}, u32[]{:S(2)}, u32[]{:S(2)}) collective-permute-start(bf16[8,96,768]{2,1,0:T(8,128)(2,1)S(1)} %sum_others.15.refs_1_.refs_2_), channel_id=1, source_target_pairs={{0,1},{1,0},{2,3},{3,2},{4,5},{5,4},{6,7},{7,6},{8,9},{9,8},{10,11... | collective-permute-start | bytes 3538952 | tf_op jit(solution)/shard_map/ppermute | solution.py:482
  (21 other events, 105.9 us)

commit v4 on v3

--- a/solution.py
+++ b/solution.py
@@ -19,6 +19,7 @@
 GF = FF // GROUPS
 TOK = 768
 BLK = 256
+SHORT = 128
 EXT = 512
 WIDTH = 640
 HALF = D // 2
@@ -59,6 +60,26 @@
             second(items[t - lag])
         if 0 <= t - last < n:
             third(items[t - last])
+
+
+def stages(items, first, second, third, lag, last):
+    n = len(items)
+    for t in range(n + last):
+        if t < n:
+            first(items[t])
+        if 0 <= t - lag < n:
+            second(items[t - lag])
+        if 0 <= t - last < n:
+            third(items[t - last])
+        yield
+
+
+def weave(*streams):
+    streams = list(streams)
+    while streams:
+        for stream in list(streams):
+            if next(stream, streams) is streams:
+                streams.remove(stream)
 
 
 def project_kernel(
@@ -93,7 +114,7 @@
     bias_ref[0, :BLK] = same(1, 1)
     bias_ref[0, BLK:] = jnp.where(two, jnp.zeros((BLK, BLK), BF16), same(2, 1))
     bias_ref[1, :BLK] = same(2, 2)
-    bias_ref[1, BLK:] = same(1, 2)
+    bias_ref[1, BLK : BLK + SHORT] = same(1, 2)[SHORT:]
 
 
 def pick(ref, far_ref, hr, b, two):
@@ -102,7 +123,7 @@
     elif b == 1:
         other = jnp.where(two, far_ref[hr, BLK:], ref[hr, 2 * BLK :])
     else:
-        other = ref[hr, BLK : 2 * BLK]
+        other = ref[hr, BLK + SHORT : 2 * BLK]
     return jnp.concatenate([ref[hr, b * BLK : (b + 1) * BLK], other], 1)
 
 
@@ -127,7 +148,7 @@
         def scores(d):
             s = tn(pick(k_ref, kp_ref, d["hr"], d["b"], two), q_ref[d["hr"], d["qc"]])
             if d["b"]:
-                s = s + bias_ref[d["b"] - 1].astype(F32)
+                s = s + bias_ref[d["b"] - 1, : s.shape[0]].astype(F32)
             d["s"] = s
 
         def weights(d):
@@ -171,7 +192,7 @@
 def forward_kernel(
     code_ref, xt_ref, ctx_ref, wo_ref, w1_ref, w2t_ref, cot_ref, ag_ref, as_ref, fg_ref, fs_ref,
     out_ref, hid_ref, n1_ref, inv1_ref, gpr_ref, gsec_ref, gfeed_ref, keep_ref, send_ref, gvec_ref,
-    wot, w1t, act, nb, gacc,
+    wot, w1t, act, nb, gacc, held,
 ):
     core, low, far = code_ref[0], code_ref[3], code_ref[4]
     for j, ref in enumerate((ag_ref, as_ref, fg_ref, fs_ref)):
@@ -181,49 +202,91 @@
         w1t[g] = w1_ref[g].T
     gacc[...] = jnp.zeros_like(gacc)
 
-    def tile(t, carry):
-        tc = pl.ds(pl.multiple_of(t * BLK, BLK), BLK)
-        r = xt_ref[:, tc].astype(F32) + nn(wot[...], ctx_ref[:, tc])
-        centre = r - jnp.mean(r, 0, keepdims=True)
-        inv1 = lax.rsqrt(jnp.mean(centre * centre, 0, keepdims=True) + EPSILON)
-        n1 = centre * inv1
-        n1_ref[:, tc] = n1
+    channels = [slice(g * GD, (g + 1) * GD) for g in range(GROUPS)]
+
+    def at(t):
+        return pl.ds(pl.multiple_of(t * BLK, BLK), BLK)
+
+    def mean(pieces):
+        return sum(jnp.sum(x, 0, keepdims=True) for x in pieces) * (1.0 / D)
+
+    def enter(t):
+        tc, r = at(t), []
+        for ch in channels:
+            r.append(xt_ref[ch, tc].astype(F32) + nn(wot[ch], ctx_ref[:, tc]))
+            yield
+        average = mean(r)
+        centre = [x - average for x in r]
+        yield
+        inv1 = lax.rsqrt(mean([x * x for x in centre]) + EPSILON)
         inv1_ref[:, tc] = inv1
-        hidden = n1 * nb[0] + nb[1]
-        hid_ref[:, tc] = hidden.astype(BF16)
-        up, feeds = {}, []
+        yield
+        for ch, x in zip(channels, centre):
+            n1 = x * inv1
+            n1_ref[ch, tc] = n1
+            hidden = n1 * nb[0, ch] + nb[1, ch]
+            hid_ref[ch, tc] = hidden.astype(BF16)
+            held[t & 1, ch] = hidden
+            yield
+
+    def middle(t, feeds):
+        tc, up = at(t), {}
 
         def rise(p):
             g, fr = p
-            up[g, fr.start] = nn(w1t[g, fr], hid_ref[g * GD : (g + 1) * GD, tc])
+            up[g, fr.start] = nn(w1t[g, fr], hid_ref[channels[g], tc])
 
         def bend(p):
             g, fr = p
-            a, d = gelu_parts(up.pop((g, fr.start)))
+            a, slope = gelu_parts(up.pop((g, fr.start)))
             act[g, fr, tc] = a.astype(BF16)
-            gpr_ref[g, fr, tc] = d.astype(BF16)
+            gpr_ref[g, fr, tc] = slope.astype(BF16)
 
         def fall(p):
             if p[1].stop == GF:
                 feeds.append(nn(w2t_ref[p[0]], act[p[0], :, tc]))
 
-        pipelined(PARTS, rise, bend, fall, 2, 3)
-        r2 = hidden + jnp.concatenate(feeds, 0)
-        centre2 = r2 - jnp.mean(r2, 0, keepdims=True)
-        inv2 = lax.rsqrt(jnp.mean(centre2 * centre2, 0, keepdims=True) + EPSILON)
-        n2 = centre2 * inv2
-        out_ref[tc, :] = (n2 * nb[2] + nb[3]).astype(BF16).T
-        c = cot_ref[tc, :].T.astype(F32)
-        gacc[0] += halves(c * n2)
-        gacc[1] += halves(c)
-        cg = c * nb[2]
-        gsec = inv2 * (
-            cg - jnp.mean(cg, 0, keepdims=True) - n2 * jnp.mean(cg * n2, 0, keepdims=True)
-        )
-        gsec_ref[:, tc] = gsec
-        gfeed_ref[:, tc] = gsec.astype(BF16)
+        yield from stages(PARTS, rise, bend, fall, 2, 3)
+
+    def leave(t, feeds):
+        tc = at(t)
+        r2 = [held[t & 1, ch] + x for ch, x in zip(channels, feeds)]
+        average = mean(r2)
+        centre = [x - average for x in r2]
+        yield
+        inv2 = lax.rsqrt(mean([x * x for x in centre]) + EPSILON)
+        yield
+        n2, low = [], []
+        for ch, x in zip(channels, centre):
+            n2.append(x * inv2)
+            low.append((n2[-1] * nb[2, ch] + nb[3, ch]).astype(BF16))
+            yield
+        out_ref[tc, :] = jnp.concatenate(low, 0).T
+        turned = cot_ref[tc, :].T
+        yield
+        cg = []
+        for ch, n in zip(channels, n2):
+            c = turned[ch].astype(F32)
+            gacc[0, ch] += halves(c * n)
+            gacc[1, ch] += halves(c)
+            cg.append(c * nb[2, ch])
+            yield
+        first = mean(cg)
+        second = mean([x * n for x, n in zip(cg, n2)])
+        yield
+        for ch, x, n in zip(channels, cg, n2):
+            gsec = inv2 * (x - first - n * second)
+            gsec_ref[ch, tc] = gsec
+            gfeed_ref[ch, tc] = gsec.astype(BF16)
+            yield
+
+    def tile(t, carry):
+        feeds = []
+        weave(middle(t, feeds), enter(jnp.minimum(t + 1, TOK // BLK - 1)))
+        weave(leave(t, feeds))
         return carry
 
+    weave(enter(0))
     lax.fori_loop(0, TOK // BLK, tile, 0)
     for j in range(2):
         gvec_ref[:, j : j + 1] = jnp.sum(gacc[j], 1, keepdims=True)
@@ -305,7 +368,7 @@
         hr, qc, b = d["hr"], d["qc"], d["b"]
         s = tn(pick(k_ref, kp_ref, hr, b, two), q_ref[hr, qc])
         if b:
-            s = s + bias_ref[b - 1].astype(F32)
+            s = s + bias_ref[b - 1, : s.shape[0]].astype(F32)
         d["s"] = s
         d["dp"] = tn(pick(v_ref, vp_ref, hr, b, two), gctx_ref[hr, qc])
 
@@ -331,7 +394,7 @@
                 far_ref[slot, hr, BLK:] = (other * scale).astype(BF16)
                 acc[hr, 2 * BLK :] += other * (1.0 - scale)
             else:
-                acc[hr, BLK : 2 * BLK] += other
+                acc[hr, BLK + SHORT : 2 * BLK] += other
 
     pipelined(items, scores, weights, mix, 1, 2)
     dk_ref[...] = dk[...]
@@ -563,7 +626,7 @@
         + [((D, 2), F32, VMEM)],
         [
             pltpu.VMEM((D, D), BF16), pltpu.VMEM((GROUPS, GF, GD), BF16), pltpu.VMEM(large, BF16),
-            pltpu.VMEM((4, D, BLK), F32), pltpu.VMEM((2, D, 128), F32),
+            pltpu.VMEM((4, D, BLK), F32), pltpu.VMEM((2, D, 128), F32), pltpu.VMEM((2, D, BLK), F32),
         ],
         20,
     )
@@ -657,21 +720,21 @@
     qkv = Total(run, links, "sum_qkv", keep, swap(send, links, -1))
     qkv.fold()
     ffn_out.whole()
+    ffn_out.join()
     qkv.fold()
-    ffn_out.join()
     others.whole()
     qkv.fold()
-    ffn_out.join()
     others.join()
     qkv.meet()
+    ffn_out.join()
     others.join()
     qkv.whole()
     ffn_out.join()
     qkv.join()
     near_out = finish(ffn_out, 0, [], 1, 1)
     qkv.join()
+    others.join()
     (g2,) = finish(ffn_out, 1, near_out, 1, 1)
-    others.join()
     half_way = finish(others, 0, [], 0, 2)
     qkv.join()
     g1, go = finish(others, 1, half_way, 0, 2)

time: 126 us -> 124 us (0.984)
  waiting for transfers between devices: 22.6 us -> 19.3 us
  starting transfers between devices: 27.5 us -> 30.7 us
  Pallas kernels: 71.8 us -> 69.2 us
    ppermute x32, waiting for transfers between devices: 22.6 us -> 19.3 us  [swap(): return lax.ppermute(x, 'dev', links.pairs(step))]
    ppermute x32, starting transfers between devices: 27.5 us -> 30.7 us  [swap(): return lax.ppermute(x, 'dev', links.pairs(step))]
    pallas_call x40, Pallas kernels: 71.8 us -> 69.2 us  [__call__(): pl.pallas_call(kernel if free else lambda *refs: kernel(*refs[:n], *refs[...]
  transfers between devices with their start and end apart: 32 -> 32, of which waited for: 11 -> 10; matrix products, arithmetic and copies ran while one was open for 0% -> 0% of each run, Pallas kernels for 33% -> 33%
where the time goes in v4:
time: 124 us
  Pallas kernels  69.2 us (56%)
  starting transfers between devices  30.7 us (25%)
  waiting for transfers between devices  19.3 us (16%)
  local copies, waits for them, and re-layouts  3.37 us (3%)
    pallas_call x40, Pallas kernels, __call__(): pl.pallas_call(kernel if free else lambda *refs: kernel(*refs[:n], *refs[...  69.2 us
    ppermute x32, starting transfers between devices, swap(): return lax.ppermute(x, 'dev', links.pairs(step))  30.7 us
    ppermute x32, waiting for transfers between devices, swap(): return lax.ppermute(x, 'dev', links.pairs(step))  19.3 us
    unnamed x26, local copies, waits for them, and re-layouts  3.28 us
  transfers between devices with their start and end apart: 32, of which 10 were waited for; matrix products, arithmetic and copies ran while one was open for 0% of the time, Pallas kernels for 33%

profile of v4, /device:TPU:1, one launch (start us, length us, event | category | flops | bytes accessed | tf_op | source)
XLA Modules:
  0.0 123.6 jit_solution(4972346989605480619)
XLA Ops:
  4.1 2.3 %project.1 = (bf16[768,768]{1,0:T(8,128)(2,1)S(1)}, bf16[768,768]{1,0:T(8,128)(2,1)S(1)}, bf16[768,768]{1,0:T(8,128)(2,1)S(1)}, bf16[768,768]{1,0:T(8,128)(2,1)S(1)}, bf16[2,512,256]{2,1,0:T(8,128)(2,1)S(1)}) custom-call(s32[768]{0:T(1024)S(1)} %copy-done.11, bf16[768,768]{1,0:T(8,128)(2,1)S(1)} %copy-done.2, s32[768]{0:T(1024)S(1)} %copy-done.11, ...), custom_call_target="tpu_custom_call" | custom-call | flops 3000000000 | bytes 1024 | tf_op jit(solution)/shard_map/project/pallas_call | solution.py:510
  6.5 7.8 %attend.1 = (bf16[768,512]{1,0:T(8,128)(2,1)S(1)}, bf16[768,512]{1,0:T(8,128)(2,1)S(1)}, bf16[768,768]{1,0:T(8,128)(2,1)S(1)}, f32[12,1,768]{2,1,0:T(1,128)S(1)}) custom-call(s32[768]{0:T(1024)S(1)} %copy-done.11, bf16[768,768]{1,0:T(8,128)(2,1)S(1)} %collective-permute-done.refs_1_, bf16[3,4,192,192]{3,2,1,0:T(8,128)(2,1)S(1)} %copy-done.1, ...), custom_call_target="tpu_custom_call" | custom-call | flops 8999999488 | bytes 1024 | tf_op jit(solution)/shard_map/attend/pallas_call | solution.py:510
  14.4 18.1 %forward.1 = (bf16[768,768]{1,0:T(8,128)(2,1)}, bf16[768,768]{1,0:T(8,128)(2,1)S(1)}, f32[768,768]{1,0:T(8,128)S(1)}, f32[1,768]{1,0:T(1,128)S(1)}, bf16[4,768,7...) custom-call(s32[5]{0:T(128)S(1)} %stack.23.refs_0_, ...), custom_call_target="tpu_custom_call" | custom-call | flops 19000000512 | bytes 1024 | tf_op jit(solution)/shard_map/forward/pallas_call | solution.py:510
  33.0 6.3 %backward.1 = (bf16[768,768]{1,0:T(8,128)(2,1)S(1)}, f32[768,768]{1,0:T(8,128)S(1)}, bf16[4,768,768]{2,1,0:T(8,128)(2,1)S(1)}, bf16[768,768]{1,0:T(8,128)(2,1)S(1)}, f32[768,2]{1,0:T(8,128)S(1)}) custom-call(bf16[768,768]{1,0:T(8,128)(2,1)S(1)} %copy-done.4, bf16[4,192,768]{2,1,0:T(8,128)(2,1)S(1)} %copy-done.5, bf16[4,192,768]{2,1,0:T(8,128)(2,1)S(1)} %bitcast.9, ...), custom_call_target="tpu_custom_call" | custom-call | flops 6000000000 | bytes 1024 | tf_op jit(solution)/shard_map/backward/pallas_call | solution.py:510
  39.5 2.3 %collective-permute-start.2 = (bf16[4,48,768]{2,1,0:T(8,128)(2,1)S(1)}, bf16[4,48,768]{2,1,0:T(8,128)(2,1)S(1)}, u32[]{:S(2)}, u32[]{:S(2)}) collective-permute-start(bf16[4,48,768]{2,1,0:T(8,128)(2,1)S(1)} %get-tuple-element.111.refs_5_), channel_id=1, source_target_pairs={{0,8},{1,3},{2,10},{3,1},{4,12},{5,7},{6,14},{7,5},{8,0},{9,11},{1... | collective-permute-start | bytes 884744 | tf_op jit(solution)/shard_map/ppermute | solution.py:545
  41.8 3.7 %weights.1 = (bf16[8,96,768]{2,1,0:T(8,128)(2,1)S(1)}, bf16[8,96,768]{2,1,0:T(8,128)(2,1)S(1)}) custom-call(s32[5]{0:T(128)S(1)} %stack.23.refs_0_, bf16[768,768]{1,0:T(8,128)(2,1)S(1)} %get-tuple-element.95.refs_2_.refs_1_, bf16[768,768]{1,0:T(8,128)(2,1)S(1)} %get-tuple-element.112.refs_2_, bf16[4,768,768]{2,1,0:T(8,128)(2,1)S(1)} %get-tuple-element.113.refs_3_, ...), custom_call_target="tpu_custom_call" | custom-call | flops 4000000000 | bytes 1024 | tf_op jit(solution)/shard_map/weights/pallas_call | solution.py:510
  46.4 3.6 %attention_back.4 = (bf16[192,768]{1,0:T(8,128)(2,1)S(1)}, f32[192,768]{1,0:T(8,128)S(1)}, f32[192,768]{1,0:T(8,128)S(1)}, bf16[2,192,512]{2,1,0:T(8,128)(2,1)S(1)}) custom-call(s32[768]{0:T(1024)S(1)} %copy-done.12, bf16[768,768]{1,0:T(8,128)(2,1)S(1)} %get-tuple-element.91.refs_3_.refs_1_, bf16[768,768]{1,0:T(8,128)(2,1)S(1)} %get-tuple-element.92.refs_4_.refs_2_, ...), custom_call_target="tpu_custom_call" | custom-call | flops 4000000000 | bytes 1024 | tf_op jit(solution)/shard_map/attention_back/pallas_call | solution.py:510
  52.7 3.6 %attention_back.5 = (bf16[192,768]{1,0:T(8,128)(2,1)S(1)}, f32[192,768]{1,0:T(8,128)S(1)}, f32[192,768]{1,0:T(8,128)S(1)}, bf16[2,192,512]{2,1,0:T(8,128)(2,1)S(1)}) custom-call(s32[768]{0:T(1024)S(1)} %copy-done.12, bf16[768,768]{1,0:T(8,128)(2,1)S(1)} %get-tuple-element.91.refs_3_.refs_1_, bf16[768,768]{1,0:T(8,128)(2,1)S(1)} %get-tuple-element.92.refs_4_.refs_2_, ...), custom_call_target="tpu_custom_call" | custom-call | flops 4000000000 | bytes 1024 | tf_op jit(solution)/shard_map/attention_back/pallas_call | solution.py:510
  58.0 3.6 %attention_back.6 = (bf16[192,768]{1,0:T(8,128)(2,1)S(1)}, f32[192,768]{1,0:T(8,128)S(1)}, f32[192,768]{1,0:T(8,128)S(1)}, bf16[2,192,512]{2,1,0:T(8,128)(2,1)S(1)}) custom-call(s32[768]{0:T(1024)S(1)} %copy-done.12, bf16[768,768]{1,0:T(8,128)(2,1)S(1)} %get-tuple-element.91.refs_3_.refs_1_, bf16[768,768]{1,0:T(8,128)(2,1)S(1)} %get-tuple-element.92.refs_4_.refs_2_, ...), custom_call_target="tpu_custom_call" | custom-call | flops 4000000000 | bytes 1024 | tf_op jit(solution)/shard_map/attention_back/pallas_call | solution.py:510
  62.6 2.9 %through_qkv.2 = (bf16[768,768]{1,0:T(8,128)(2,1)}, f32[8,48,640]{2,1,0:T(8,128)S(1)}) custom-call(s32[5]{0:T(128)S(1)} %stack.23.refs_0_, bf16[768,768]{1,0:T(8,128)(2,1)S(1)} %get-tuple-element.90.refs_1_, bf16[192,768]{1,0:T(8,128)(2,1)S(1)} %get-tuple-element.128.refs_2_, f32[192,768]{1,0:T(8,128)S(1)} %get-tuple-element.129.refs_3_, ...), custom_call_target="tpu_custom_call" | custom-call | flops 3000000000 | bytes 1024 | tf_op jit(solution)/shard_map/through_qkv/pallas_call | solution.py:510
  65.5 2.4 %collective-permute-start.15 = (bf16[1,48,768]{2,1,0:T(8,128)(2,1)S(1)}, bf16[1,48,768]{2,1,0:T(8,128)(2,1)S(1)}, u32[]{:S(2)}, u32[]{:S(2)}) collective-permute-start(bf16[1,48,768]{2,1,0:T(8,128)(2,1)S(1)} %sum_ffn_out.11.refs_9_.refs_0_), channel_id=1, source_target_pairs={{0,16},{1,17},{2,18},{3,19},{4,20},{5,21},{6,22},{7,23},{8,24},{9,... | collective-permute-start | bytes 221192 | tf_op jit(solution)/shard_map/ppermute | solution.py:545
  67.9 3.6 %attention_back.7 = (bf16[192,768]{1,0:T(8,128)(2,1)S(1)}, f32[192,768]{1,0:T(8,128)S(1)}, f32[192,768]{1,0:T(8,128)S(1)}, bf16[2,192,512]{2,1,0:T(8,128)(2,1)S(1)}) custom-call(s32[768]{0:T(1024)S(1)} %copy-done.12, bf16[768,768]{1,0:T(8,128)(2,1)S(1)} %get-tuple-element.91.refs_3_.refs_1_, bf16[768,768]{1,0:T(8,128)(2,1)S(1)} %get-tuple-element.92.refs_4_.refs_2_, ...), custom_call_target="tpu_custom_call" | custom-call | flops 4000000000 | bytes 1024 | tf_op jit(solution)/shard_map/attention_back/pallas_call | solution.py:510
  71.5 1.8 %collective-permute-start.10 = (bf16[2,192,512]{2,1,0:T(8,128)(2,1)S(1)}, bf16[2,192,512]{2,1,0:T(8,128)(2,1)S(1)}, u32[]{:S(2)}, u32[]{:S(2)}) collective-permute-start(bf16[2,192,512]{2,1,0:T(8,128)(2,1)S(1)} %get-tuple-element.141.refs_2_), channel_id=1, source_target_pairs={{0,1},{1,0},{2,3},{3,2},{4,5},{5,4},{6,7},{7,6},{8,9},{9,8},{10,11... | collective-permute-start | bytes 1179656 | tf_op jit(solution)/shard_map/ppermute | solution.py:545
  74.6 2.9 %through_qkv.3 = (bf16[768,768]{1,0:T(8,128)(2,1)}, f32[8,48,640]{2,1,0:T(8,128)S(1)}, bf16[8,48,640]{2,1,0:T(8,128)(2,1)S(1)}) custom-call(s32[5]{0:T(128)S(1)} %stack.23.refs_0_, bf16[768,768]{1,0:T(8,128)(2,1)S(1)} %get-tuple-element.90.refs_1_, bf16[192,768]{1,0:T(8,128)(2,1)S(1)} %get-tuple-element.123.refs_2_, ...), custom_call_target="tpu_custom_call", output_to_operand_aliasing={{0}: (15, {})} | custom-call | flops 3000000000 | bytes 1024 | tf_op jit(solution)/shard_map/through_qkv/pallas_call | solution.py:510
  81.1 1.7 %collective-permute-done.16.refs_1_ = bf16[1,48,768]{2,1,0:T(8,128)(2,1)S(1)} collective-permute-done((bf16[1,48,768]{2,1,0:T(8,128)(2,1)S(1)}, bf16[1,48,768]{2,1,0:T(8,128)(2,1)S(1)}, u32[]{:S(2)}, u32[]{:S(2)}) %collective-permute-start.16) | collective-permute-done | bytes 73760 | tf_op jit(solution)/shard_map/ppermute | solution.py:545
  83.1 3.4 %collective-permute-done.14.refs_1_ = bf16[4,48,640]{2,1,0:T(8,128)(2,1)S(1)} collective-permute-done((bf16[4,48,640]{2,1,0:T(8,128)(2,1)S(1)}, bf16[4,48,640]{2,1,0:T(8,128)(2,1)S(1)}, u32[]{:S(2)}, u32[]{:S(2)}) %collective-permute-start.14) | collective-permute-done | bytes 245792 | tf_op jit(solution)/shard_map/ppermute | solution.py:545
  86.9 2.8 %collective-permute-done.18.refs_1_ = bf16[1,96,768]{2,1,0:T(8,128)(2,1)S(1)} collective-permute-done((bf16[1,96,768]{2,1,0:T(8,128)(2,1)S(1)}, bf16[1,96,768]{2,1,0:T(8,128)(2,1)S(1)}, u32[]{:S(2)}, u32[]{:S(2)}) %collective-permute-start.18) | collective-permute-done | bytes 147488 | tf_op jit(solution)/shard_map/ppermute | solution.py:545
  96.2 4.5 %collective-permute-done.22.refs_1_ = bf16[2,96,768]{2,1,0:T(8,128)(2,1)S(1)} collective-permute-done((bf16[2,96,768]{2,1,0:T(8,128)(2,1)S(1)}, bf16[2,96,768]{2,1,0:T(8,128)(2,1)S(1)}, u32[]{:S(2)}, u32[]{:S(2)}) %collective-permute-start.22) | collective-permute-done | bytes 294944 | tf_op jit(solution)/shard_map/ppermute | solution.py:545
  103.0 3.6 %collective-permute-start.29 = (bf16[8,48,768]{2,1,0:T(8,128)(2,1)S(1)}, bf16[8,48,768]{2,1,0:T(8,128)(2,1)S(1)}, u32[]{:S(2)}, u32[]{:S(2)}) collective-permute-start(bf16[8,48,768]{2,1,0:T(8,128)(2,1)S(1)} %sum_ffn_out.15.refs_2_.refs_1_), channel_id=1, source_target_pairs={{0,1},{1,0},{2,3},{3,2},{4,5},{5,4},{6,7},{7,6},{8,9},{9,8},{10,11... | collective-permute-start | bytes 1769480 | tf_op jit(solution)/shard_map/ppermute | solution.py:545
  108.6 2.1 %collective-permute-done.26.refs_1_ = bf16[2,48,640]{2,1,0:T(8,128)(2,1)S(1)} collective-permute-done((bf16[2,48,640]{2,1,0:T(8,128)(2,1)S(1)}, bf16[2,48,640]{2,1,0:T(8,128)(2,1)S(1)}, u32[]{:S(2)}, u32[]{:S(2)}) %collective-permute-start.26) | collective-permute-done | bytes 122912 | tf_op jit(solution)/shard_map/ppermute | solution.py:545
  112.1 1.8 %collective-permute-start.31 = (bf16[8,96,768]{2,1,0:T(8,128)(2,1)S(1)}, bf16[8,96,768]{2,1,0:T(8,128)(2,1)S(1)}, u32[]{:S(2)}, u32[]{:S(2)}) collective-permute-start(bf16[8,96,768]{2,1,0:T(8,128)(2,1)S(1)} %sum_others.15.refs_3_.refs_1_), channel_id=1, source_target_pairs={{0,1},{1,0},{2,3},{3,2},{4,5},{5,4},{6,7},{7,6},{8,9},{9,8},{10,11... | collective-permute-start | bytes 3538952 | tf_op jit(solution)/shard_map/ppermute | solution.py:545
  115.5 2.1 %finish.6 = (f32[4,192,768]{2,1,0:T(8,128)}, f32[4,192,768]{2,1,0:T(8,128)}, f32[8,128]{1,0:T(8,128)S(1)}) custom-call(s32[5]{0:T(128)S(1)} %stack.23.refs_0_, bf16[8,96,768]{2,1,0:T(8,128)(2,1)S(1)} %sum_others.15.refs_3_.refs_1_, f32[8,128]{1,0:T(8,128)S(1)} %get-tuple-element.157.refs_2_), custom_call_target="tpu_custom_call" | custom-call | flops 3000000000 | bytes 1024 | tf_op jit(solution)/shard_map/finish/pallas_call | solution.py:510
  119.3 2.1 %finish.7 = (f32[4,192,768]{2,1,0:T(8,128)}, f32[4,192,768]{2,1,0:T(8,128)}, f32[8,128]{1,0:T(8,128)S(1)}) custom-call(s32[5]{0:T(128)S(1)} %stack.23.refs_0_, bf16[8,96,768]{2,1,0:T(8,128)(2,1)S(1)} %collective-permute-done.31.refs_1_, f32[4,192,768]{2,1,0:T(8,128)} %get-tuple-element.159.refs_2_, ...), custom_call_target="tpu_custom_call", output_to_operand_aliasing={{0}: (2, {}), {1}: (3, {})} | custom-call | flops 3000000000 | bytes 1024 | tf_op jit(solution)/shard_map/finish/pallas_call | solution.py:510
  121.3 2.2 %finish_qkv.1 = (f32[3,4,192,192]{3,2,1,0:T(8,128)}, f32[768]{0:T(1024)}, f32[768]{0:T(1024)}, f32[768]{0:T(1024)}, f32[768]{0:T(1024)}) custom-call(s32[5]{0:T(128)S(1)} %stack.23.refs_0_, bf16[8,48,640]{2,1,0:T(8,128)(2,1)S(1)} %sum_qkv.15.refs_4_.refs_1_, bf16[8,48,640]{2,1,0:T(8,128)(2,1)S(1)} %collective-permute-done.30.refs_2_, ...), custom_call_target="tpu_custom_call" | custom-call | flops 3000000000 | bytes 1024 | tf_op jit(solution)/shard_map/finish_qkv/pallas_call | solution.py:510
  (107 shorter events, 31.6 us)
Async XLA Ops:
  0.6 5.8 %collective-permute-start = (bf16[768,768]{1,0:T(8,128)(2,1)}, bf16[768,768]{1,0:T(8,128)(2,1)S(1)}, u32[]{:S(2)}, u32[]{:S(2)}) collective-permute-start(bf16[768,768]{1,0:T(8,128)(2,1)} %x_hbm.1), channel_id=1, source_target_pairs={{0,1},{1,0},{2,3},{3,2},{4,5},{5,4},{6,7},{7,6},{8,9},{9,8},{10,11... | collective-permute-start | bytes 3538952 | tf_op jit(solution)/shard_map/ppermute | solution.py:545
  32.5 6.8 %collective-permute-start.1 = (bf16[8,48,768]{2,1,0:T(8,128)(2,1)S(1)}, bf16[8,48,768]{2,1,0:T(8,128)(2,1)S(1)}, u32[]{:S(2)}, u32[]{:S(2)}) collective-permute-start(bf16[8,48,768]{2,1,0:T(8,128)(2,1)S(1)} %get-tuple-element.108), channel_id=1, source_target_pairs={{0,1},{1,0},{2,3},{3,2},{4,5},{5,4},{6,7},{7,6},{8,9},{9,8},{10,11... | collective-permute-start | bytes 1769480 | tf_op jit(solution)/shard_map/ppermute | solution.py:545
  39.5 10.6 %collective-permute-start.2 = (bf16[4,48,768]{2,1,0:T(8,128)(2,1)S(1)}, bf16[4,48,768]{2,1,0:T(8,128)(2,1)S(1)}, u32[]{:S(2)}, u32[]{:S(2)}) collective-permute-start(bf16[4,48,768]{2,1,0:T(8,128)(2,1)S(1)} %get-tuple-element.111.refs_5_), channel_id=1, source_target_pairs={{0,8},{1,3},{2,10},{3,1},{4,12},{5,7},{6,14},{7,5},{8,0},{9,11},{1... | collective-permute-start | bytes 884744 | tf_op jit(solution)/shard_map/ppermute | solution.py:545
  45.5 5.7 %collective-permute-start.4 = (bf16[8,96,768]{2,1,0:T(8,128)(2,1)S(1)}, bf16[8,96,768]{2,1,0:T(8,128)(2,1)S(1)}, u32[]{:S(2)}, u32[]{:S(2)}) collective-permute-start(bf16[8,96,768]{2,1,0:T(8,128)(2,1)S(1)} %get-tuple-element.115.refs_9_), channel_id=1, source_target_pairs={{0,1},{1,0},{2,3},{3,2},{4,5},{5,4},{6,7},{7,6},{8,9},{9,8},{10,11... | collective-permute-start | bytes 3538952 | tf_op jit(solution)/shard_map/ppermute | solution.py:545
  50.0 12.6 %collective-permute-start.7 = (bf16[2,192,512]{2,1,0:T(8,128)(2,1)S(1)}, bf16[2,192,512]{2,1,0:T(8,128)(2,1)S(1)}, u32[]{:S(2)}, u32[]{:S(2)}) collective-permute-start(bf16[2,192,512]{2,1,0:T(8,128)(2,1)S(1)} %get-tuple-element.116.refs_2_), channel_id=1, source_target_pairs={{0,1},{1,0},{2,3},{3,2},{4,5},{5,4},{6,7},{7,6},{8,9},{9,8},{10,11... | collective-permute-start | bytes 1179656 | tf_op jit(solution)/shard_map/ppermute | solution.py:545
  50.1 6.5 %collective-permute-start.3 = (bf16[2,48,768]{2,1,0:T(8,128)(2,1)S(1)}, bf16[2,48,768]{2,1,0:T(8,128)(2,1)S(1)}, u32[]{:S(2)}, u32[]{:S(2)}) collective-permute-start(bf16[2,48,768]{2,1,0:T(8,128)(2,1)S(1)} %get-tuple-element.118.refs_2_), channel_id=1, source_target_pairs={{0,2},{1,9},{2,0},{3,11},{4,6},{5,13},{6,4},{7,15},{8,10},{9,1},{1... | collective-permute-start | bytes 442376 | tf_op jit(solution)/shard_map/ppermute | solution.py:545
  51.4 10.5 %collective-permute-start.9 = (bf16[4,96,768]{2,1,0:T(8,128)(2,1)S(1)}, bf16[4,96,768]{2,1,0:T(8,128)(2,1)S(1)}, u32[]{:S(2)}, u32[]{:S(2)}) collective-permute-start(bf16[4,96,768]{2,1,0:T(8,128)(2,1)S(1)} %get-tuple-element.120.refs_9_), channel_id=1, source_target_pairs={{0,2},{1,5},{2,0},{3,7},{4,6},{5,1},{6,4},{7,3},{8,10},{9,13},{10,... | collective-permute-start | bytes 1769480 | tf_op jit(solution)/shard_map/ppermute | solution.py:545
  56.3 6.3 %collective-permute-start.8 = (bf16[2,192,512]{2,1,0:T(8,128)(2,1)S(1)}, bf16[2,192,512]{2,1,0:T(8,128)(2,1)S(1)}, u32[]{:S(2)}, u32[]{:S(2)}) collective-permute-start(bf16[2,192,512]{2,1,0:T(8,128)(2,1)S(1)} %get-tuple-element.121.refs_2_), channel_id=1, source_target_pairs={{0,1},{1,0},{2,3},{3,2},{4,5},{5,4},{6,7},{7,6},{8,9},{9,8},{10,11... | collective-permute-start | bytes 1179656 | tf_op jit(solution)/shard_map/ppermute | solution.py:545
  56.7 8.8 %collective-permute-start.6 = (bf16[1,48,768]{2,1,0:T(8,128)(2,1)S(1)}, bf16[1,48,768]{2,1,0:T(8,128)(2,1)S(1)}, u32[]{:S(2)}, u32[]{:S(2)}) collective-permute-start(bf16[1,48,768]{2,1,0:T(8,128)(2,1)S(1)} %get-tuple-element.122.refs_9_), channel_id=1, source_target_pairs={{0,4},{1,5},{2,6},{3,7},{4,0},{5,1},{6,2},{7,3},{8,12},{9,13},{10,... | collective-permute-start | bytes 221192 | tf_op jit(solution)/shard_map/ppermute | solution.py:545
  61.6 12.8 %collective-permute-start.5 = (bf16[2,192,512]{2,1,0:T(8,128)(2,1)S(1)}, bf16[2,192,512]{2,1,0:T(8,128)(2,1)S(1)}, u32[]{:S(2)}, u32[]{:S(2)}) collective-permute-start(bf16[2,192,512]{2,1,0:T(8,128)(2,1)S(1)} %get-tuple-element.126.refs_2_), channel_id=1, source_target_pairs={{0,1},{1,0},{2,3},{3,2},{4,5},{5,4},{6,7},{7,6},{8,9},{9,8},{10,11... | collective-permute-start | bytes 1179656 | tf_op jit(solution)/shard_map/ppermute | solution.py:545
  62.1 11.2 %collective-permute-start.11 = (bf16[2,96,768]{2,1,0:T(8,128)(2,1)S(1)}, bf16[2,96,768]{2,1,0:T(8,128)(2,1)S(1)}, u32[]{:S(2)}, u32[]{:S(2)}) collective-permute-start(bf16[2,96,768]{2,1,0:T(8,128)(2,1)S(1)} %get-tuple-element.136.refs_14_), channel_id=1, source_target_pairs={{0,4},{1,9},{2,6},{3,11},{4,0},{5,13},{6,2},{7,15},{8,12},{9,1},{1... | collective-permute-start | bytes 884744 | tf_op jit(solution)/shard_map/ppermute | solution.py:545
  65.5 14.0 %collective-permute-start.15 = (bf16[1,48,768]{2,1,0:T(8,128)(2,1)S(1)}, bf16[1,48,768]{2,1,0:T(8,128)(2,1)S(1)}, u32[]{:S(2)}, u32[]{:S(2)}) collective-permute-start(bf16[1,48,768]{2,1,0:T(8,128)(2,1)S(1)} %sum_ffn_out.11.refs_9_.refs_0_), channel_id=1, source_target_pairs={{0,16},{1,17},{2,18},{3,19},{4,20},{5,21},{6,22},{7,23},{8,24},{9,... | collective-permute-start | bytes 221192 | tf_op jit(solution)/shard_map/ppermute | solution.py:545
  79.8 9.8 %collective-permute-start.18 = (bf16[1,96,768]{2,1,0:T(8,128)(2,1)S(1)}, bf16[1,96,768]{2,1,0:T(8,128)(2,1)S(1)}, u32[]{:S(2)}, u32[]{:S(2)}) collective-permute-start(bf16[1,96,768]{2,1,0:T(8,128)(2,1)S(1)} %sum_others.11.refs_2_.refs_0_), channel_id=1, source_target_pairs={{0,16},{1,17},{2,18},{3,19},{4,20},{5,21},{6,22},{7,23},{8,24},{9,... | collective-permute-start | bytes 442376 | tf_op jit(solution)/shard_map/ppermute | solution.py:545
  79.9 6.6 %collective-permute-start.14 = (bf16[4,48,640]{2,1,0:T(8,128)(2,1)S(1)}, bf16[4,48,640]{2,1,0:T(8,128)(2,1)S(1)}, u32[]{:S(2)}, u32[]{:S(2)}) collective-permute-start(bf16[4,48,640]{2,1,0:T(8,128)(2,1)S(1)} %get-tuple-element.150.refs_2_), channel_id=1, source_target_pairs={{0,2},{1,5},{2,0},{3,7},{4,6},{5,1},{6,4},{7,3},{8,10},{9,13},{10,... | collective-permute-start | bytes 737288 | tf_op jit(solution)/shard_map/ppermute | solution.py:545
  82.8 12.3 %collective-permute-start.23 = (bf16[2,48,768]{2,1,0:T(8,128)(2,1)S(1)}, bf16[2,48,768]{2,1,0:T(8,128)(2,1)S(1)}, u32[]{:S(2)}, u32[]{:S(2)}) collective-permute-start(bf16[2,48,768]{2,1,0:T(8,128)(2,1)S(1)} %sum_ffn_out.13.refs_2_.refs_0_), channel_id=1, source_target_pairs={{0,2},{1,9},{2,0},{3,11},{4,6},{5,13},{6,4},{7,15},{8,10},{9,1},{1... | collective-permute-start | bytes 442376 | tf_op jit(solution)/shard_map/ppermute | solution.py:545
  86.5 5.0 %collective-permute-start.17 = (bf16[2,48,640]{2,1,0:T(8,128)(2,1)S(1)}, bf16[2,48,640]{2,1,0:T(8,128)(2,1)S(1)}, u32[]{:S(2)}, u32[]{:S(2)}) collective-permute-start(bf16[2,48,640]{2,1,0:T(8,128)(2,1)S(1)} %get-tuple-element.152.refs_2_), channel_id=1, source_target_pairs={{0,4},{1,9},{2,6},{3,11},{4,0},{5,13},{6,2},{7,15},{8,12},{9,1},{1... | collective-permute-start | bytes 368648 | tf_op jit(solution)/shard_map/ppermute | solution.py:545
  94.1 6.6 %collective-permute-start.22 = (bf16[2,96,768]{2,1,0:T(8,128)(2,1)S(1)}, bf16[2,96,768]{2,1,0:T(8,128)(2,1)S(1)}, u32[]{:S(2)}, u32[]{:S(2)}) collective-permute-start(bf16[2,96,768]{2,1,0:T(8,128)(2,1)S(1)} %sum_others.13.refs_2_.refs_0_), channel_id=1, source_target_pairs={{0,4},{1,9},{2,6},{3,11},{4,0},{5,13},{6,2},{7,15},{8,12},{9,1},{1... | collective-permute-start | bytes 884744 | tf_op jit(solution)/shard_map/ppermute | solution.py:545
  95.0 6.9 %collective-permute-start.21 = (bf16[1,48,640]{2,1,0:T(8,128)(2,1)S(1)}, bf16[1,48,640]{2,1,0:T(8,128)(2,1)S(1)}, u32[]{:S(2)}, u32[]{:S(2)}) collective-permute-start(bf16[1,48,640]{2,1,0:T(8,128)(2,1)S(1)} %sum_qkv.11.refs_2_.refs_0_), channel_id=1, source_target_pairs={{0,16},{1,17},{2,18},{3,19},{4,20},{5,21},{6,22},{7,23},{8,24},{9,... | collective-permute-start | bytes 184328 | tf_op jit(solution)/shard_map/ppermute | solution.py:545
  95.1 7.9 %collective-permute-start.25 = (bf16[4,48,768]{2,1,0:T(8,128)(2,1)S(1)}, bf16[4,48,768]{2,1,0:T(8,128)(2,1)S(1)}, u32[]{:S(2)}, u32[]{:S(2)}) collective-permute-start(bf16[4,48,768]{2,1,0:T(8,128)(2,1)S(1)} %sum_ffn_out.14.refs_2_.refs_0_), channel_id=1, source_target_pairs={{0,8},{1,3},{2,10},{3,1},{4,12},{5,7},{6,14},{7,5},{8,0},{9,11},{1... | collective-permute-start | bytes 884744 | tf_op jit(solution)/shard_map/ppermute | solution.py:545
  100.7 11.4 %collective-permute-start.28 = (bf16[4,96,768]{2,1,0:T(8,128)(2,1)S(1)}, bf16[4,96,768]{2,1,0:T(8,128)(2,1)S(1)}, u32[]{:S(2)}, u32[]{:S(2)}) collective-permute-start(bf16[4,96,768]{2,1,0:T(8,128)(2,1)S(1)} %sum_others.14.refs_2_.refs_0_), channel_id=1, source_target_pairs={{0,2},{1,5},{2,0},{3,7},{4,6},{5,1},{6,4},{7,3},{8,10},{9,13},{10,... | collective-permute-start | bytes 1769480 | tf_op jit(solution)/shard_map/ppermute | solution.py:545
  102.0 4.6 %collective-permute-start.24 = (bf16[1,48,640]{2,1,0:T(8,128)(2,1)S(1)}, bf16[1,48,640]{2,1,0:T(8,128)(2,1)S(1)}, u32[]{:S(2)}, u32[]{:S(2)}) collective-permute-start(bf16[1,48,640]{2,1,0:T(8,128)(2,1)S(1)} %sum_qkv.12.refs_2_.refs_0_), channel_id=1, source_target_pairs={{0,8},{1,3},{2,10},{3,1},{4,12},{5,7},{6,14},{7,5},{8,0},{9,11},{1... | collective-permute-start | bytes 184328 | tf_op jit(solution)/shard_map/ppermute | solution.py:545
  103.0 10.9 %collective-permute-start.29 = (bf16[8,48,768]{2,1,0:T(8,128)(2,1)S(1)}, bf16[8,48,768]{2,1,0:T(8,128)(2,1)S(1)}, u32[]{:S(2)}, u32[]{:S(2)}) collective-permute-start(bf16[8,48,768]{2,1,0:T(8,128)(2,1)S(1)} %sum_ffn_out.15.refs_2_.refs_1_), channel_id=1, source_target_pairs={{0,1},{1,0},{2,3},{3,2},{4,5},{5,4},{6,7},{7,6},{8,9},{9,8},{10,11... | collective-permute-start | bytes 1769480 | tf_op jit(solution)/shard_map/ppermute | solution.py:545
  110.7 6.9 %collective-permute-start.27 = (bf16[4,48,640]{2,1,0:T(8,128)(2,1)S(1)}, bf16[4,48,640]{2,1,0:T(8,128)(2,1)S(1)}, u32[]{:S(2)}, u32[]{:S(2)}) collective-permute-start(bf16[4,48,640]{2,1,0:T(8,128)(2,1)S(1)} %sum_qkv.14.refs_2_.refs_0_), channel_id=1, source_target_pairs={{0,2},{1,5},{2,0},{3,7},{4,6},{5,1},{6,4},{7,3},{8,10},{9,13},{10,... | collective-permute-start | bytes 737288 | tf_op jit(solution)/shard_map/ppermute | solution.py:545
  112.1 7.1 %collective-permute-start.31 = (bf16[8,96,768]{2,1,0:T(8,128)(2,1)S(1)}, bf16[8,96,768]{2,1,0:T(8,128)(2,1)S(1)}, u32[]{:S(2)}, u32[]{:S(2)}) collective-permute-start(bf16[8,96,768]{2,1,0:T(8,128)(2,1)S(1)} %sum_others.15.refs_3_.refs_1_), channel_id=1, source_target_pairs={{0,1},{1,0},{2,3},{3,2},{4,5},{5,4},{6,7},{7,6},{8,9},{9,8},{10,11... | collective-permute-start | bytes 3538952 | tf_op jit(solution)/shard_map/ppermute | solution.py:545
  (21 other events, 101.9 us)

commit v5 on v4

--- a/solution.py
+++ b/solution.py
@@ -82,20 +82,7 @@
                 streams.remove(stream)
 
 
-def project_kernel(
-    seg_ref, x_hbm, ids_hbm, wqkv_hbm,
-    xt_ref, q_ref, k_ref, v_ref, bias_ref,
-    x_ref, ids_ref, wqkv_ref, sem,
-):
-    loads = [
-        pltpu.make_async_copy(source, ref, sem.at[i])
-        for i, (source, ref) in enumerate(((x_hbm, x_ref), (wqkv_hbm, wqkv_ref), (ids_hbm, ids_ref)))
-    ]
-    for copy in loads:
-        copy.start()
-    for copy in loads:
-        copy.wait()
-    two = seg_ref[BLK] == 1
+def project_kernel(x_ref, wqkv_ref, xt_ref, q_ref, k_ref, v_ref):
     xt_ref[...] = x_ref[...].T
     for g in range(GROUPS):
         rows = slice(g * GD, (g + 1) * GD)
@@ -103,18 +90,6 @@
         q_ref[rows, :] = (tn(wqkv_ref[0, g], xg).astype(BF16).astype(F32) * 0.125).astype(BF16)
         k_ref[rows, :] = tn(wqkv_ref[1, g], xg).astype(BF16)
         v_ref[rows, :] = tn(wqkv_ref[2, g], xg).astype(BF16)
-    row = ids_ref[...].reshape(1, TOK)
-
-    def lanes(b):
-        return jnp.broadcast_to(row[:, b * BLK : (b + 1) * BLK], (BLK, BLK))
-
-    def same(kb, qb):
-        return jnp.where(lanes(kb).T == lanes(qb), 0.0, -1e30).astype(BF16)
-
-    bias_ref[0, :BLK] = same(1, 1)
-    bias_ref[0, BLK:] = jnp.where(two, jnp.zeros((BLK, BLK), BF16), same(2, 1))
-    bias_ref[1, :BLK] = same(2, 2)
-    bias_ref[1, BLK : BLK + SHORT] = same(1, 2)[SHORT:]
 
 
 def pick(ref, far_ref, hr, b, two):
@@ -128,10 +103,22 @@
 
 
 def attend_kernel(
-    seg_ref, xp_ref, wqkv_ref, q_ref, k_ref, v_ref, bias_ref,
-    kp_ref, vp_ref, ctx_ref, lse_ref,
+    seg_ref, ids_ref, xp_ref, wqkv_ref, q_ref, k_ref, v_ref,
+    kp_ref, vp_ref, ctx_ref, lse_ref, bias_ref,
 ):
     two = seg_ref[BLK] == 1
+    row = ids_ref[...].reshape(1, TOK)
+
+    def lanes(b):
+        return jnp.broadcast_to(row[:, b * BLK : (b + 1) * BLK], (BLK, BLK))
+
+    def same(kb, qb):
+        return jnp.where(lanes(kb).T == lanes(qb), 0.0, -1e30).astype(BF16)
+
+    bias_ref[0, :BLK] = same(1, 1)
+    bias_ref[0, BLK:] = jnp.where(two, jnp.zeros((BLK, BLK), BF16), same(2, 1))
+    bias_ref[1, :BLK] = same(2, 2)
+    bias_ref[1, BLK : BLK + SHORT] = same(1, 2)[SHORT:]
     xpt = xp_ref[:EXT, :].T
     for g in range(GROUPS):
         rows = slice(g * GD, (g + 1) * GD)
@@ -140,8 +127,8 @@
 
     def heads(i, carry):
         items = []
-        for u in range(4):
-            h = i * 4 + u
+        for u in range(6):
+            h = i * 6 + u
             hr = pl.ds(pl.multiple_of(h * HEAD_DIM, HEAD_DIM), HEAD_DIM)
             items += [{"h": h, "hr": hr, "b": b, "qc": slice(b * BLK, (b + 1) * BLK)} for b in range(3)]
 
@@ -166,7 +153,7 @@
         pipelined(items, scores, weights, mix, 2, 3)
         return carry
 
-    lax.fori_loop(0, HEADS // 4, heads, 0)
+    lax.fori_loop(0, HEADS // 6, heads, 0)
 
 
 PARTS = [(g, slice(j * BLK, (j + 1) * BLK)) for g in range(GROUPS) for j in range(GF // BLK)]
@@ -347,7 +334,11 @@
         g = jj ^ (2 * core)
         gr = pl.ds(pl.multiple_of(g * GD, GD), GD)
         scatter(nt(hid_ref[gr, :], gup_ref[g]), jj, g, keep_ref, send_ref, 0, low, far)
-        scatter(nt(ctx_ref[gr, :], gatt_ref[...]), jj, g, keep_ref, send_ref, 48, low, far)
+        if jj & 1 == 0:
+            rows = pl.ds(pl.multiple_of((jj // 2 ^ core) * HALF, HALF), HALF)
+            both = nt(ctx_ref[rows, :], gatt_ref[...])
+        mine = both[:GD] if jj & 1 == 0 else both[GD:]
+        scatter(mine, jj, g, keep_ref, send_ref, 48, low, far)
 
 
 def back_kernel(
@@ -596,22 +587,21 @@
     square = (D, TOK)
     large = (GROUPS, GF, TOK)
     run = Steps()
-    xt, q, k, v, bias = run(
+    xt, q, k, v = run(
         project_kernel,
         "project",
-        [(segment_ids, SMEM), (inputs, ANY), (segment_ids, ANY), (qkv_weight, ANY)],
-        [(square, BF16, VMEM)] * 4 + [((2, 2 * BLK, BLK), BF16, VMEM)],
-        [
-            pltpu.VMEM((TOK, D), BF16), pltpu.VMEM((TOK,), jnp.int32), pltpu.VMEM((3, GROUPS, GD, GD), BF16),
-            pltpu.SemaphoreType.DMA((3,)),
-        ],
+        [(inputs, VMEM), (qkv_weight, VMEM)],
+        [(square, BF16, VMEM)] * 4,
+        [],
         12,
     )
-    kp, vp, ctx, lse = run(
+    kp, vp, ctx, lse, bias = run(
         attend_kernel,
         "attend",
-        [(segment_ids, SMEM), (partner, VMEM), (qkv_weight, VMEM), (q, VMEM), (k, VMEM), (v, VMEM), (bias, VMEM)],
-        [((D, EXT), BF16, VMEM), ((D, EXT), BF16, VMEM), (square, BF16, VMEM), ((HEADS, 1, TOK), F32, VMEM)],
+        [(segment_ids, SMEM), (segment_ids, VMEM), (partner, VMEM), (qkv_weight, VMEM)]
+        + [(q, VMEM), (k, VMEM), (v, VMEM)],
+        [((D, EXT), BF16, VMEM), ((D, EXT), BF16, VMEM), (square, BF16, VMEM), ((HEADS, 1, TOK), F32, VMEM)]
+        + [((2, 2 * BLK, BLK), BF16, VMEM)],
         [],
         12,
     )

time: 124 us -> 121 us (0.976)
  Pallas kernels: 69.2 us -> 67.2 us
    pallas_call x40, Pallas kernels: 69.2 us -> 67.2 us  [__call__(): pl.pallas_call(kernel if free else lambda *refs: kernel(*refs[:n], *refs[...]
    unnamed x26 -> x24, local copies, waits for them, and re-layouts: 3.28 us -> 2.62 us
  transfers between devices with their start and end apart: 32 -> 32, of which waited for: 10 -> 10; matrix products, arithmetic and copies ran while one was open for 0% -> 0% of each run, Pallas kernels for 33% -> 32%
where the time goes in v5:
time: 121 us
  Pallas kernels  67.2 us (56%)
  starting transfers between devices  30.7 us (25%)
  waiting for transfers between devices  19.3 us (16%)
  local copies, waits for them, and re-layouts  2.7 us (2%)
    pallas_call x40, Pallas kernels, __call__(): pl.pallas_call(kernel if free else lambda *refs: kernel(*refs[:n], *refs[...  67.2 us
    ppermute x32, starting transfers between devices, swap(): return lax.ppermute(x, 'dev', links.pairs(step))  30.7 us
    ppermute x32, waiting for transfers between devices, swap(): return lax.ppermute(x, 'dev', links.pairs(step))  19.3 us
    unnamed x24, local copies, waits for them, and re-layouts  2.62 us
  transfers between devices with their start and end apart: 32, of which 10 were waited for; matrix products, arithmetic and copies ran while one was open for 0% of the time, Pallas kernels for 32%

profile of v5, /device:TPU:1, one launch (start us, length us, event | category | flops | bytes accessed | tf_op | source)
XLA Modules:
  0.0 120.9 jit_solution(13306099129912024781)
XLA Ops:
  4.7 7.5 %attend.1 = (bf16[768,512]{1,0:T(8,128)(2,1)S(1)}, bf16[768,512]{1,0:T(8,128)(2,1)S(1)}, bf16[768,768]{1,0:T(8,128)(2,1)S(1)}, f32[12,1,768]{2,1,0:T(1,128)S(1)}, bf16[2,512,256]{2,1,0:T(8,128)(2,1)S(1)}) custom-call(s32[768]{0:T(1024)S(1)} %copy-done.11, s32[768]{0:T(1024)S(1)} %copy-done.11, bf16[768,768]{1,0:T(8,128)(2,1)S(1)} %collective-permute-done.refs_2_, ...), custom_call_target="tpu_custom_call" | custom-call | flops 8999999488 | bytes 1024 | tf_op jit(solution)/shard_map/attend/pallas_call | solution.py:501
  12.3 18.1 %forward.1 = (bf16[768,768]{1,0:T(8,128)(2,1)}, bf16[768,768]{1,0:T(8,128)(2,1)S(1)}, f32[768,768]{1,0:T(8,128)S(1)}, f32[1,768]{1,0:T(1,128)S(1)}, bf16[4,768,7...) custom-call(s32[5]{0:T(128)S(1)} %stack.23.refs_0_, ...), custom_call_target="tpu_custom_call" | custom-call | flops 19000000512 | bytes 1024 | tf_op jit(solution)/shard_map/forward/pallas_call | solution.py:501
  30.9 6.4 %backward.1 = (bf16[768,768]{1,0:T(8,128)(2,1)S(1)}, f32[768,768]{1,0:T(8,128)S(1)}, bf16[4,768,768]{2,1,0:T(8,128)(2,1)S(1)}, bf16[768,768]{1,0:T(8,128)(2,1)S(1)}, f32[768,2]{1,0:T(8,128)S(1)}) custom-call(bf16[768,768]{1,0:T(8,128)(2,1)S(1)} %copy-done.4, bf16[4,192,768]{2,1,0:T(8,128)(2,1)S(1)} %copy-done.5, bf16[4,192,768]{2,1,0:T(8,128)(2,1)S(1)} %bitcast.9, ...), custom_call_target="tpu_custom_call" | custom-call | flops 6000000000 | bytes 1024 | tf_op jit(solution)/shard_map/backward/pallas_call | solution.py:501
  37.4 2.3 %collective-permute-start.2 = (bf16[4,48,768]{2,1,0:T(8,128)(2,1)S(1)}, bf16[4,48,768]{2,1,0:T(8,128)(2,1)S(1)}, u32[]{:S(2)}, u32[]{:S(2)}) collective-permute-start(bf16[4,48,768]{2,1,0:T(8,128)(2,1)S(1)} %get-tuple-element.111.refs_5_), channel_id=1, source_target_pairs={{0,8},{1,3},{2,10},{3,1},{4,12},{5,7},{6,14},{7,5},{8,0},{9,11},{1... | collective-permute-start | bytes 884744 | tf_op jit(solution)/shard_map/ppermute | solution.py:536
  39.7 3.1 %weights.1 = (bf16[8,96,768]{2,1,0:T(8,128)(2,1)S(1)}, bf16[8,96,768]{2,1,0:T(8,128)(2,1)S(1)}) custom-call(s32[5]{0:T(128)S(1)} %stack.23.refs_0_, bf16[768,768]{1,0:T(8,128)(2,1)S(1)} %get-tuple-element.94.refs_2_.refs_1_, bf16[768,768]{1,0:T(8,128)(2,1)S(1)} %get-tuple-element.112.refs_2_, bf16[4,768,768]{2,1,0:T(8,128)(2,1)S(1)} %get-tuple-element.113.refs_3_, ...), custom_call_target="tpu_custom_call" | custom-call | flops 4000000000 | bytes 1024 | tf_op jit(solution)/shard_map/weights/pallas_call | solution.py:501
  43.8 3.6 %attention_back.4 = (bf16[192,768]{1,0:T(8,128)(2,1)S(1)}, f32[192,768]{1,0:T(8,128)S(1)}, f32[192,768]{1,0:T(8,128)S(1)}, bf16[2,192,512]{2,1,0:T(8,128)(2,1)S(1)}) custom-call(s32[768]{0:T(1024)S(1)} %copy-done.11, bf16[768,768]{1,0:T(8,128)(2,1)S(1)} %get-tuple-element.91.refs_4_.refs_1_, bf16[768,768]{1,0:T(8,128)(2,1)S(1)} %get-tuple-element.92.refs_5_.refs_2_, ...), custom_call_target="tpu_custom_call" | custom-call | flops 4000000000 | bytes 1024 | tf_op jit(solution)/shard_map/attention_back/pallas_call | solution.py:501
  50.0 3.5 %attention_back.5 = (bf16[192,768]{1,0:T(8,128)(2,1)S(1)}, f32[192,768]{1,0:T(8,128)S(1)}, f32[192,768]{1,0:T(8,128)S(1)}, bf16[2,192,512]{2,1,0:T(8,128)(2,1)S(1)}) custom-call(s32[768]{0:T(1024)S(1)} %copy-done.11, bf16[768,768]{1,0:T(8,128)(2,1)S(1)} %get-tuple-element.91.refs_4_.refs_1_, bf16[768,768]{1,0:T(8,128)(2,1)S(1)} %get-tuple-element.92.refs_5_.refs_2_, ...), custom_call_target="tpu_custom_call" | custom-call | flops 4000000000 | bytes 1024 | tf_op jit(solution)/shard_map/attention_back/pallas_call | solution.py:501
  55.3 3.6 %attention_back.6 = (bf16[192,768]{1,0:T(8,128)(2,1)S(1)}, f32[192,768]{1,0:T(8,128)S(1)}, f32[192,768]{1,0:T(8,128)S(1)}, bf16[2,192,512]{2,1,0:T(8,128)(2,1)S(1)}) custom-call(s32[768]{0:T(1024)S(1)} %copy-done.11, bf16[768,768]{1,0:T(8,128)(2,1)S(1)} %get-tuple-element.91.refs_4_.refs_1_, bf16[768,768]{1,0:T(8,128)(2,1)S(1)} %get-tuple-element.92.refs_5_.refs_2_, ...), custom_call_target="tpu_custom_call" | custom-call | flops 4000000000 | bytes 1024 | tf_op jit(solution)/shard_map/attention_back/pallas_call | solution.py:501
  60.0 2.9 %through_qkv.2 = (bf16[768,768]{1,0:T(8,128)(2,1)}, f32[8,48,640]{2,1,0:T(8,128)S(1)}) custom-call(s32[5]{0:T(128)S(1)} %stack.23.refs_0_, bf16[768,768]{1,0:T(8,128)(2,1)S(1)} %get-tuple-element.90.refs_1_, bf16[192,768]{1,0:T(8,128)(2,1)S(1)} %get-tuple-element.128.refs_2_, f32[192,768]{1,0:T(8,128)S(1)} %get-tuple-element.129.refs_3_, ...), custom_call_target="tpu_custom_call" | custom-call | flops 3000000000 | bytes 1024 | tf_op jit(solution)/shard_map/through_qkv/pallas_call | solution.py:501
  62.8 2.4 %collective-permute-start.15 = (bf16[1,48,768]{2,1,0:T(8,128)(2,1)S(1)}, bf16[1,48,768]{2,1,0:T(8,128)(2,1)S(1)}, u32[]{:S(2)}, u32[]{:S(2)}) collective-permute-start(bf16[1,48,768]{2,1,0:T(8,128)(2,1)S(1)} %sum_ffn_out.11.refs_9_.refs_0_), channel_id=1, source_target_pairs={{0,16},{1,17},{2,18},{3,19},{4,20},{5,21},{6,22},{7,23},{8,24},{9,... | collective-permute-start | bytes 221192 | tf_op jit(solution)/shard_map/ppermute | solution.py:536
  65.2 3.6 %attention_back.7 = (bf16[192,768]{1,0:T(8,128)(2,1)S(1)}, f32[192,768]{1,0:T(8,128)S(1)}, f32[192,768]{1,0:T(8,128)S(1)}, bf16[2,192,512]{2,1,0:T(8,128)(2,1)S(1)}) custom-call(s32[768]{0:T(1024)S(1)} %copy-done.11, bf16[768,768]{1,0:T(8,128)(2,1)S(1)} %get-tuple-element.91.refs_4_.refs_1_, bf16[768,768]{1,0:T(8,128)(2,1)S(1)} %get-tuple-element.92.refs_5_.refs_2_, ...), custom_call_target="tpu_custom_call" | custom-call | flops 4000000000 | bytes 1024 | tf_op jit(solution)/shard_map/attention_back/pallas_call | solution.py:501
  68.8 1.8 %collective-permute-start.10 = (bf16[2,192,512]{2,1,0:T(8,128)(2,1)S(1)}, bf16[2,192,512]{2,1,0:T(8,128)(2,1)S(1)}, u32[]{:S(2)}, u32[]{:S(2)}) collective-permute-start(bf16[2,192,512]{2,1,0:T(8,128)(2,1)S(1)} %get-tuple-element.141.refs_2_), channel_id=1, source_target_pairs={{0,1},{1,0},{2,3},{3,2},{4,5},{5,4},{6,7},{7,6},{8,9},{9,8},{10,11... | collective-permute-start | bytes 1179656 | tf_op jit(solution)/shard_map/ppermute | solution.py:536
  72.0 2.9 %through_qkv.3 = (bf16[768,768]{1,0:T(8,128)(2,1)}, f32[8,48,640]{2,1,0:T(8,128)S(1)}, bf16[8,48,640]{2,1,0:T(8,128)(2,1)S(1)}) custom-call(s32[5]{0:T(128)S(1)} %stack.23.refs_0_, bf16[768,768]{1,0:T(8,128)(2,1)S(1)} %get-tuple-element.90.refs_1_, bf16[192,768]{1,0:T(8,128)(2,1)S(1)} %get-tuple-element.123.refs_2_, ...), custom_call_target="tpu_custom_call", output_to_operand_aliasing={{0}: (15, {})} | custom-call | flops 3000000000 | bytes 1024 | tf_op jit(solution)/shard_map/through_qkv/pallas_call | solution.py:501
  78.4 1.7 %collective-permute-done.16.refs_1_ = bf16[1,48,768]{2,1,0:T(8,128)(2,1)S(1)} collective-permute-done((bf16[1,48,768]{2,1,0:T(8,128)(2,1)S(1)}, bf16[1,48,768]{2,1,0:T(8,128)(2,1)S(1)}, u32[]{:S(2)}, u32[]{:S(2)}) %collective-permute-start.16) | collective-permute-done | bytes 73760 | tf_op jit(solution)/shard_map/ppermute | solution.py:536
  80.5 3.4 %collective-permute-done.14.refs_1_ = bf16[4,48,640]{2,1,0:T(8,128)(2,1)S(1)} collective-permute-done((bf16[4,48,640]{2,1,0:T(8,128)(2,1)S(1)}, bf16[4,48,640]{2,1,0:T(8,128)(2,1)S(1)}, u32[]{:S(2)}, u32[]{:S(2)}) %collective-permute-start.14) | collective-permute-done | bytes 245792 | tf_op jit(solution)/shard_map/ppermute | solution.py:536
  84.2 2.8 %collective-permute-done.18.refs_1_ = bf16[1,96,768]{2,1,0:T(8,128)(2,1)S(1)} collective-permute-done((bf16[1,96,768]{2,1,0:T(8,128)(2,1)S(1)}, bf16[1,96,768]{2,1,0:T(8,128)(2,1)S(1)}, u32[]{:S(2)}, u32[]{:S(2)}) %collective-permute-start.18) | collective-permute-done | bytes 147488 | tf_op jit(solution)/shard_map/ppermute | solution.py:536
  93.5 4.5 %collective-permute-done.22.refs_1_ = bf16[2,96,768]{2,1,0:T(8,128)(2,1)S(1)} collective-permute-done((bf16[2,96,768]{2,1,0:T(8,128)(2,1)S(1)}, bf16[2,96,768]{2,1,0:T(8,128)(2,1)S(1)}, u32[]{:S(2)}, u32[]{:S(2)}) %collective-permute-start.22) | collective-permute-done | bytes 294944 | tf_op jit(solution)/shard_map/ppermute | solution.py:536
  100.4 3.6 %collective-permute-start.29 = (bf16[8,48,768]{2,1,0:T(8,128)(2,1)S(1)}, bf16[8,48,768]{2,1,0:T(8,128)(2,1)S(1)}, u32[]{:S(2)}, u32[]{:S(2)}) collective-permute-start(bf16[8,48,768]{2,1,0:T(8,128)(2,1)S(1)} %sum_ffn_out.15.refs_2_.refs_1_), channel_id=1, source_target_pairs={{0,1},{1,0},{2,3},{3,2},{4,5},{5,4},{6,7},{7,6},{8,9},{9,8},{10,11... | collective-permute-start | bytes 1769480 | tf_op jit(solution)/shard_map/ppermute | solution.py:536
  105.9 2.1 %collective-permute-done.26.refs_1_ = bf16[2,48,640]{2,1,0:T(8,128)(2,1)S(1)} collective-permute-done((bf16[2,48,640]{2,1,0:T(8,128)(2,1)S(1)}, bf16[2,48,640]{2,1,0:T(8,128)(2,1)S(1)}, u32[]{:S(2)}, u32[]{:S(2)}) %collective-permute-start.26) | collective-permute-done | bytes 122912 | tf_op jit(solution)/shard_map/ppermute | solution.py:536
  109.5 1.8 %collective-permute-start.31 = (bf16[8,96,768]{2,1,0:T(8,128)(2,1)S(1)}, bf16[8,96,768]{2,1,0:T(8,128)(2,1)S(1)}, u32[]{:S(2)}, u32[]{:S(2)}) collective-permute-start(bf16[8,96,768]{2,1,0:T(8,128)(2,1)S(1)} %sum_others.15.refs_3_.refs_1_), channel_id=1, source_target_pairs={{0,1},{1,0},{2,3},{3,2},{4,5},{5,4},{6,7},{7,6},{8,9},{9,8},{10,11... | collective-permute-start | bytes 3538952 | tf_op jit(solution)/shard_map/ppermute | solution.py:536
  111.2 1.6 %finish.5 = (f32[4,192,768]{2,1,0:T(8,128)}, f32[8,128]{1,0:T(8,128)S(1)}) custom-call(s32[5]{0:T(128)S(1)} %stack.23.refs_0_, bf16[8,48,768]{2,1,0:T(8,128)(2,1)S(1)} %collective-permute-done.29.refs_1_, f32[4,192,768]{2,1,0:T(8,128)} %get-tuple-element.156.refs_2_, bf16[8,96,768]{2,1,0:T(8,128)(2,1)S(1)} %sum_others.15.refs_3_.refs_1_), custom_call_target="tpu_custom_call", output_to_operand_aliasing={{0}: (2, {})} | custom-call | flops 3000000000 | bytes 1024 | tf_op jit(solution)/shard_map/finish/pallas_call | solution.py:501
  112.9 2.1 %finish.6 = (f32[4,192,768]{2,1,0:T(8,128)}, f32[4,192,768]{2,1,0:T(8,128)}, f32[8,128]{1,0:T(8,128)S(1)}) custom-call(s32[5]{0:T(128)S(1)} %stack.23.refs_0_, bf16[8,96,768]{2,1,0:T(8,128)(2,1)S(1)} %sum_others.15.refs_3_.refs_1_, f32[8,128]{1,0:T(8,128)S(1)} %get-tuple-element.157.refs_2_), custom_call_target="tpu_custom_call" | custom-call | flops 3000000000 | bytes 1024 | tf_op jit(solution)/shard_map/finish/pallas_call | solution.py:501
  116.6 2.1 %finish.7 = (f32[4,192,768]{2,1,0:T(8,128)}, f32[4,192,768]{2,1,0:T(8,128)}, f32[8,128]{1,0:T(8,128)S(1)}) custom-call(s32[5]{0:T(128)S(1)} %stack.23.refs_0_, bf16[8,96,768]{2,1,0:T(8,128)(2,1)S(1)} %collective-permute-done.31.refs_1_, f32[4,192,768]{2,1,0:T(8,128)} %get-tuple-element.159.refs_2_, ...), custom_call_target="tpu_custom_call", output_to_operand_aliasing={{0}: (2, {}), {1}: (3, {})} | custom-call | flops 3000000000 | bytes 1024 | tf_op jit(solution)/shard_map/finish/pallas_call | solution.py:501
  118.7 2.2 %finish_qkv.1 = (f32[3,4,192,192]{3,2,1,0:T(8,128)}, f32[768]{0:T(1024)}, f32[768]{0:T(1024)}, f32[768]{0:T(1024)}, f32[768]{0:T(1024)}) custom-call(s32[5]{0:T(128)S(1)} %stack.23.refs_0_, bf16[8,48,640]{2,1,0:T(8,128)(2,1)S(1)} %sum_qkv.15.refs_4_.refs_1_, bf16[8,48,640]{2,1,0:T(8,128)(2,1)S(1)} %collective-permute-done.30.refs_2_, ...), custom_call_target="tpu_custom_call" | custom-call | flops 3000000000 | bytes 1024 | tf_op jit(solution)/shard_map/finish_qkv/pallas_call | solution.py:501
  (105 shorter events, 30.6 us)
Async XLA Ops:
  30.4 6.9 %collective-permute-start.1 = (bf16[8,48,768]{2,1,0:T(8,128)(2,1)S(1)}, bf16[8,48,768]{2,1,0:T(8,128)(2,1)S(1)}, u32[]{:S(2)}, u32[]{:S(2)}) collective-permute-start(bf16[8,48,768]{2,1,0:T(8,128)(2,1)S(1)} %get-tuple-element.108), channel_id=1, source_target_pairs={{0,1},{1,0},{2,3},{3,2},{4,5},{5,4},{6,7},{7,6},{8,9},{9,8},{10,11... | collective-permute-start | bytes 1769480 | tf_op jit(solution)/shard_map/ppermute | solution.py:536
  37.4 10.0 %collective-permute-start.2 = (bf16[4,48,768]{2,1,0:T(8,128)(2,1)S(1)}, bf16[4,48,768]{2,1,0:T(8,128)(2,1)S(1)}, u32[]{:S(2)}, u32[]{:S(2)}) collective-permute-start(bf16[4,48,768]{2,1,0:T(8,128)(2,1)S(1)} %get-tuple-element.111.refs_5_), channel_id=1, source_target_pairs={{0,8},{1,3},{2,10},{3,1},{4,12},{5,7},{6,14},{7,5},{8,0},{9,11},{1... | collective-permute-start | bytes 884744 | tf_op jit(solution)/shard_map/ppermute | solution.py:536
  42.9 5.6 %collective-permute-start.4 = (bf16[8,96,768]{2,1,0:T(8,128)(2,1)S(1)}, bf16[8,96,768]{2,1,0:T(8,128)(2,1)S(1)}, u32[]{:S(2)}, u32[]{:S(2)}) collective-permute-start(bf16[8,96,768]{2,1,0:T(8,128)(2,1)S(1)} %get-tuple-element.115.refs_9_), channel_id=1, source_target_pairs={{0,1},{1,0},{2,3},{3,2},{4,5},{5,4},{6,7},{7,6},{8,9},{9,8},{10,11... | collective-permute-start | bytes 3538952 | tf_op jit(solution)/shard_map/ppermute | solution.py:536
  47.3 12.6 %collective-permute-start.7 = (bf16[2,192,512]{2,1,0:T(8,128)(2,1)S(1)}, bf16[2,192,512]{2,1,0:T(8,128)(2,1)S(1)}, u32[]{:S(2)}, u32[]{:S(2)}) collective-permute-start(bf16[2,192,512]{2,1,0:T(8,128)(2,1)S(1)} %get-tuple-element.116.refs_2_), channel_id=1, source_target_pairs={{0,1},{1,0},{2,3},{3,2},{4,5},{5,4},{6,7},{7,6},{8,9},{9,8},{10,11... | collective-permute-start | bytes 1179656 | tf_op jit(solution)/shard_map/ppermute | solution.py:536
  47.5 6.5 %collective-permute-start.3 = (bf16[2,48,768]{2,1,0:T(8,128)(2,1)S(1)}, bf16[2,48,768]{2,1,0:T(8,128)(2,1)S(1)}, u32[]{:S(2)}, u32[]{:S(2)}) collective-permute-start(bf16[2,48,768]{2,1,0:T(8,128)(2,1)S(1)} %get-tuple-element.118.refs_2_), channel_id=1, source_target_pairs={{0,2},{1,9},{2,0},{3,11},{4,6},{5,13},{6,4},{7,15},{8,10},{9,1},{1... | collective-permute-start | bytes 442376 | tf_op jit(solution)/shard_map/ppermute | solution.py:536
  48.8 10.5 %collective-permute-start.9 = (bf16[4,96,768]{2,1,0:T(8,128)(2,1)S(1)}, bf16[4,96,768]{2,1,0:T(8,128)(2,1)S(1)}, u32[]{:S(2)}, u32[]{:S(2)}) collective-permute-start(bf16[4,96,768]{2,1,0:T(8,128)(2,1)S(1)} %get-tuple-element.120.refs_9_), channel_id=1, source_target_pairs={{0,2},{1,5},{2,0},{3,7},{4,6},{5,1},{6,4},{7,3},{8,10},{9,13},{10,... | collective-permute-start | bytes 1769480 | tf_op jit(solution)/shard_map/ppermute | solution.py:536
  53.6 6.4 %collective-permute-start.8 = (bf16[2,192,512]{2,1,0:T(8,128)(2,1)S(1)}, bf16[2,192,512]{2,1,0:T(8,128)(2,1)S(1)}, u32[]{:S(2)}, u32[]{:S(2)}) collective-permute-start(bf16[2,192,512]{2,1,0:T(8,128)(2,1)S(1)} %get-tuple-element.121.refs_2_), channel_id=1, source_target_pairs={{0,1},{1,0},{2,3},{3,2},{4,5},{5,4},{6,7},{7,6},{8,9},{9,8},{10,11... | collective-permute-start | bytes 1179656 | tf_op jit(solution)/shard_map/ppermute | solution.py:536
  54.0 8.8 %collective-permute-start.6 = (bf16[1,48,768]{2,1,0:T(8,128)(2,1)S(1)}, bf16[1,48,768]{2,1,0:T(8,128)(2,1)S(1)}, u32[]{:S(2)}, u32[]{:S(2)}) collective-permute-start(bf16[1,48,768]{2,1,0:T(8,128)(2,1)S(1)} %get-tuple-element.122.refs_9_), channel_id=1, source_target_pairs={{0,4},{1,5},{2,6},{3,7},{4,0},{5,1},{6,2},{7,3},{8,12},{9,13},{10,... | collective-permute-start | bytes 221192 | tf_op jit(solution)/shard_map/ppermute | solution.py:536
  58.9 12.9 %collective-permute-start.5 = (bf16[2,192,512]{2,1,0:T(8,128)(2,1)S(1)}, bf16[2,192,512]{2,1,0:T(8,128)(2,1)S(1)}, u32[]{:S(2)}, u32[]{:S(2)}) collective-permute-start(bf16[2,192,512]{2,1,0:T(8,128)(2,1)S(1)} %get-tuple-element.126.refs_2_), channel_id=1, source_target_pairs={{0,1},{1,0},{2,3},{3,2},{4,5},{5,4},{6,7},{7,6},{8,9},{9,8},{10,11... | collective-permute-start | bytes 1179656 | tf_op jit(solution)/shard_map/ppermute | solution.py:536
  59.4 11.2 %collective-permute-start.11 = (bf16[2,96,768]{2,1,0:T(8,128)(2,1)S(1)}, bf16[2,96,768]{2,1,0:T(8,128)(2,1)S(1)}, u32[]{:S(2)}, u32[]{:S(2)}) collective-permute-start(bf16[2,96,768]{2,1,0:T(8,128)(2,1)S(1)} %get-tuple-element.136.refs_14_), channel_id=1, source_target_pairs={{0,4},{1,9},{2,6},{3,11},{4,0},{5,13},{6,2},{7,15},{8,12},{9,1},{1... | collective-permute-start | bytes 884744 | tf_op jit(solution)/shard_map/ppermute | solution.py:536
  62.8 14.0 %collective-permute-start.15 = (bf16[1,48,768]{2,1,0:T(8,128)(2,1)S(1)}, bf16[1,48,768]{2,1,0:T(8,128)(2,1)S(1)}, u32[]{:S(2)}, u32[]{:S(2)}) collective-permute-start(bf16[1,48,768]{2,1,0:T(8,128)(2,1)S(1)} %sum_ffn_out.11.refs_9_.refs_0_), channel_id=1, source_target_pairs={{0,16},{1,17},{2,18},{3,19},{4,20},{5,21},{6,22},{7,23},{8,24},{9,... | collective-permute-start | bytes 221192 | tf_op jit(solution)/shard_map/ppermute | solution.py:536
  70.7 4.5 %collective-permute-start.13 = (bf16[1,96,768]{2,1,0:T(8,128)(2,1)S(1)}, bf16[1,96,768]{2,1,0:T(8,128)(2,1)S(1)}, u32[]{:S(2)}, u32[]{:S(2)}) collective-permute-start(bf16[1,96,768]{2,1,0:T(8,128)(2,1)S(1)} %get-tuple-element.144.refs_16_), channel_id=1, source_target_pairs={{0,8},{1,3},{2,10},{3,1},{4,12},{5,7},{6,14},{7,5},{8,0},{9,11},{1... | collective-permute-start | bytes 442376 | tf_op jit(solution)/shard_map/ppermute | solution.py:536
  77.1 9.8 %collective-permute-start.18 = (bf16[1,96,768]{2,1,0:T(8,128)(2,1)S(1)}, bf16[1,96,768]{2,1,0:T(8,128)(2,1)S(1)}, u32[]{:S(2)}, u32[]{:S(2)}) collective-permute-start(bf16[1,96,768]{2,1,0:T(8,128)(2,1)S(1)} %sum_others.11.refs_2_.refs_0_), channel_id=1, source_target_pairs={{0,16},{1,17},{2,18},{3,19},{4,20},{5,21},{6,22},{7,23},{8,24},{9,... | collective-permute-start | bytes 442376 | tf_op jit(solution)/shard_map/ppermute | solution.py:536
  77.2 6.7 %collective-permute-start.14 = (bf16[4,48,640]{2,1,0:T(8,128)(2,1)S(1)}, bf16[4,48,640]{2,1,0:T(8,128)(2,1)S(1)}, u32[]{:S(2)}, u32[]{:S(2)}) collective-permute-start(bf16[4,48,640]{2,1,0:T(8,128)(2,1)S(1)} %get-tuple-element.150.refs_2_), channel_id=1, source_target_pairs={{0,2},{1,5},{2,0},{3,7},{4,6},{5,1},{6,4},{7,3},{8,10},{9,13},{10,... | collective-permute-start | bytes 737288 | tf_op jit(solution)/shard_map/ppermute | solution.py:536
  80.1 12.3 %collective-permute-start.23 = (bf16[2,48,768]{2,1,0:T(8,128)(2,1)S(1)}, bf16[2,48,768]{2,1,0:T(8,128)(2,1)S(1)}, u32[]{:S(2)}, u32[]{:S(2)}) collective-permute-start(bf16[2,48,768]{2,1,0:T(8,128)(2,1)S(1)} %sum_ffn_out.13.refs_2_.refs_0_), channel_id=1, source_target_pairs={{0,2},{1,9},{2,0},{3,11},{4,6},{5,13},{6,4},{7,15},{8,10},{9,1},{1... | collective-permute-start | bytes 442376 | tf_op jit(solution)/shard_map/ppermute | solution.py:536
  83.9 5.0 %collective-permute-start.17 = (bf16[2,48,640]{2,1,0:T(8,128)(2,1)S(1)}, bf16[2,48,640]{2,1,0:T(8,128)(2,1)S(1)}, u32[]{:S(2)}, u32[]{:S(2)}) collective-permute-start(bf16[2,48,640]{2,1,0:T(8,128)(2,1)S(1)} %get-tuple-element.152.refs_2_), channel_id=1, source_target_pairs={{0,4},{1,9},{2,6},{3,11},{4,0},{5,13},{6,2},{7,15},{8,12},{9,1},{1... | collective-permute-start | bytes 368648 | tf_op jit(solution)/shard_map/ppermute | solution.py:536
  91.4 6.6 %collective-permute-start.22 = (bf16[2,96,768]{2,1,0:T(8,128)(2,1)S(1)}, bf16[2,96,768]{2,1,0:T(8,128)(2,1)S(1)}, u32[]{:S(2)}, u32[]{:S(2)}) collective-permute-start(bf16[2,96,768]{2,1,0:T(8,128)(2,1)S(1)} %sum_others.13.refs_2_.refs_0_), channel_id=1, source_target_pairs={{0,4},{1,9},{2,6},{3,11},{4,0},{5,13},{6,2},{7,15},{8,12},{9,1},{1... | collective-permute-start | bytes 884744 | tf_op jit(solution)/shard_map/ppermute | solution.py:536
  92.3 7.0 %collective-permute-start.21 = (bf16[1,48,640]{2,1,0:T(8,128)(2,1)S(1)}, bf16[1,48,640]{2,1,0:T(8,128)(2,1)S(1)}, u32[]{:S(2)}, u32[]{:S(2)}) collective-permute-start(bf16[1,48,640]{2,1,0:T(8,128)(2,1)S(1)} %sum_qkv.11.refs_2_.refs_0_), channel_id=1, source_target_pairs={{0,16},{1,17},{2,18},{3,19},{4,20},{5,21},{6,22},{7,23},{8,24},{9,... | collective-permute-start | bytes 184328 | tf_op jit(solution)/shard_map/ppermute | solution.py:536
  92.5 7.8 %collective-permute-start.25 = (bf16[4,48,768]{2,1,0:T(8,128)(2,1)S(1)}, bf16[4,48,768]{2,1,0:T(8,128)(2,1)S(1)}, u32[]{:S(2)}, u32[]{:S(2)}) collective-permute-start(bf16[4,48,768]{2,1,0:T(8,128)(2,1)S(1)} %sum_ffn_out.14.refs_2_.refs_0_), channel_id=1, source_target_pairs={{0,8},{1,3},{2,10},{3,1},{4,12},{5,7},{6,14},{7,5},{8,0},{9,11},{1... | collective-permute-start | bytes 884744 | tf_op jit(solution)/shard_map/ppermute | solution.py:536
  98.0 11.4 %collective-permute-start.28 = (bf16[4,96,768]{2,1,0:T(8,128)(2,1)S(1)}, bf16[4,96,768]{2,1,0:T(8,128)(2,1)S(1)}, u32[]{:S(2)}, u32[]{:S(2)}) collective-permute-start(bf16[4,96,768]{2,1,0:T(8,128)(2,1)S(1)} %sum_others.14.refs_2_.refs_0_), channel_id=1, source_target_pairs={{0,2},{1,5},{2,0},{3,7},{4,6},{5,1},{6,4},{7,3},{8,10},{9,13},{10,... | collective-permute-start | bytes 1769480 | tf_op jit(solution)/shard_map/ppermute | solution.py:536
  99.3 4.6 %collective-permute-start.24 = (bf16[1,48,640]{2,1,0:T(8,128)(2,1)S(1)}, bf16[1,48,640]{2,1,0:T(8,128)(2,1)S(1)}, u32[]{:S(2)}, u32[]{:S(2)}) collective-permute-start(bf16[1,48,640]{2,1,0:T(8,128)(2,1)S(1)} %sum_qkv.12.refs_2_.refs_0_), channel_id=1, source_target_pairs={{0,8},{1,3},{2,10},{3,1},{4,12},{5,7},{6,14},{7,5},{8,0},{9,11},{1... | collective-permute-start | bytes 184328 | tf_op jit(solution)/shard_map/ppermute | solution.py:536
  100.4 10.9 %collective-permute-start.29 = (bf16[8,48,768]{2,1,0:T(8,128)(2,1)S(1)}, bf16[8,48,768]{2,1,0:T(8,128)(2,1)S(1)}, u32[]{:S(2)}, u32[]{:S(2)}) collective-permute-start(bf16[8,48,768]{2,1,0:T(8,128)(2,1)S(1)} %sum_ffn_out.15.refs_2_.refs_1_), channel_id=1, source_target_pairs={{0,1},{1,0},{2,3},{3,2},{4,5},{5,4},{6,7},{7,6},{8,9},{9,8},{10,11... | collective-permute-start | bytes 1769480 | tf_op jit(solution)/shard_map/ppermute | solution.py:536
  108.1 6.9 %collective-permute-start.27 = (bf16[4,48,640]{2,1,0:T(8,128)(2,1)S(1)}, bf16[4,48,640]{2,1,0:T(8,128)(2,1)S(1)}, u32[]{:S(2)}, u32[]{:S(2)}) collective-permute-start(bf16[4,48,640]{2,1,0:T(8,128)(2,1)S(1)} %sum_qkv.14.refs_2_.refs_0_), channel_id=1, source_target_pairs={{0,2},{1,5},{2,0},{3,7},{4,6},{5,1},{6,4},{7,3},{8,10},{9,13},{10,... | collective-permute-start | bytes 737288 | tf_op jit(solution)/shard_map/ppermute | solution.py:536
  109.5 7.1 %collective-permute-start.31 = (bf16[8,96,768]{2,1,0:T(8,128)(2,1)S(1)}, bf16[8,96,768]{2,1,0:T(8,128)(2,1)S(1)}, u32[]{:S(2)}, u32[]{:S(2)}) collective-permute-start(bf16[8,96,768]{2,1,0:T(8,128)(2,1)S(1)} %sum_others.15.refs_3_.refs_1_), channel_id=1, source_target_pairs={{0,1},{1,0},{2,3},{3,2},{4,5},{5,4},{6,7},{7,6},{8,9},{9,8},{10,11... | collective-permute-start | bytes 3538952 | tf_op jit(solution)/shard_map/ppermute | solution.py:536
  (20 other events, 93.7 us)

commit v6 on v5

--- a/solution.py
+++ b/solution.py
@@ -286,44 +286,66 @@
 def backward_kernel(
     wo_ref, w1_ref, w2t_ref, n1_ref, inv1_ref, gpr_ref, gsec_ref, gfeed_ref, ag_ref,
     gctx_ref, gfirst_ref, gup, gatt, gvec_ref,
-    w2, nb, gacc,
+    w2, nb, gacc, held,
 ):
     nb[...] = columns(ag_ref)
     for g in range(GROUPS):
         w2[g] = w2t_ref[g].T
     gacc[...] = jnp.zeros_like(gacc)
 
-    def tile(t, carry):
-        tc = pl.ds(pl.multiple_of(t * BLK, BLK), BLK)
-        back, gh = {}, []
+    channels = [slice(g * GD, (g + 1) * GD) for g in range(GROUPS)]
+
+    def at(t):
+        return pl.ds(pl.multiple_of(t * BLK, BLK), BLK)
+
+    def mean(pieces):
+        return sum(jnp.sum(x, 0, keepdims=True) for x in pieces) * (1.0 / D)
+
+    def feed_back(t):
+        tc, back = at(t), {}
 
         def lift(p):
             g, fr = p
-            back[g, fr.start] = nn(w2[g, fr], gfeed_ref[g * GD : (g + 1) * GD, tc])
+            back[g, fr.start] = nn(w2[g, fr], gfeed_ref[channels[g], tc])
 
         def scale(p):
             g, fr = p
             gup[g, fr, tc] = (back.pop((g, fr.start)) * gpr_ref[g, fr, tc].astype(F32)).astype(BF16)
 
         def drop(p):
-            if p[1].stop == GF:
-                gh.append(nn(w1_ref[p[0]], gup[p[0], :, tc]))
-
-        pipelined(PARTS, lift, scale, drop, 2, 3)
-        ghid = gsec_ref[:, tc] + jnp.concatenate(gh, 0)
-        n1 = n1_ref[:, tc]
-        gacc[0] += halves(ghid * n1)
-        gacc[1] += halves(ghid)
-        sc = ghid * nb[...]
-        gfirst = inv1_ref[:, tc] * (
-            sc - jnp.mean(sc, 0, keepdims=True) - n1 * jnp.mean(sc * n1, 0, keepdims=True)
-        )
-        gfirst_ref[:, tc] = gfirst
-        gatt[:, tc] = gfirst.astype(BF16)
-        gctx_ref[:, tc] = nn(wo_ref[...], gatt[:, tc]).astype(BF16)
+            g, fr = p
+            if fr.stop == GF:
+                held[t & 1, channels[g]] = gsec_ref[channels[g], tc] + nn(w1_ref[g], gup[g, :, tc])
+
+        yield from stages(PARTS, lift, scale, drop, 2, 3)
+
+    def norm_back(t):
+        tc, sc = at(t), []
+        for ch in channels:
+            ghid = held[t & 1, ch]
+            gacc[0, ch] += halves(ghid * n1_ref[ch, tc])
+            gacc[1, ch] += halves(ghid)
+            sc.append(ghid * nb[ch])
+            yield
+        first = mean(sc)
+        second = mean([x * n1_ref[ch, tc] for ch, x in zip(channels, sc)])
+        yield
+        for ch, x in zip(channels, sc):
+            gfirst = inv1_ref[:, tc] * (x - first - n1_ref[ch, tc] * second)
+            gfirst_ref[ch, tc] = gfirst
+            gatt[ch, tc] = gfirst.astype(BF16)
+            yield
+        for ch in channels:
+            gctx_ref[ch, tc] = nn(wo_ref[ch, :], gatt[:, tc]).astype(BF16)
+            yield
+
+    def tile(t, carry):
+        weave(feed_back(t + 1), norm_back(t))
         return carry
 
-    lax.fori_loop(0, TOK // BLK, tile, 0)
+    weave(feed_back(0))
+    lax.fori_loop(0, TOK // BLK - 1, tile, 0)
+    weave(norm_back(TOK // BLK - 1))
     for j in range(2):
         gvec_ref[:, j : j + 1] = jnp.sum(gacc[j], 1, keepdims=True)
 
@@ -627,7 +649,10 @@
         [(out_weight, VMEM), (ffn_in_weight, VMEM), (weight2t, VMEM)]
         + [(n1, VMEM), (inv1, VMEM), (gpr, VMEM), (gsec, VMEM), (gfeed, VMEM), (attn_gain, VMEM)],
         [(square, BF16, VMEM), (square, F32, VMEM), (large, BF16, VMEM), (square, BF16, VMEM), ((D, 2), F32, VMEM)],
-        [pltpu.VMEM((GROUPS, GF, GD), BF16), pltpu.VMEM((D, BLK), F32), pltpu.VMEM((2, D, 128), F32)],
+        [
+            pltpu.VMEM((GROUPS, GF, GD), BF16), pltpu.VMEM((D, BLK), F32), pltpu.VMEM((2, D, 128), F32),
+            pltpu.VMEM((2, D, BLK), F32),
+        ],
         12,
     )
     ffn_out.fold()

time: 121 us -> 120 us (level)
  no operation moved by 1% of the time
where the time goes in v6:
time: 120 us
  Pallas kernels  66.5 us (55%)
  starting transfers between devices  30.7 us (26%)
  waiting for transfers between devices  19.3 us (16%)
  local copies, waits for them, and re-layouts  2.7 us (2%)
    pallas_call x40, Pallas kernels, __call__(): pl.pallas_call(kernel if free else lambda *refs: kernel(*refs[:n], *refs[...  66.5 us
    ppermute x32, starting transfers between devices, swap(): return lax.ppermute(x, 'dev', links.pairs(step))  30.7 us
    ppermute x32, waiting for transfers between devices, swap(): return lax.ppermute(x, 'dev', links.pairs(step))  19.3 us
    unnamed x24, local copies, waits for them, and re-layouts  2.62 us
  transfers between devices with their start and end apart: 32, of which 10 were waited for; matrix products, arithmetic and copies ran while one was open for 0% of the time, Pallas kernels for 32%

profile of v6, /device:TPU:1, one launch (start us, length us, event | category | flops | bytes accessed | tf_op | source)
XLA Modules:
  0.0 120.2 jit_solution(7652775393615447110)
XLA Ops:
  4.7 7.5 %attend.1 = (bf16[768,512]{1,0:T(8,128)(2,1)S(1)}, bf16[768,512]{1,0:T(8,128)(2,1)S(1)}, bf16[768,768]{1,0:T(8,128)(2,1)S(1)}, f32[12,1,768]{2,1,0:T(1,128)S(1)}, bf16[2,512,256]{2,1,0:T(8,128)(2,1)S(1)}) custom-call(s32[768]{0:T(1024)S(1)} %copy-done.11, s32[768]{0:T(1024)S(1)} %copy-done.11, bf16[768,768]{1,0:T(8,128)(2,1)S(1)} %collective-permute-done.refs_2_, ...), custom_call_target="tpu_custom_call" | custom-call | flops 8999999488 | bytes 1024 | tf_op jit(solution)/shard_map/attend/pallas_call | solution.py:523
  12.3 18.1 %forward.1 = (bf16[768,768]{1,0:T(8,128)(2,1)}, bf16[768,768]{1,0:T(8,128)(2,1)S(1)}, f32[768,768]{1,0:T(8,128)S(1)}, f32[1,768]{1,0:T(1,128)S(1)}, bf16[4,768,7...) custom-call(s32[5]{0:T(128)S(1)} %stack.23.refs_0_, ...), custom_call_target="tpu_custom_call" | custom-call | flops 19000000512 | bytes 1024 | tf_op jit(solution)/shard_map/forward/pallas_call | solution.py:523
  30.9 5.8 %backward.1 = (bf16[768,768]{1,0:T(8,128)(2,1)S(1)}, f32[768,768]{1,0:T(8,128)S(1)}, bf16[4,768,768]{2,1,0:T(8,128)(2,1)S(1)}, bf16[768,768]{1,0:T(8,128)(2,1)S(1)}, f32[768,2]{1,0:T(8,128)S(1)}) custom-call(bf16[768,768]{1,0:T(8,128)(2,1)S(1)} %copy-done.4, bf16[4,192,768]{2,1,0:T(8,128)(2,1)S(1)} %copy-done.5, bf16[4,192,768]{2,1,0:T(8,128)(2,1)S(1)} %bitcast.9, ...), custom_call_target="tpu_custom_call" | custom-call | flops 6000000000 | bytes 1024 | tf_op jit(solution)/shard_map/backward/pallas_call | solution.py:523
  36.8 2.3 %collective-permute-start.2 = (bf16[4,48,768]{2,1,0:T(8,128)(2,1)S(1)}, bf16[4,48,768]{2,1,0:T(8,128)(2,1)S(1)}, u32[]{:S(2)}, u32[]{:S(2)}) collective-permute-start(bf16[4,48,768]{2,1,0:T(8,128)(2,1)S(1)} %get-tuple-element.111.refs_5_), channel_id=1, source_target_pairs={{0,8},{1,3},{2,10},{3,1},{4,12},{5,7},{6,14},{7,5},{8,0},{9,11},{1... | collective-permute-start | bytes 884744 | tf_op jit(solution)/shard_map/ppermute | solution.py:558
  39.1 3.1 %weights.1 = (bf16[8,96,768]{2,1,0:T(8,128)(2,1)S(1)}, bf16[8,96,768]{2,1,0:T(8,128)(2,1)S(1)}) custom-call(s32[5]{0:T(128)S(1)} %stack.23.refs_0_, bf16[768,768]{1,0:T(8,128)(2,1)S(1)} %get-tuple-element.94.refs_2_.refs_1_, bf16[768,768]{1,0:T(8,128)(2,1)S(1)} %get-tuple-element.112.refs_2_, bf16[4,768,768]{2,1,0:T(8,128)(2,1)S(1)} %get-tuple-element.113.refs_3_, ...), custom_call_target="tpu_custom_call" | custom-call | flops 4000000000 | bytes 1024 | tf_op jit(solution)/shard_map/weights/pallas_call | solution.py:523
  43.1 3.6 %attention_back.4 = (bf16[192,768]{1,0:T(8,128)(2,1)S(1)}, f32[192,768]{1,0:T(8,128)S(1)}, f32[192,768]{1,0:T(8,128)S(1)}, bf16[2,192,512]{2,1,0:T(8,128)(2,1)S(1)}) custom-call(s32[768]{0:T(1024)S(1)} %copy-done.11, bf16[768,768]{1,0:T(8,128)(2,1)S(1)} %get-tuple-element.91.refs_4_.refs_1_, bf16[768,768]{1,0:T(8,128)(2,1)S(1)} %get-tuple-element.92.refs_5_.refs_2_, ...), custom_call_target="tpu_custom_call" | custom-call | flops 4000000000 | bytes 1024 | tf_op jit(solution)/shard_map/attention_back/pallas_call | solution.py:523
  49.4 3.5 %attention_back.5 = (bf16[192,768]{1,0:T(8,128)(2,1)S(1)}, f32[192,768]{1,0:T(8,128)S(1)}, f32[192,768]{1,0:T(8,128)S(1)}, bf16[2,192,512]{2,1,0:T(8,128)(2,1)S(1)}) custom-call(s32[768]{0:T(1024)S(1)} %copy-done.11, bf16[768,768]{1,0:T(8,128)(2,1)S(1)} %get-tuple-element.91.refs_4_.refs_1_, bf16[768,768]{1,0:T(8,128)(2,1)S(1)} %get-tuple-element.92.refs_5_.refs_2_, ...), custom_call_target="tpu_custom_call" | custom-call | flops 4000000000 | bytes 1024 | tf_op jit(solution)/shard_map/attention_back/pallas_call | solution.py:523
  54.7 3.6 %attention_back.6 = (bf16[192,768]{1,0:T(8,128)(2,1)S(1)}, f32[192,768]{1,0:T(8,128)S(1)}, f32[192,768]{1,0:T(8,128)S(1)}, bf16[2,192,512]{2,1,0:T(8,128)(2,1)S(1)}) custom-call(s32[768]{0:T(1024)S(1)} %copy-done.11, bf16[768,768]{1,0:T(8,128)(2,1)S(1)} %get-tuple-element.91.refs_4_.refs_1_, bf16[768,768]{1,0:T(8,128)(2,1)S(1)} %get-tuple-element.92.refs_5_.refs_2_, ...), custom_call_target="tpu_custom_call" | custom-call | flops 4000000000 | bytes 1024 | tf_op jit(solution)/shard_map/attention_back/pallas_call | solution.py:523
  59.3 2.8 %through_qkv.2 = (bf16[768,768]{1,0:T(8,128)(2,1)}, f32[8,48,640]{2,1,0:T(8,128)S(1)}) custom-call(s32[5]{0:T(128)S(1)} %stack.23.refs_0_, bf16[768,768]{1,0:T(8,128)(2,1)S(1)} %get-tuple-element.90.refs_1_, bf16[192,768]{1,0:T(8,128)(2,1)S(1)} %get-tuple-element.128.refs_2_, f32[192,768]{1,0:T(8,128)S(1)} %get-tuple-element.129.refs_3_, ...), custom_call_target="tpu_custom_call" | custom-call | flops 3000000000 | bytes 1024 | tf_op jit(solution)/shard_map/through_qkv/pallas_call | solution.py:523
  62.2 2.4 %collective-permute-start.15 = (bf16[1,48,768]{2,1,0:T(8,128)(2,1)S(1)}, bf16[1,48,768]{2,1,0:T(8,128)(2,1)S(1)}, u32[]{:S(2)}, u32[]{:S(2)}) collective-permute-start(bf16[1,48,768]{2,1,0:T(8,128)(2,1)S(1)} %sum_ffn_out.11.refs_9_.refs_0_), channel_id=1, source_target_pairs={{0,16},{1,17},{2,18},{3,19},{4,20},{5,21},{6,22},{7,23},{8,24},{9,... | collective-permute-start | bytes 221192 | tf_op jit(solution)/shard_map/ppermute | solution.py:558
  64.6 3.6 %attention_back.7 = (bf16[192,768]{1,0:T(8,128)(2,1)S(1)}, f32[192,768]{1,0:T(8,128)S(1)}, f32[192,768]{1,0:T(8,128)S(1)}, bf16[2,192,512]{2,1,0:T(8,128)(2,1)S(1)}) custom-call(s32[768]{0:T(1024)S(1)} %copy-done.11, bf16[768,768]{1,0:T(8,128)(2,1)S(1)} %get-tuple-element.91.refs_4_.refs_1_, bf16[768,768]{1,0:T(8,128)(2,1)S(1)} %get-tuple-element.92.refs_5_.refs_2_, ...), custom_call_target="tpu_custom_call" | custom-call | flops 4000000000 | bytes 1024 | tf_op jit(solution)/shard_map/attention_back/pallas_call | solution.py:523
  68.2 1.8 %collective-permute-start.10 = (bf16[2,192,512]{2,1,0:T(8,128)(2,1)S(1)}, bf16[2,192,512]{2,1,0:T(8,128)(2,1)S(1)}, u32[]{:S(2)}, u32[]{:S(2)}) collective-permute-start(bf16[2,192,512]{2,1,0:T(8,128)(2,1)S(1)} %get-tuple-element.141.refs_2_), channel_id=1, source_target_pairs={{0,1},{1,0},{2,3},{3,2},{4,5},{5,4},{6,7},{7,6},{8,9},{9,8},{10,11... | collective-permute-start | bytes 1179656 | tf_op jit(solution)/shard_map/ppermute | solution.py:558
  71.3 2.9 %through_qkv.3 = (bf16[768,768]{1,0:T(8,128)(2,1)}, f32[8,48,640]{2,1,0:T(8,128)S(1)}, bf16[8,48,640]{2,1,0:T(8,128)(2,1)S(1)}) custom-call(s32[5]{0:T(128)S(1)} %stack.23.refs_0_, bf16[768,768]{1,0:T(8,128)(2,1)S(1)} %get-tuple-element.90.refs_1_, bf16[192,768]{1,0:T(8,128)(2,1)S(1)} %get-tuple-element.123.refs_2_, ...), custom_call_target="tpu_custom_call", output_to_operand_aliasing={{0}: (15, {})} | custom-call | flops 3000000000 | bytes 1024 | tf_op jit(solution)/shard_map/through_qkv/pallas_call | solution.py:523
  77.8 1.7 %collective-permute-done.16.refs_1_ = bf16[1,48,768]{2,1,0:T(8,128)(2,1)S(1)} collective-permute-done((bf16[1,48,768]{2,1,0:T(8,128)(2,1)S(1)}, bf16[1,48,768]{2,1,0:T(8,128)(2,1)S(1)}, u32[]{:S(2)}, u32[]{:S(2)}) %collective-permute-start.16) | collective-permute-done | bytes 73760 | tf_op jit(solution)/shard_map/ppermute | solution.py:558
  79.8 3.4 %collective-permute-done.14.refs_1_ = bf16[4,48,640]{2,1,0:T(8,128)(2,1)S(1)} collective-permute-done((bf16[4,48,640]{2,1,0:T(8,128)(2,1)S(1)}, bf16[4,48,640]{2,1,0:T(8,128)(2,1)S(1)}, u32[]{:S(2)}, u32[]{:S(2)}) %collective-permute-start.14) | collective-permute-done | bytes 245792 | tf_op jit(solution)/shard_map/ppermute | solution.py:558
  83.6 2.8 %collective-permute-done.18.refs_1_ = bf16[1,96,768]{2,1,0:T(8,128)(2,1)S(1)} collective-permute-done((bf16[1,96,768]{2,1,0:T(8,128)(2,1)S(1)}, bf16[1,96,768]{2,1,0:T(8,128)(2,1)S(1)}, u32[]{:S(2)}, u32[]{:S(2)}) %collective-permute-start.18) | collective-permute-done | bytes 147488 | tf_op jit(solution)/shard_map/ppermute | solution.py:558
  92.9 4.5 %collective-permute-done.22.refs_1_ = bf16[2,96,768]{2,1,0:T(8,128)(2,1)S(1)} collective-permute-done((bf16[2,96,768]{2,1,0:T(8,128)(2,1)S(1)}, bf16[2,96,768]{2,1,0:T(8,128)(2,1)S(1)}, u32[]{:S(2)}, u32[]{:S(2)}) %collective-permute-start.22) | collective-permute-done | bytes 294944 | tf_op jit(solution)/shard_map/ppermute | solution.py:558
  99.7 3.6 %collective-permute-start.29 = (bf16[8,48,768]{2,1,0:T(8,128)(2,1)S(1)}, bf16[8,48,768]{2,1,0:T(8,128)(2,1)S(1)}, u32[]{:S(2)}, u32[]{:S(2)}) collective-permute-start(bf16[8,48,768]{2,1,0:T(8,128)(2,1)S(1)} %sum_ffn_out.15.refs_2_.refs_1_), channel_id=1, source_target_pairs={{0,1},{1,0},{2,3},{3,2},{4,5},{5,4},{6,7},{7,6},{8,9},{9,8},{10,11... | collective-permute-start | bytes 1769480 | tf_op jit(solution)/shard_map/ppermute | solution.py:558
  105.3 2.1 %collective-permute-done.26.refs_1_ = bf16[2,48,640]{2,1,0:T(8,128)(2,1)S(1)} collective-permute-done((bf16[2,48,640]{2,1,0:T(8,128)(2,1)S(1)}, bf16[2,48,640]{2,1,0:T(8,128)(2,1)S(1)}, u32[]{:S(2)}, u32[]{:S(2)}) %collective-permute-start.26) | collective-permute-done | bytes 122912 | tf_op jit(solution)/shard_map/ppermute | solution.py:558
  108.8 1.8 %collective-permute-start.31 = (bf16[8,96,768]{2,1,0:T(8,128)(2,1)S(1)}, bf16[8,96,768]{2,1,0:T(8,128)(2,1)S(1)}, u32[]{:S(2)}, u32[]{:S(2)}) collective-permute-start(bf16[8,96,768]{2,1,0:T(8,128)(2,1)S(1)} %sum_others.15.refs_3_.refs_1_), channel_id=1, source_target_pairs={{0,1},{1,0},{2,3},{3,2},{4,5},{5,4},{6,7},{7,6},{8,9},{9,8},{10,11... | collective-permute-start | bytes 3538952 | tf_op jit(solution)/shard_map/ppermute | solution.py:558
  110.6 1.6 %finish.5 = (f32[4,192,768]{2,1,0:T(8,128)}, f32[8,128]{1,0:T(8,128)S(1)}) custom-call(s32[5]{0:T(128)S(1)} %stack.23.refs_0_, bf16[8,48,768]{2,1,0:T(8,128)(2,1)S(1)} %collective-permute-done.29.refs_1_, f32[4,192,768]{2,1,0:T(8,128)} %get-tuple-element.156.refs_2_, bf16[8,96,768]{2,1,0:T(8,128)(2,1)S(1)} %sum_others.15.refs_3_.refs_1_), custom_call_target="tpu_custom_call", output_to_operand_aliasing={{0}: (2, {})} | custom-call | flops 3000000000 | bytes 1024 | tf_op jit(solution)/shard_map/finish/pallas_call | solution.py:523
  112.2 2.1 %finish.6 = (f32[4,192,768]{2,1,0:T(8,128)}, f32[4,192,768]{2,1,0:T(8,128)}, f32[8,128]{1,0:T(8,128)S(1)}) custom-call(s32[5]{0:T(128)S(1)} %stack.23.refs_0_, bf16[8,96,768]{2,1,0:T(8,128)(2,1)S(1)} %sum_others.15.refs_3_.refs_1_, f32[8,128]{1,0:T(8,128)S(1)} %get-tuple-element.157.refs_2_), custom_call_target="tpu_custom_call" | custom-call | flops 3000000000 | bytes 1024 | tf_op jit(solution)/shard_map/finish/pallas_call | solution.py:523
  115.9 2.1 %finish.7 = (f32[4,192,768]{2,1,0:T(8,128)}, f32[4,192,768]{2,1,0:T(8,128)}, f32[8,128]{1,0:T(8,128)S(1)}) custom-call(s32[5]{0:T(128)S(1)} %stack.23.refs_0_, bf16[8,96,768]{2,1,0:T(8,128)(2,1)S(1)} %collective-permute-done.31.refs_1_, f32[4,192,768]{2,1,0:T(8,128)} %get-tuple-element.159.refs_2_, ...), custom_call_target="tpu_custom_call", output_to_operand_aliasing={{0}: (2, {}), {1}: (3, {})} | custom-call | flops 3000000000 | bytes 1024 | tf_op jit(solution)/shard_map/finish/pallas_call | solution.py:523
  118.0 2.2 %finish_qkv.1 = (f32[3,4,192,192]{3,2,1,0:T(8,128)}, f32[768]{0:T(1024)}, f32[768]{0:T(1024)}, f32[768]{0:T(1024)}, f32[768]{0:T(1024)}) custom-call(s32[5]{0:T(128)S(1)} %stack.23.refs_0_, bf16[8,48,640]{2,1,0:T(8,128)(2,1)S(1)} %sum_qkv.15.refs_4_.refs_1_, bf16[8,48,640]{2,1,0:T(8,128)(2,1)S(1)} %collective-permute-done.30.refs_2_, ...), custom_call_target="tpu_custom_call" | custom-call | flops 3000000000 | bytes 1024 | tf_op jit(solution)/shard_map/finish_qkv/pallas_call | solution.py:523
  (105 shorter events, 30.5 us)
Async XLA Ops:
  30.4 6.2 %collective-permute-start.1 = (bf16[8,48,768]{2,1,0:T(8,128)(2,1)S(1)}, bf16[8,48,768]{2,1,0:T(8,128)(2,1)S(1)}, u32[]{:S(2)}, u32[]{:S(2)}) collective-permute-start(bf16[8,48,768]{2,1,0:T(8,128)(2,1)S(1)} %get-tuple-element.108), channel_id=1, source_target_pairs={{0,1},{1,0},{2,3},{3,2},{4,5},{5,4},{6,7},{7,6},{8,9},{9,8},{10,11... | collective-permute-start | bytes 1769480 | tf_op jit(solution)/shard_map/ppermute | solution.py:558
  36.8 10.0 %collective-permute-start.2 = (bf16[4,48,768]{2,1,0:T(8,128)(2,1)S(1)}, bf16[4,48,768]{2,1,0:T(8,128)(2,1)S(1)}, u32[]{:S(2)}, u32[]{:S(2)}) collective-permute-start(bf16[4,48,768]{2,1,0:T(8,128)(2,1)S(1)} %get-tuple-element.111.refs_5_), channel_id=1, source_target_pairs={{0,8},{1,3},{2,10},{3,1},{4,12},{5,7},{6,14},{7,5},{8,0},{9,11},{1... | collective-permute-start | bytes 884744 | tf_op jit(solution)/shard_map/ppermute | solution.py:558
  42.2 5.6 %collective-permute-start.4 = (bf16[8,96,768]{2,1,0:T(8,128)(2,1)S(1)}, bf16[8,96,768]{2,1,0:T(8,128)(2,1)S(1)}, u32[]{:S(2)}, u32[]{:S(2)}) collective-permute-start(bf16[8,96,768]{2,1,0:T(8,128)(2,1)S(1)} %get-tuple-element.115.refs_9_), channel_id=1, source_target_pairs={{0,1},{1,0},{2,3},{3,2},{4,5},{5,4},{6,7},{7,6},{8,9},{9,8},{10,11... | collective-permute-start | bytes 3538952 | tf_op jit(solution)/shard_map/ppermute | solution.py:558
  46.7 12.6 %collective-permute-start.7 = (bf16[2,192,512]{2,1,0:T(8,128)(2,1)S(1)}, bf16[2,192,512]{2,1,0:T(8,128)(2,1)S(1)}, u32[]{:S(2)}, u32[]{:S(2)}) collective-permute-start(bf16[2,192,512]{2,1,0:T(8,128)(2,1)S(1)} %get-tuple-element.116.refs_2_), channel_id=1, source_target_pairs={{0,1},{1,0},{2,3},{3,2},{4,5},{5,4},{6,7},{7,6},{8,9},{9,8},{10,11... | collective-permute-start | bytes 1179656 | tf_op jit(solution)/shard_map/ppermute | solution.py:558
  46.9 6.5 %collective-permute-start.3 = (bf16[2,48,768]{2,1,0:T(8,128)(2,1)S(1)}, bf16[2,48,768]{2,1,0:T(8,128)(2,1)S(1)}, u32[]{:S(2)}, u32[]{:S(2)}) collective-permute-start(bf16[2,48,768]{2,1,0:T(8,128)(2,1)S(1)} %get-tuple-element.118.refs_2_), channel_id=1, source_target_pairs={{0,2},{1,9},{2,0},{3,11},{4,6},{5,13},{6,4},{7,15},{8,10},{9,1},{1... | collective-permute-start | bytes 442376 | tf_op jit(solution)/shard_map/ppermute | solution.py:558
  48.1 10.5 %collective-permute-start.9 = (bf16[4,96,768]{2,1,0:T(8,128)(2,1)S(1)}, bf16[4,96,768]{2,1,0:T(8,128)(2,1)S(1)}, u32[]{:S(2)}, u32[]{:S(2)}) collective-permute-start(bf16[4,96,768]{2,1,0:T(8,128)(2,1)S(1)} %get-tuple-element.120.refs_9_), channel_id=1, source_target_pairs={{0,2},{1,5},{2,0},{3,7},{4,6},{5,1},{6,4},{7,3},{8,10},{9,13},{10,... | collective-permute-start | bytes 1769480 | tf_op jit(solution)/shard_map/ppermute | solution.py:558
  53.0 6.4 %collective-permute-start.8 = (bf16[2,192,512]{2,1,0:T(8,128)(2,1)S(1)}, bf16[2,192,512]{2,1,0:T(8,128)(2,1)S(1)}, u32[]{:S(2)}, u32[]{:S(2)}) collective-permute-start(bf16[2,192,512]{2,1,0:T(8,128)(2,1)S(1)} %get-tuple-element.121.refs_2_), channel_id=1, source_target_pairs={{0,1},{1,0},{2,3},{3,2},{4,5},{5,4},{6,7},{7,6},{8,9},{9,8},{10,11... | collective-permute-start | bytes 1179656 | tf_op jit(solution)/shard_map/ppermute | solution.py:558
  53.4 8.8 %collective-permute-start.6 = (bf16[1,48,768]{2,1,0:T(8,128)(2,1)S(1)}, bf16[1,48,768]{2,1,0:T(8,128)(2,1)S(1)}, u32[]{:S(2)}, u32[]{:S(2)}) collective-permute-start(bf16[1,48,768]{2,1,0:T(8,128)(2,1)S(1)} %get-tuple-element.122.refs_9_), channel_id=1, source_target_pairs={{0,4},{1,5},{2,6},{3,7},{4,0},{5,1},{6,2},{7,3},{8,12},{9,13},{10,... | collective-permute-start | bytes 221192 | tf_op jit(solution)/shard_map/ppermute | solution.py:558
  58.3 12.8 %collective-permute-start.5 = (bf16[2,192,512]{2,1,0:T(8,128)(2,1)S(1)}, bf16[2,192,512]{2,1,0:T(8,128)(2,1)S(1)}, u32[]{:S(2)}, u32[]{:S(2)}) collective-permute-start(bf16[2,192,512]{2,1,0:T(8,128)(2,1)S(1)} %get-tuple-element.126.refs_2_), channel_id=1, source_target_pairs={{0,1},{1,0},{2,3},{3,2},{4,5},{5,4},{6,7},{7,6},{8,9},{9,8},{10,11... | collective-permute-start | bytes 1179656 | tf_op jit(solution)/shard_map/ppermute | solution.py:558
  58.8 11.2 %collective-permute-start.11 = (bf16[2,96,768]{2,1,0:T(8,128)(2,1)S(1)}, bf16[2,96,768]{2,1,0:T(8,128)(2,1)S(1)}, u32[]{:S(2)}, u32[]{:S(2)}) collective-permute-start(bf16[2,96,768]{2,1,0:T(8,128)(2,1)S(1)} %get-tuple-element.136.refs_14_), channel_id=1, source_target_pairs={{0,4},{1,9},{2,6},{3,11},{4,0},{5,13},{6,2},{7,15},{8,12},{9,1},{1... | collective-permute-start | bytes 884744 | tf_op jit(solution)/shard_map/ppermute | solution.py:558
  62.2 14.0 %collective-permute-start.15 = (bf16[1,48,768]{2,1,0:T(8,128)(2,1)S(1)}, bf16[1,48,768]{2,1,0:T(8,128)(2,1)S(1)}, u32[]{:S(2)}, u32[]{:S(2)}) collective-permute-start(bf16[1,48,768]{2,1,0:T(8,128)(2,1)S(1)} %sum_ffn_out.11.refs_9_.refs_0_), channel_id=1, source_target_pairs={{0,16},{1,17},{2,18},{3,19},{4,20},{5,21},{6,22},{7,23},{8,24},{9,... | collective-permute-start | bytes 221192 | tf_op jit(solution)/shard_map/ppermute | solution.py:558
  70.1 4.5 %collective-permute-start.13 = (bf16[1,96,768]{2,1,0:T(8,128)(2,1)S(1)}, bf16[1,96,768]{2,1,0:T(8,128)(2,1)S(1)}, u32[]{:S(2)}, u32[]{:S(2)}) collective-permute-start(bf16[1,96,768]{2,1,0:T(8,128)(2,1)S(1)} %get-tuple-element.144.refs_16_), channel_id=1, source_target_pairs={{0,8},{1,3},{2,10},{3,1},{4,12},{5,7},{6,14},{7,5},{8,0},{9,11},{1... | collective-permute-start | bytes 442376 | tf_op jit(solution)/shard_map/ppermute | solution.py:558
  76.5 9.8 %collective-permute-start.18 = (bf16[1,96,768]{2,1,0:T(8,128)(2,1)S(1)}, bf16[1,96,768]{2,1,0:T(8,128)(2,1)S(1)}, u32[]{:S(2)}, u32[]{:S(2)}) collective-permute-start(bf16[1,96,768]{2,1,0:T(8,128)(2,1)S(1)} %sum_others.11.refs_2_.refs_0_), channel_id=1, source_target_pairs={{0,16},{1,17},{2,18},{3,19},{4,20},{5,21},{6,22},{7,23},{8,24},{9,... | collective-permute-start | bytes 442376 | tf_op jit(solution)/shard_map/ppermute | solution.py:558
  76.5 6.7 %collective-permute-start.14 = (bf16[4,48,640]{2,1,0:T(8,128)(2,1)S(1)}, bf16[4,48,640]{2,1,0:T(8,128)(2,1)S(1)}, u32[]{:S(2)}, u32[]{:S(2)}) collective-permute-start(bf16[4,48,640]{2,1,0:T(8,128)(2,1)S(1)} %get-tuple-element.150.refs_2_), channel_id=1, source_target_pairs={{0,2},{1,5},{2,0},{3,7},{4,6},{5,1},{6,4},{7,3},{8,10},{9,13},{10,... | collective-permute-start | bytes 737288 | tf_op jit(solution)/shard_map/ppermute | solution.py:558
  79.5 12.3 %collective-permute-start.23 = (bf16[2,48,768]{2,1,0:T(8,128)(2,1)S(1)}, bf16[2,48,768]{2,1,0:T(8,128)(2,1)S(1)}, u32[]{:S(2)}, u32[]{:S(2)}) collective-permute-start(bf16[2,48,768]{2,1,0:T(8,128)(2,1)S(1)} %sum_ffn_out.13.refs_2_.refs_0_), channel_id=1, source_target_pairs={{0,2},{1,9},{2,0},{3,11},{4,6},{5,13},{6,4},{7,15},{8,10},{9,1},{1... | collective-permute-start | bytes 442376 | tf_op jit(solution)/shard_map/ppermute | solution.py:558
  83.2 5.0 %collective-permute-start.17 = (bf16[2,48,640]{2,1,0:T(8,128)(2,1)S(1)}, bf16[2,48,640]{2,1,0:T(8,128)(2,1)S(1)}, u32[]{:S(2)}, u32[]{:S(2)}) collective-permute-start(bf16[2,48,640]{2,1,0:T(8,128)(2,1)S(1)} %get-tuple-element.152.refs_2_), channel_id=1, source_target_pairs={{0,4},{1,9},{2,6},{3,11},{4,0},{5,13},{6,2},{7,15},{8,12},{9,1},{1... | collective-permute-start | bytes 368648 | tf_op jit(solution)/shard_map/ppermute | solution.py:558
  90.7 6.6 %collective-permute-start.22 = (bf16[2,96,768]{2,1,0:T(8,128)(2,1)S(1)}, bf16[2,96,768]{2,1,0:T(8,128)(2,1)S(1)}, u32[]{:S(2)}, u32[]{:S(2)}) collective-permute-start(bf16[2,96,768]{2,1,0:T(8,128)(2,1)S(1)} %sum_others.13.refs_2_.refs_0_), channel_id=1, source_target_pairs={{0,4},{1,9},{2,6},{3,11},{4,0},{5,13},{6,2},{7,15},{8,12},{9,1},{1... | collective-permute-start | bytes 884744 | tf_op jit(solution)/shard_map/ppermute | solution.py:558
  91.7 7.0 %collective-permute-start.21 = (bf16[1,48,640]{2,1,0:T(8,128)(2,1)S(1)}, bf16[1,48,640]{2,1,0:T(8,128)(2,1)S(1)}, u32[]{:S(2)}, u32[]{:S(2)}) collective-permute-start(bf16[1,48,640]{2,1,0:T(8,128)(2,1)S(1)} %sum_qkv.11.refs_2_.refs_0_), channel_id=1, source_target_pairs={{0,16},{1,17},{2,18},{3,19},{4,20},{5,21},{6,22},{7,23},{8,24},{9,... | collective-permute-start | bytes 184328 | tf_op jit(solution)/shard_map/ppermute | solution.py:558
  91.8 7.9 %collective-permute-start.25 = (bf16[4,48,768]{2,1,0:T(8,128)(2,1)S(1)}, bf16[4,48,768]{2,1,0:T(8,128)(2,1)S(1)}, u32[]{:S(2)}, u32[]{:S(2)}) collective-permute-start(bf16[4,48,768]{2,1,0:T(8,128)(2,1)S(1)} %sum_ffn_out.14.refs_2_.refs_0_), channel_id=1, source_target_pairs={{0,8},{1,3},{2,10},{3,1},{4,12},{5,7},{6,14},{7,5},{8,0},{9,11},{1... | collective-permute-start | bytes 884744 | tf_op jit(solution)/shard_map/ppermute | solution.py:558
  97.4 11.4 %collective-permute-start.28 = (bf16[4,96,768]{2,1,0:T(8,128)(2,1)S(1)}, bf16[4,96,768]{2,1,0:T(8,128)(2,1)S(1)}, u32[]{:S(2)}, u32[]{:S(2)}) collective-permute-start(bf16[4,96,768]{2,1,0:T(8,128)(2,1)S(1)} %sum_others.14.refs_2_.refs_0_), channel_id=1, source_target_pairs={{0,2},{1,5},{2,0},{3,7},{4,6},{5,1},{6,4},{7,3},{8,10},{9,13},{10,... | collective-permute-start | bytes 1769480 | tf_op jit(solution)/shard_map/ppermute | solution.py:558
  98.7 4.6 %collective-permute-start.24 = (bf16[1,48,640]{2,1,0:T(8,128)(2,1)S(1)}, bf16[1,48,640]{2,1,0:T(8,128)(2,1)S(1)}, u32[]{:S(2)}, u32[]{:S(2)}) collective-permute-start(bf16[1,48,640]{2,1,0:T(8,128)(2,1)S(1)} %sum_qkv.12.refs_2_.refs_0_), channel_id=1, source_target_pairs={{0,8},{1,3},{2,10},{3,1},{4,12},{5,7},{6,14},{7,5},{8,0},{9,11},{1... | collective-permute-start | bytes 184328 | tf_op jit(solution)/shard_map/ppermute | solution.py:558
  99.7 10.9 %collective-permute-start.29 = (bf16[8,48,768]{2,1,0:T(8,128)(2,1)S(1)}, bf16[8,48,768]{2,1,0:T(8,128)(2,1)S(1)}, u32[]{:S(2)}, u32[]{:S(2)}) collective-permute-start(bf16[8,48,768]{2,1,0:T(8,128)(2,1)S(1)} %sum_ffn_out.15.refs_2_.refs_1_), channel_id=1, source_target_pairs={{0,1},{1,0},{2,3},{3,2},{4,5},{5,4},{6,7},{7,6},{8,9},{9,8},{10,11... | collective-permute-start | bytes 1769480 | tf_op jit(solution)/shard_map/ppermute | solution.py:558
  107.4 6.9 %collective-permute-start.27 = (bf16[4,48,640]{2,1,0:T(8,128)(2,1)S(1)}, bf16[4,48,640]{2,1,0:T(8,128)(2,1)S(1)}, u32[]{:S(2)}, u32[]{:S(2)}) collective-permute-start(bf16[4,48,640]{2,1,0:T(8,128)(2,1)S(1)} %sum_qkv.14.refs_2_.refs_0_), channel_id=1, source_target_pairs={{0,2},{1,5},{2,0},{3,7},{4,6},{5,1},{6,4},{7,3},{8,10},{9,13},{10,... | collective-permute-start | bytes 737288 | tf_op jit(solution)/shard_map/ppermute | solution.py:558
  108.8 7.1 %collective-permute-start.31 = (bf16[8,96,768]{2,1,0:T(8,128)(2,1)S(1)}, bf16[8,96,768]{2,1,0:T(8,128)(2,1)S(1)}, u32[]{:S(2)}, u32[]{:S(2)}) collective-permute-start(bf16[8,96,768]{2,1,0:T(8,128)(2,1)S(1)} %sum_others.15.refs_3_.refs_1_), channel_id=1, source_target_pairs={{0,1},{1,0},{2,3},{3,2},{4,5},{5,4},{6,7},{7,6},{8,9},{9,8},{10,11... | collective-permute-start | bytes 3538952 | tf_op jit(solution)/shard_map/ppermute | solution.py:558
  (20 other events, 93.6 us)

commit v7 on v6

--- a/solution.py
+++ b/solution.py
@@ -727,9 +727,9 @@
     parts += [attention_back(2)]
     others.fold()
     first = through(0, parts[:2], None)
-    ffn_out.meet()
     parts += [attention_back(3)]
     others.fold()
+    ffn_out.meet()
     grad_input, keep, send = through(1, parts[2:], first)
     others.meet()
     qkv = Total(run, links, "sum_qkv", keep, swap(send, links, -1))

time: 120 us -> 120 us (level)
  starting transfers between devices: 30.7 us -> 28.2 us
  waiting for transfers between devices: 19.3 us -> 20.8 us
    ppermute x32, starting transfers between devices: 30.7 us -> 28.2 us  [swap(): return lax.ppermute(x, 'dev', links.pairs(step))]
    ppermute x32, waiting for transfers between devices: 19.3 us -> 20.8 us  [swap(): return lax.ppermute(x, 'dev', links.pairs(step))]
  transfers between devices with their start and end apart: 32 -> 32, of which waited for: 10 -> 9; matrix products, arithmetic and copies ran while one was open for 0% -> 0% of each run, Pallas kernels for 32% -> 32%
where the time goes in v7:
time: 120 us
  Pallas kernels  66.9 us (56%)
  starting transfers between devices  28.2 us (24%)
  waiting for transfers between devices  20.8 us (17%)
  local copies, waits for them, and re-layouts  2.7 us (2%)
    pallas_call x40, Pallas kernels, __call__(): pl.pallas_call(kernel if free else lambda *refs: kernel(*refs[:n], *refs[...  66.9 us
    ppermute x32, starting transfers between devices, swap(): return lax.ppermute(x, 'dev', links.pairs(step))  28.2 us
    ppermute x32, waiting for transfers between devices, swap(): return lax.ppermute(x, 'dev', links.pairs(step))  20.8 us
    unnamed x24, local copies, waits for them, and re-layouts  2.62 us
  transfers between devices with their start and end apart: 32, of which 9 were waited for; matrix products, arithmetic and copies ran while one was open for 0% of the time, Pallas kernels for 32%

profile of v7, /device:TPU:1, one launch (start us, length us, event | category | flops | bytes accessed | tf_op | source)
XLA Modules:
  0.0 119.6 jit_solution(14977184059320001272)
XLA Ops:
  4.7 7.7 %attend.1 = (bf16[768,512]{1,0:T(8,128)(2,1)S(1)}, bf16[768,512]{1,0:T(8,128)(2,1)S(1)}, bf16[768,768]{1,0:T(8,128)(2,1)S(1)}, f32[12,1,768]{2,1,0:T(1,128)S(1)}, bf16[2,512,256]{2,1,0:T(8,128)(2,1)S(1)}) custom-call(s32[768]{0:T(1024)S(1)} %copy-done.11, s32[768]{0:T(1024)S(1)} %copy-done.11, bf16[768,768]{1,0:T(8,128)(2,1)S(1)} %collective-permute-done.refs_2_, ...), custom_call_target="tpu_custom_call" | custom-call | flops 8999999488 | bytes 1024 | tf_op jit(solution)/shard_map/attend/pallas_call | solution.py:523
  12.5 18.1 %forward.1 = (bf16[768,768]{1,0:T(8,128)(2,1)}, bf16[768,768]{1,0:T(8,128)(2,1)S(1)}, f32[768,768]{1,0:T(8,128)S(1)}, f32[1,768]{1,0:T(1,128)S(1)}, bf16[4,768,7...) custom-call(s32[5]{0:T(128)S(1)} %stack.23.refs_0_, ...), custom_call_target="tpu_custom_call" | custom-call | flops 19000000512 | bytes 1024 | tf_op jit(solution)/shard_map/forward/pallas_call | solution.py:523
  31.1 5.8 %backward.1 = (bf16[768,768]{1,0:T(8,128)(2,1)S(1)}, f32[768,768]{1,0:T(8,128)S(1)}, bf16[4,768,768]{2,1,0:T(8,128)(2,1)S(1)}, bf16[768,768]{1,0:T(8,128)(2,1)S(1)}, f32[768,2]{1,0:T(8,128)S(1)}) custom-call(bf16[768,768]{1,0:T(8,128)(2,1)S(1)} %copy-done.4, bf16[4,192,768]{2,1,0:T(8,128)(2,1)S(1)} %copy-done.5, bf16[4,192,768]{2,1,0:T(8,128)(2,1)S(1)} %bitcast.9, ...), custom_call_target="tpu_custom_call" | custom-call | flops 6000000000 | bytes 1024 | tf_op jit(solution)/shard_map/backward/pallas_call | solution.py:523
  37.0 2.3 %collective-permute-start.2 = (bf16[4,48,768]{2,1,0:T(8,128)(2,1)S(1)}, bf16[4,48,768]{2,1,0:T(8,128)(2,1)S(1)}, u32[]{:S(2)}, u32[]{:S(2)}) collective-permute-start(bf16[4,48,768]{2,1,0:T(8,128)(2,1)S(1)} %get-tuple-element.111.refs_5_), channel_id=1, source_target_pairs={{0,8},{1,3},{2,10},{3,1},{4,12},{5,7},{6,14},{7,5},{8,0},{9,11},{1... | collective-permute-start | bytes 884744 | tf_op jit(solution)/shard_map/ppermute | solution.py:558
  39.3 3.1 %weights.1 = (bf16[8,96,768]{2,1,0:T(8,128)(2,1)S(1)}, bf16[8,96,768]{2,1,0:T(8,128)(2,1)S(1)}) custom-call(s32[5]{0:T(128)S(1)} %stack.23.refs_0_, bf16[768,768]{1,0:T(8,128)(2,1)S(1)} %get-tuple-element.94.refs_2_.refs_1_, bf16[768,768]{1,0:T(8,128)(2,1)S(1)} %get-tuple-element.112.refs_2_, bf16[4,768,768]{2,1,0:T(8,128)(2,1)S(1)} %get-tuple-element.113.refs_3_, ...), custom_call_target="tpu_custom_call" | custom-call | flops 4000000000 | bytes 1024 | tf_op jit(solution)/shard_map/weights/pallas_call | solution.py:523
  43.3 3.6 %attention_back.4 = (bf16[192,768]{1,0:T(8,128)(2,1)S(1)}, f32[192,768]{1,0:T(8,128)S(1)}, f32[192,768]{1,0:T(8,128)S(1)}, bf16[2,192,512]{2,1,0:T(8,128)(2,1)S(1)}) custom-call(s32[768]{0:T(1024)S(1)} %copy-done.11, bf16[768,768]{1,0:T(8,128)(2,1)S(1)} %get-tuple-element.91.refs_4_.refs_1_, bf16[768,768]{1,0:T(8,128)(2,1)S(1)} %get-tuple-element.92.refs_5_.refs_2_, ...), custom_call_target="tpu_custom_call" | custom-call | flops 4000000000 | bytes 1024 | tf_op jit(solution)/shard_map/attention_back/pallas_call | solution.py:523
  49.7 3.6 %attention_back.5 = (bf16[192,768]{1,0:T(8,128)(2,1)S(1)}, f32[192,768]{1,0:T(8,128)S(1)}, f32[192,768]{1,0:T(8,128)S(1)}, bf16[2,192,512]{2,1,0:T(8,128)(2,1)S(1)}) custom-call(s32[768]{0:T(1024)S(1)} %copy-done.11, bf16[768,768]{1,0:T(8,128)(2,1)S(1)} %get-tuple-element.91.refs_4_.refs_1_, bf16[768,768]{1,0:T(8,128)(2,1)S(1)} %get-tuple-element.92.refs_5_.refs_2_, ...), custom_call_target="tpu_custom_call" | custom-call | flops 4000000000 | bytes 1024 | tf_op jit(solution)/shard_map/attention_back/pallas_call | solution.py:523
  55.0 3.6 %attention_back.6 = (bf16[192,768]{1,0:T(8,128)(2,1)S(1)}, f32[192,768]{1,0:T(8,128)S(1)}, f32[192,768]{1,0:T(8,128)S(1)}, bf16[2,192,512]{2,1,0:T(8,128)(2,1)S(1)}) custom-call(s32[768]{0:T(1024)S(1)} %copy-done.11, bf16[768,768]{1,0:T(8,128)(2,1)S(1)} %get-tuple-element.91.refs_4_.refs_1_, bf16[768,768]{1,0:T(8,128)(2,1)S(1)} %get-tuple-element.92.refs_5_.refs_2_, ...), custom_call_target="tpu_custom_call" | custom-call | flops 4000000000 | bytes 1024 | tf_op jit(solution)/shard_map/attention_back/pallas_call | solution.py:523
  59.6 2.8 %through_qkv.2 = (bf16[768,768]{1,0:T(8,128)(2,1)}, f32[8,48,640]{2,1,0:T(8,128)S(1)}) custom-call(s32[5]{0:T(128)S(1)} %stack.23.refs_0_, bf16[768,768]{1,0:T(8,128)(2,1)S(1)} %get-tuple-element.90.refs_1_, bf16[192,768]{1,0:T(8,128)(2,1)S(1)} %get-tuple-element.127.refs_2_, f32[192,768]{1,0:T(8,128)S(1)} %get-tuple-element.128.refs_3_, ...), custom_call_target="tpu_custom_call" | custom-call | flops 3000000000 | bytes 1024 | tf_op jit(solution)/shard_map/through_qkv/pallas_call | solution.py:523
  62.5 3.6 %attention_back.7 = (bf16[192,768]{1,0:T(8,128)(2,1)S(1)}, f32[192,768]{1,0:T(8,128)S(1)}, f32[192,768]{1,0:T(8,128)S(1)}, bf16[2,192,512]{2,1,0:T(8,128)(2,1)S(1)}) custom-call(s32[768]{0:T(1024)S(1)} %copy-done.11, bf16[768,768]{1,0:T(8,128)(2,1)S(1)} %get-tuple-element.91.refs_4_.refs_1_, bf16[768,768]{1,0:T(8,128)(2,1)S(1)} %get-tuple-element.92.refs_5_.refs_2_, ...), custom_call_target="tpu_custom_call" | custom-call | flops 4000000000 | bytes 1024 | tf_op jit(solution)/shard_map/attention_back/pallas_call | solution.py:523
  68.6 2.4 %collective-permute-start.15 = (bf16[1,48,768]{2,1,0:T(8,128)(2,1)S(1)}, bf16[1,48,768]{2,1,0:T(8,128)(2,1)S(1)}, u32[]{:S(2)}, u32[]{:S(2)}) collective-permute-start(bf16[1,48,768]{2,1,0:T(8,128)(2,1)S(1)} %sum_ffn_out.11.refs_16_.refs_0_), channel_id=1, source_target_pairs={{0,16},{1,17},{2,18},{3,19},{4,20},{5,21},{6,22},{7,23},{8,24},{9,... | collective-permute-start | bytes 221192 | tf_op jit(solution)/shard_map/ppermute | solution.py:558
  71.0 2.9 %through_qkv.3 = (bf16[768,768]{1,0:T(8,128)(2,1)}, f32[8,48,640]{2,1,0:T(8,128)S(1)}, bf16[8,48,640]{2,1,0:T(8,128)(2,1)S(1)}) custom-call(s32[5]{0:T(128)S(1)} %stack.23.refs_0_, bf16[768,768]{1,0:T(8,128)(2,1)S(1)} %get-tuple-element.90.refs_1_, bf16[192,768]{1,0:T(8,128)(2,1)S(1)} %get-tuple-element.123.refs_2_, ...), custom_call_target="tpu_custom_call", output_to_operand_aliasing={{0}: (15, {})} | custom-call | flops 3000000000 | bytes 1024 | tf_op jit(solution)/shard_map/through_qkv/pallas_call | solution.py:523
  74.0 1.8 %collective-permute-done.12.refs_1_ = bf16[8,48,640]{2,1,0:T(8,128)(2,1)S(1)} collective-permute-done((bf16[8,48,640]{2,1,0:T(8,128)(2,1)S(1)}, bf16[8,48,640]{2,1,0:T(8,128)(2,1)S(1)}, u32[]{:S(2)}, u32[]{:S(2)}) %collective-permute-start.12) | collective-permute-done | bytes 491552 | tf_op jit(solution)/shard_map/ppermute | solution.py:558
  77.7 2.0 %collective-permute-done.16.refs_1_ = bf16[1,48,768]{2,1,0:T(8,128)(2,1)S(1)} collective-permute-done((bf16[1,48,768]{2,1,0:T(8,128)(2,1)S(1)}, bf16[1,48,768]{2,1,0:T(8,128)(2,1)S(1)}, u32[]{:S(2)}, u32[]{:S(2)}) %collective-permute-start.16) | collective-permute-done | bytes 73760 | tf_op jit(solution)/shard_map/ppermute | solution.py:558
  80.0 2.9 %collective-permute-done.14.refs_1_ = bf16[4,48,640]{2,1,0:T(8,128)(2,1)S(1)} collective-permute-done((bf16[4,48,640]{2,1,0:T(8,128)(2,1)S(1)}, bf16[4,48,640]{2,1,0:T(8,128)(2,1)S(1)}, u32[]{:S(2)}, u32[]{:S(2)}) %collective-permute-start.14) | collective-permute-done | bytes 245792 | tf_op jit(solution)/shard_map/ppermute | solution.py:558
  83.8 2.1 %collective-permute-done.18.refs_1_ = bf16[1,96,768]{2,1,0:T(8,128)(2,1)S(1)} collective-permute-done((bf16[1,96,768]{2,1,0:T(8,128)(2,1)S(1)}, bf16[1,96,768]{2,1,0:T(8,128)(2,1)S(1)}, u32[]{:S(2)}, u32[]{:S(2)}) %collective-permute-start.18) | collective-permute-done | bytes 147488 | tf_op jit(solution)/shard_map/ppermute | solution.py:558
  86.0 2.2 %collective-permute-done.17.refs_1_ = bf16[2,48,640]{2,1,0:T(8,128)(2,1)S(1)} collective-permute-done((bf16[2,48,640]{2,1,0:T(8,128)(2,1)S(1)}, bf16[2,48,640]{2,1,0:T(8,128)(2,1)S(1)}, u32[]{:S(2)}, u32[]{:S(2)}) %collective-permute-start.17) | collective-permute-done | bytes 122912 | tf_op jit(solution)/shard_map/ppermute | solution.py:558
  88.3 2.0 %collective-permute-done.20.refs_1_ = bf16[1,96,768]{2,1,0:T(8,128)(2,1)S(1)} collective-permute-done((bf16[1,96,768]{2,1,0:T(8,128)(2,1)S(1)}, bf16[1,96,768]{2,1,0:T(8,128)(2,1)S(1)}, u32[]{:S(2)}, u32[]{:S(2)}) %collective-permute-start.20) | collective-permute-done | bytes 147488 | tf_op jit(solution)/shard_map/ppermute | solution.py:558
  92.0 4.9 %collective-permute-done.22.refs_1_ = bf16[2,96,768]{2,1,0:T(8,128)(2,1)S(1)} collective-permute-done((bf16[2,96,768]{2,1,0:T(8,128)(2,1)S(1)}, bf16[2,96,768]{2,1,0:T(8,128)(2,1)S(1)}, u32[]{:S(2)}, u32[]{:S(2)}) %collective-permute-start.22) | collective-permute-done | bytes 294944 | tf_op jit(solution)/shard_map/ppermute | solution.py:558
  98.6 4.3 %collective-permute-start.29 = (bf16[8,48,768]{2,1,0:T(8,128)(2,1)S(1)}, bf16[8,48,768]{2,1,0:T(8,128)(2,1)S(1)}, u32[]{:S(2)}, u32[]{:S(2)}) collective-permute-start(bf16[8,48,768]{2,1,0:T(8,128)(2,1)S(1)} %sum_ffn_out.15.refs_2_.refs_1_), channel_id=1, source_target_pairs={{0,1},{1,0},{2,3},{3,2},{4,5},{5,4},{6,7},{7,6},{8,9},{9,8},{10,11... | collective-permute-start | bytes 1769480 | tf_op jit(solution)/shard_map/ppermute | solution.py:558
  108.5 2.0 %collective-permute-start.31 = (bf16[8,96,768]{2,1,0:T(8,128)(2,1)S(1)}, bf16[8,96,768]{2,1,0:T(8,128)(2,1)S(1)}, u32[]{:S(2)}, u32[]{:S(2)}) collective-permute-start(bf16[8,96,768]{2,1,0:T(8,128)(2,1)S(1)} %sum_others.15.refs_3_.refs_1_), channel_id=1, source_target_pairs={{0,1},{1,0},{2,3},{3,2},{4,5},{5,4},{6,7},{7,6},{8,9},{9,8},{10,11... | collective-permute-start | bytes 3538952 | tf_op jit(solution)/shard_map/ppermute | solution.py:558
  112.1 2.1 %finish.6 = (f32[4,192,768]{2,1,0:T(8,128)}, f32[4,192,768]{2,1,0:T(8,128)}, f32[8,128]{1,0:T(8,128)S(1)}) custom-call(s32[5]{0:T(128)S(1)} %stack.23.refs_0_, bf16[8,96,768]{2,1,0:T(8,128)(2,1)S(1)} %sum_others.15.refs_3_.refs_1_, f32[8,128]{1,0:T(8,128)S(1)} %get-tuple-element.157.refs_2_), custom_call_target="tpu_custom_call" | custom-call | flops 3000000000 | bytes 1024 | tf_op jit(solution)/shard_map/finish/pallas_call | solution.py:523
  115.3 2.1 %finish.7 = (f32[4,192,768]{2,1,0:T(8,128)}, f32[4,192,768]{2,1,0:T(8,128)}, f32[8,128]{1,0:T(8,128)S(1)}) custom-call(s32[5]{0:T(128)S(1)} %stack.23.refs_0_, bf16[8,96,768]{2,1,0:T(8,128)(2,1)S(1)} %collective-permute-done.31.refs_1_, f32[4,192,768]{2,1,0:T(8,128)} %get-tuple-element.159.refs_2_, ...), custom_call_target="tpu_custom_call", output_to_operand_aliasing={{0}: (2, {}), {1}: (3, {})} | custom-call | flops 3000000000 | bytes 1024 | tf_op jit(solution)/shard_map/finish/pallas_call | solution.py:523
  117.4 2.2 %finish_qkv.1 = (f32[3,4,192,192]{3,2,1,0:T(8,128)}, f32[768]{0:T(1024)}, f32[768]{0:T(1024)}, f32[768]{0:T(1024)}, f32[768]{0:T(1024)}) custom-call(s32[5]{0:T(128)S(1)} %stack.23.refs_0_, bf16[8,48,640]{2,1,0:T(8,128)(2,1)S(1)} %sum_qkv.15.refs_4_.refs_1_, bf16[8,48,640]{2,1,0:T(8,128)(2,1)S(1)} %collective-permute-done.30.refs_2_, ...), custom_call_target="tpu_custom_call" | custom-call | flops 3000000000 | bytes 1024 | tf_op jit(solution)/shard_map/finish_qkv/pallas_call | solution.py:523
  (105 shorter events, 28.5 us)
Async XLA Ops:
  30.6 6.2 %collective-permute-start.1 = (bf16[8,48,768]{2,1,0:T(8,128)(2,1)S(1)}, bf16[8,48,768]{2,1,0:T(8,128)(2,1)S(1)}, u32[]{:S(2)}, u32[]{:S(2)}) collective-permute-start(bf16[8,48,768]{2,1,0:T(8,128)(2,1)S(1)} %get-tuple-element.108), channel_id=1, source_target_pairs={{0,1},{1,0},{2,3},{3,2},{4,5},{5,4},{6,7},{7,6},{8,9},{9,8},{10,11... | collective-permute-start | bytes 1769480 | tf_op jit(solution)/shard_map/ppermute | solution.py:558
  37.0 10.0 %collective-permute-start.2 = (bf16[4,48,768]{2,1,0:T(8,128)(2,1)S(1)}, bf16[4,48,768]{2,1,0:T(8,128)(2,1)S(1)}, u32[]{:S(2)}, u32[]{:S(2)}) collective-permute-start(bf16[4,48,768]{2,1,0:T(8,128)(2,1)S(1)} %get-tuple-element.111.refs_5_), channel_id=1, source_target_pairs={{0,8},{1,3},{2,10},{3,1},{4,12},{5,7},{6,14},{7,5},{8,0},{9,11},{1... | collective-permute-start | bytes 884744 | tf_op jit(solution)/shard_map/ppermute | solution.py:558
  42.4 5.7 %collective-permute-start.4 = (bf16[8,96,768]{2,1,0:T(8,128)(2,1)S(1)}, bf16[8,96,768]{2,1,0:T(8,128)(2,1)S(1)}, u32[]{:S(2)}, u32[]{:S(2)}) collective-permute-start(bf16[8,96,768]{2,1,0:T(8,128)(2,1)S(1)} %get-tuple-element.115.refs_9_), channel_id=1, source_target_pairs={{0,1},{1,0},{2,3},{3,2},{4,5},{5,4},{6,7},{7,6},{8,9},{9,8},{10,11... | collective-permute-start | bytes 3538952 | tf_op jit(solution)/shard_map/ppermute | solution.py:558
  46.9 12.7 %collective-permute-start.6 = (bf16[2,192,512]{2,1,0:T(8,128)(2,1)S(1)}, bf16[2,192,512]{2,1,0:T(8,128)(2,1)S(1)}, u32[]{:S(2)}, u32[]{:S(2)}) collective-permute-start(bf16[2,192,512]{2,1,0:T(8,128)(2,1)S(1)} %get-tuple-element.116.refs_2_), channel_id=1, source_target_pairs={{0,1},{1,0},{2,3},{3,2},{4,5},{5,4},{6,7},{7,6},{8,9},{9,8},{10,11... | collective-permute-start | bytes 1179656 | tf_op jit(solution)/shard_map/ppermute | solution.py:558
  47.1 6.6 %collective-permute-start.3 = (bf16[2,48,768]{2,1,0:T(8,128)(2,1)S(1)}, bf16[2,48,768]{2,1,0:T(8,128)(2,1)S(1)}, u32[]{:S(2)}, u32[]{:S(2)}) collective-permute-start(bf16[2,48,768]{2,1,0:T(8,128)(2,1)S(1)} %get-tuple-element.118.refs_2_), channel_id=1, source_target_pairs={{0,2},{1,9},{2,0},{3,11},{4,6},{5,13},{6,4},{7,15},{8,10},{9,1},{1... | collective-permute-start | bytes 442376 | tf_op jit(solution)/shard_map/ppermute | solution.py:558
  48.4 10.6 %collective-permute-start.8 = (bf16[4,96,768]{2,1,0:T(8,128)(2,1)S(1)}, bf16[4,96,768]{2,1,0:T(8,128)(2,1)S(1)}, u32[]{:S(2)}, u32[]{:S(2)}) collective-permute-start(bf16[4,96,768]{2,1,0:T(8,128)(2,1)S(1)} %get-tuple-element.120.refs_9_), channel_id=1, source_target_pairs={{0,2},{1,5},{2,0},{3,7},{4,6},{5,1},{6,4},{7,3},{8,10},{9,13},{10,... | collective-permute-start | bytes 1769480 | tf_op jit(solution)/shard_map/ppermute | solution.py:558
  53.2 6.4 %collective-permute-start.7 = (bf16[2,192,512]{2,1,0:T(8,128)(2,1)S(1)}, bf16[2,192,512]{2,1,0:T(8,128)(2,1)S(1)}, u32[]{:S(2)}, u32[]{:S(2)}) collective-permute-start(bf16[2,192,512]{2,1,0:T(8,128)(2,1)S(1)} %get-tuple-element.121.refs_2_), channel_id=1, source_target_pairs={{0,1},{1,0},{2,3},{3,2},{4,5},{5,4},{6,7},{7,6},{8,9},{9,8},{10,11... | collective-permute-start | bytes 1179656 | tf_op jit(solution)/shard_map/ppermute | solution.py:558
  53.7 14.9 %collective-permute-start.10 = (bf16[1,48,768]{2,1,0:T(8,128)(2,1)S(1)}, bf16[1,48,768]{2,1,0:T(8,128)(2,1)S(1)}, u32[]{:S(2)}, u32[]{:S(2)}) collective-permute-start(bf16[1,48,768]{2,1,0:T(8,128)(2,1)S(1)} %get-tuple-element.122.refs_9_), channel_id=1, source_target_pairs={{0,4},{1,5},{2,6},{3,7},{4,0},{5,1},{6,2},{7,3},{8,12},{9,13},{10,... | collective-permute-start | bytes 221192 | tf_op jit(solution)/shard_map/ppermute | solution.py:558
  58.6 12.4 %collective-permute-start.5 = (bf16[2,192,512]{2,1,0:T(8,128)(2,1)S(1)}, bf16[2,192,512]{2,1,0:T(8,128)(2,1)S(1)}, u32[]{:S(2)}, u32[]{:S(2)}) collective-permute-start(bf16[2,192,512]{2,1,0:T(8,128)(2,1)S(1)} %get-tuple-element.126.refs_2_), channel_id=1, source_target_pairs={{0,1},{1,0},{2,3},{3,2},{4,5},{5,4},{6,7},{7,6},{8,9},{9,8},{10,11... | collective-permute-start | bytes 1179656 | tf_op jit(solution)/shard_map/ppermute | solution.py:558
  59.1 8.5 %collective-permute-start.11 = (bf16[2,96,768]{2,1,0:T(8,128)(2,1)S(1)}, bf16[2,96,768]{2,1,0:T(8,128)(2,1)S(1)}, u32[]{:S(2)}, u32[]{:S(2)}) collective-permute-start(bf16[2,96,768]{2,1,0:T(8,128)(2,1)S(1)} %get-tuple-element.135.refs_14_), channel_id=1, source_target_pairs={{0,4},{1,9},{2,6},{3,11},{4,0},{5,13},{6,2},{7,15},{8,12},{9,1},{1... | collective-permute-start | bytes 884744 | tf_op jit(solution)/shard_map/ppermute | solution.py:558
  66.0 5.0 %collective-permute-start.9 = (bf16[2,192,512]{2,1,0:T(8,128)(2,1)S(1)}, bf16[2,192,512]{2,1,0:T(8,128)(2,1)S(1)}, u32[]{:S(2)}, u32[]{:S(2)}) collective-permute-start(bf16[2,192,512]{2,1,0:T(8,128)(2,1)S(1)} %get-tuple-element.140.refs_2_), channel_id=1, source_target_pairs={{0,1},{1,0},{2,3},{3,2},{4,5},{5,4},{6,7},{7,6},{8,9},{9,8},{10,11... | collective-permute-start | bytes 1179656 | tf_op jit(solution)/shard_map/ppermute | solution.py:558
  67.6 6.4 %collective-permute-start.13 = (bf16[1,96,768]{2,1,0:T(8,128)(2,1)S(1)}, bf16[1,96,768]{2,1,0:T(8,128)(2,1)S(1)}, u32[]{:S(2)}, u32[]{:S(2)}) collective-permute-start(bf16[1,96,768]{2,1,0:T(8,128)(2,1)S(1)} %get-tuple-element.144.refs_2_), channel_id=1, source_target_pairs={{0,8},{1,3},{2,10},{3,1},{4,12},{5,7},{6,14},{7,5},{8,0},{9,11},{1... | collective-permute-start | bytes 442376 | tf_op jit(solution)/shard_map/ppermute | solution.py:558
  68.6 7.3 %collective-permute-start.15 = (bf16[1,48,768]{2,1,0:T(8,128)(2,1)S(1)}, bf16[1,48,768]{2,1,0:T(8,128)(2,1)S(1)}, u32[]{:S(2)}, u32[]{:S(2)}) collective-permute-start(bf16[1,48,768]{2,1,0:T(8,128)(2,1)S(1)} %sum_ffn_out.11.refs_16_.refs_0_), channel_id=1, source_target_pairs={{0,16},{1,17},{2,18},{3,19},{4,20},{5,21},{6,22},{7,23},{8,24},{9,... | collective-permute-start | bytes 221192 | tf_op jit(solution)/shard_map/ppermute | solution.py:558
  76.4 9.5 %collective-permute-start.18 = (bf16[1,96,768]{2,1,0:T(8,128)(2,1)S(1)}, bf16[1,96,768]{2,1,0:T(8,128)(2,1)S(1)}, u32[]{:S(2)}, u32[]{:S(2)}) collective-permute-start(bf16[1,96,768]{2,1,0:T(8,128)(2,1)S(1)} %sum_others.11.refs_2_.refs_0_), channel_id=1, source_target_pairs={{0,16},{1,17},{2,18},{3,19},{4,20},{5,21},{6,22},{7,23},{8,24},{9,... | collective-permute-start | bytes 442376 | tf_op jit(solution)/shard_map/ppermute | solution.py:558
  76.6 6.4 %collective-permute-start.14 = (bf16[4,48,640]{2,1,0:T(8,128)(2,1)S(1)}, bf16[4,48,640]{2,1,0:T(8,128)(2,1)S(1)}, u32[]{:S(2)}, u32[]{:S(2)}) collective-permute-start(bf16[4,48,640]{2,1,0:T(8,128)(2,1)S(1)} %get-tuple-element.150.refs_2_), channel_id=1, source_target_pairs={{0,2},{1,5},{2,0},{3,7},{4,6},{5,1},{6,4},{7,3},{8,10},{9,13},{10,... | collective-permute-start | bytes 737288 | tf_op jit(solution)/shard_map/ppermute | solution.py:558
  79.8 11.9 %collective-permute-start.23 = (bf16[2,48,768]{2,1,0:T(8,128)(2,1)S(1)}, bf16[2,48,768]{2,1,0:T(8,128)(2,1)S(1)}, u32[]{:S(2)}, u32[]{:S(2)}) collective-permute-start(bf16[2,48,768]{2,1,0:T(8,128)(2,1)S(1)} %sum_ffn_out.13.refs_2_.refs_0_), channel_id=1, source_target_pairs={{0,2},{1,9},{2,0},{3,11},{4,6},{5,13},{6,4},{7,15},{8,10},{9,1},{1... | collective-permute-start | bytes 442376 | tf_op jit(solution)/shard_map/ppermute | solution.py:558
  83.0 5.1 %collective-permute-start.17 = (bf16[2,48,640]{2,1,0:T(8,128)(2,1)S(1)}, bf16[2,48,640]{2,1,0:T(8,128)(2,1)S(1)}, u32[]{:S(2)}, u32[]{:S(2)}) collective-permute-start(bf16[2,48,640]{2,1,0:T(8,128)(2,1)S(1)} %get-tuple-element.152.refs_2_), channel_id=1, source_target_pairs={{0,4},{1,9},{2,6},{3,11},{4,0},{5,13},{6,2},{7,15},{8,12},{9,1},{1... | collective-permute-start | bytes 368648 | tf_op jit(solution)/shard_map/ppermute | solution.py:558
  90.3 6.6 %collective-permute-start.22 = (bf16[2,96,768]{2,1,0:T(8,128)(2,1)S(1)}, bf16[2,96,768]{2,1,0:T(8,128)(2,1)S(1)}, u32[]{:S(2)}, u32[]{:S(2)}) collective-permute-start(bf16[2,96,768]{2,1,0:T(8,128)(2,1)S(1)} %sum_others.13.refs_2_.refs_0_), channel_id=1, source_target_pairs={{0,4},{1,9},{2,6},{3,11},{4,0},{5,13},{6,2},{7,15},{8,12},{9,1},{1... | collective-permute-start | bytes 884744 | tf_op jit(solution)/shard_map/ppermute | solution.py:558
  91.6 6.4 %collective-permute-start.21 = (bf16[1,48,640]{2,1,0:T(8,128)(2,1)S(1)}, bf16[1,48,640]{2,1,0:T(8,128)(2,1)S(1)}, u32[]{:S(2)}, u32[]{:S(2)}) collective-permute-start(bf16[1,48,640]{2,1,0:T(8,128)(2,1)S(1)} %sum_qkv.11.refs_2_.refs_0_), channel_id=1, source_target_pairs={{0,16},{1,17},{2,18},{3,19},{4,20},{5,21},{6,22},{7,23},{8,24},{9,... | collective-permute-start | bytes 184328 | tf_op jit(solution)/shard_map/ppermute | solution.py:558
  91.8 6.8 %collective-permute-start.25 = (bf16[4,48,768]{2,1,0:T(8,128)(2,1)S(1)}, bf16[4,48,768]{2,1,0:T(8,128)(2,1)S(1)}, u32[]{:S(2)}, u32[]{:S(2)}) collective-permute-start(bf16[4,48,768]{2,1,0:T(8,128)(2,1)S(1)} %sum_ffn_out.14.refs_2_.refs_0_), channel_id=1, source_target_pairs={{0,8},{1,3},{2,10},{3,1},{4,12},{5,7},{6,14},{7,5},{8,0},{9,11},{1... | collective-permute-start | bytes 884744 | tf_op jit(solution)/shard_map/ppermute | solution.py:558
  96.9 11.5 %collective-permute-start.28 = (bf16[4,96,768]{2,1,0:T(8,128)(2,1)S(1)}, bf16[4,96,768]{2,1,0:T(8,128)(2,1)S(1)}, u32[]{:S(2)}, u32[]{:S(2)}) collective-permute-start(bf16[4,96,768]{2,1,0:T(8,128)(2,1)S(1)} %sum_others.14.refs_2_.refs_0_), channel_id=1, source_target_pairs={{0,2},{1,5},{2,0},{3,7},{4,6},{5,1},{6,4},{7,3},{8,10},{9,13},{10,... | collective-permute-start | bytes 1769480 | tf_op jit(solution)/shard_map/ppermute | solution.py:558
  98.6 11.9 %collective-permute-start.29 = (bf16[8,48,768]{2,1,0:T(8,128)(2,1)S(1)}, bf16[8,48,768]{2,1,0:T(8,128)(2,1)S(1)}, u32[]{:S(2)}, u32[]{:S(2)}) collective-permute-start(bf16[8,48,768]{2,1,0:T(8,128)(2,1)S(1)} %sum_ffn_out.15.refs_2_.refs_1_), channel_id=1, source_target_pairs={{0,1},{1,0},{2,3},{3,2},{4,5},{5,4},{6,7},{7,6},{8,9},{9,8},{10,11... | collective-permute-start | bytes 1769480 | tf_op jit(solution)/shard_map/ppermute | solution.py:558
  107.1 7.1 %collective-permute-start.27 = (bf16[4,48,640]{2,1,0:T(8,128)(2,1)S(1)}, bf16[4,48,640]{2,1,0:T(8,128)(2,1)S(1)}, u32[]{:S(2)}, u32[]{:S(2)}) collective-permute-start(bf16[4,48,640]{2,1,0:T(8,128)(2,1)S(1)} %sum_qkv.14.refs_2_.refs_0_), channel_id=1, source_target_pairs={{0,2},{1,5},{2,0},{3,7},{4,6},{5,1},{6,4},{7,3},{8,10},{9,13},{10,... | collective-permute-start | bytes 737288 | tf_op jit(solution)/shard_map/ppermute | solution.py:558
  108.5 6.8 %collective-permute-start.31 = (bf16[8,96,768]{2,1,0:T(8,128)(2,1)S(1)}, bf16[8,96,768]{2,1,0:T(8,128)(2,1)S(1)}, u32[]{:S(2)}, u32[]{:S(2)}) collective-permute-start(bf16[8,96,768]{2,1,0:T(8,128)(2,1)S(1)} %sum_others.15.refs_3_.refs_1_), channel_id=1, source_target_pairs={{0,1},{1,0},{2,3},{3,2},{4,5},{5,4},{6,7},{7,6},{8,9},{9,8},{10,11... | collective-permute-start | bytes 3538952 | tf_op jit(solution)/shard_map/ppermute | solution.py:558
  (20 other events, 96.9 us)
